TPU v7x, 32 devices: a whole 2x2x4 slice. The times are simulated.
32 devices in a mesh: row: 4 (over x, core), col: 8 (over z, y).
Axes of the slice: x: 2, y: 2, z: 4, core: 2. Of those that a mesh axis runs over, the one named last changes fastest.
Arguments:
- geometry: float32 [4, 49152], P(None, ('row', 'col')), may hold values from -1 to 1, as said below
- charges: bfloat16 [32, 49152], P(None, ('row', 'col')), may hold values from -6 to 6
- near_index: int32 [384, 128], P(('row', 'col')), may hold values from 0 to 4607
- near_count: int32 [384], P(('row', 'col')), may hold values from 1 to 128
- near_weight: bfloat16 [384, 128, 128], P(('row', 'col')), may hold values from -0.5 to 0.5
- conductor: int32 [49152], P(('row', 'col')), may hold values from 0 to 31
Outputs:
- potential: float32 [32, 49152], P(None, ('row', 'col'))
- conductor_totals: float32 [32, 32], replicated
Inputs may be any that keep to these rules, and one draw needn't show every extreme that they name: `geometry`: rows 0 to 2 are coordinates in [-1, 1]; row 3 is a panel size in [0.05, 0.2].
All inputs are finite; a program needn't handle non-finite values.
Results may differ from a plain program's by a relative error of at most 0.0044.
Values may be sent and summed in bfloat16 or wider, within the bound.
No kernel may reach another device: no remote copies, remote signals or barrier semaphores. Data moves between devices by JAX's collectives and lax.ppermute only.
A program may use at most 64 MiB of HBM per device.

v0:
```python
import functools

import jax
import jax.numpy as jnp
import numpy as np
from jax import lax
from jax.experimental import pallas as pl
from jax.experimental.pallas import tpu as pltpu
from jax.sharding import PartitionSpec as P

ROUNDS = 8
AXES = ("row", "col")
F32 = jnp.float32
BF16 = jnp.bfloat16

X, NORM, AREA, MEMBER, ONE = 0, 6, 9, 11, 12
FEATURES = 16
DEPTH = 32
VMEM_LIMIT = 48 * 2**20


def chooser(left):
    table = np.zeros((DEPTH, FEATURES), np.float32)
    row = 0
    for axis in range(3):
        for first in range(2):
            for second in range(2):
                feature = X + 2 * axis + (first if left else second)
                table[row, feature] = 1.0 if left else -2.0
                row += 1
    for term in range(3):
        table[row, NORM + term if left else ONE] = 1.0
        table[row + 3, ONE if left else NORM + term] = 1.0
        row += 1
    return jnp.asarray(table, BF16)


def in_vmem(body, out_shape, scratch=(), flops=0):
    return pl.pallas_call(
        body,
        out_shape=out_shape,
        scratch_shapes=list(scratch),
        compiler_params=pltpu.CompilerParams(vmem_limit_bytes=VMEM_LIMIT),
        cost_estimate=pl.CostEstimate(flops=flops, bytes_accessed=2**20, transcendentals=0),
    )


def rounded(value):
    return value.astype(BF16).astype(F32)


def bundle_body(geo_ref, charges_ref, conductor_ref, out_ref, rows_ref):
    rhs = charges_ref.shape[0]
    size = geo_ref[3:4, :]
    area = size * size
    out_ref[0:rhs, :] = (charges_ref[...].astype(F32) * area).astype(BF16)
    rows_ref[...] = jnp.zeros_like(rows_ref)
    norm = area
    for axis in range(3):
        value = geo_ref[axis : axis + 1, :]
        high = rounded(value)
        low = rounded(value - high)
        rows_ref[X + 2 * axis : X + 2 * axis + 1, :] = high
        rows_ref[X + 2 * axis + 1 : X + 2 * axis + 2, :] = low
        kept = high + low
        norm = norm + kept * kept
    for term in range(3):
        part = rounded(norm)
        rows_ref[NORM + term : NORM + term + 1, :] = part
        norm = norm - part
    high = rounded(area)
    rows_ref[AREA : AREA + 1, :] = high
    rows_ref[AREA + 1 : AREA + 2, :] = area - high
    rows_ref[MEMBER : MEMBER + 1, :] = conductor_ref[...].astype(F32)
    rows_ref[ONE : ONE + 1, :] = jnp.ones_like(area)
    out_ref[rhs:, :] = rows_ref[...].astype(BF16)


def make_bundle(geometry, charges, conductor):
    rhs, panels = charges.shape
    return in_vmem(
        bundle_body,
        jax.ShapeDtypeStruct((rhs + FEATURES, panels), BF16),
        [pltpu.VMEM((FEATURES, panels), F32)],
    )(geometry, charges, conductor.reshape(1, panels))


def left_side(features, table):
    return lax.dot_general(
        features, table, (((0,), (1,)), ((), ())), preferred_element_type=F32
    ).astype(BF16)


def right_side(features, table):
    return jnp.dot(table, features, preferred_element_type=F32).astype(BF16)


def tile_of(left, right):
    return lax.rsqrt(jnp.dot(left, right, preferred_element_type=F32)).astype(BF16)


def two_stage(steps, make, use, slots):
    slots[0][...] = make(0)

    @pl.loop(0, steps // 2 - 1)
    def _(half):
        step = 2 * half
        slots[1][...] = make(step + 1)
        use(step, slots[0][...])
        slots[0][...] = make(step + 2)
        use(step + 1, slots[1][...])

    slots[1][...] = make(steps - 1)
    use(steps - 2, slots[0][...])
    use(steps - 1, slots[1][...])


def totals_of(field, bundle):
    rhs = field.shape[0]
    features = bundle[rhs:, :].astype(F32)
    area = features[AREA : AREA + 1, :] + features[AREA + 1 : AREA + 2, :]
    names = lax.broadcasted_iota(jnp.int32, field.shape, 0).astype(F32)
    member = jnp.where(names == features[MEMBER : MEMBER + 1, :], 1.0, 0.0).astype(BF16)
    scaled = field * area
    high = scaled.astype(BF16)
    low = (scaled - high.astype(F32)).astype(BF16)
    dims = (((1,), (1,)), ((), ()))
    return lax.dot_general(high, member, dims, preferred_element_type=F32) + lax.dot_general(
        low, member, dims, preferred_element_type=F32
    )


def self_body(rowblk, own_ref, ltab_ref, rtab_ref, out_ref, left_ref, right_ref, *slots):
    rhs, panels = out_ref.shape
    features = own_ref[rhs:, :]
    left_ref[...] = left_side(features, ltab_ref[...])
    right_ref[...] = right_side(features, rtab_ref[...])
    out_ref[...] = jnp.zeros_like(out_ref)

    def make(step):
        start = pl.multiple_of(step * rowblk, rowblk)
        return tile_of(left_ref[pl.ds(start, rowblk), :], right_ref[...])

    def use(step, tile):
        start = pl.multiple_of(step * rowblk, rowblk)
        out_ref[...] += jnp.dot(
            own_ref[0:rhs, pl.ds(start, rowblk)], tile, preferred_element_type=F32
        )

    two_stage(panels // rowblk, make, use, slots)


def self_field(own, tables):
    rows, panels = own.shape
    rhs = rows - FEATURES
    rowblk = 256
    return in_vmem(
        functools.partial(self_body, rowblk),
        jax.ShapeDtypeStruct((rhs, panels), F32),
        [
            pltpu.VMEM((panels, DEPTH), BF16),
            pltpu.VMEM((DEPTH, panels), BF16),
            pltpu.VMEM((rowblk, panels), BF16),
            pltpu.VMEM((rowblk, panels), BF16),
        ],
        flops=2 * 400 * panels * panels,
    )(own, *tables)


def pairs_body(
    rowblk, last, pair_ref, far_ref, ltab_ref, rtab_ref, field_in, totals_in,
    field_ref, back_ref, totals_ref, left_ref, right_ref, sum_ref, *slots
):
    blocks, rhs, panels = field_ref.shape
    for block in range(blocks):
        left_ref[block] = left_side(far_ref[block, rhs:, :], ltab_ref[...])
        right_ref[block] = right_side(pair_ref[block, rhs:, :], rtab_ref[...])
    field_ref[...] = field_in[...]
    sum_ref[...] = jnp.zeros_like(sum_ref)
    chunks = panels // rowblk

    def place(step):
        turn = step // chunks
        start = pl.multiple_of((step % chunks) * rowblk, rowblk)
        return turn // blocks, turn % blocks, start

    def make(step):
        far, own, start = place(step)
        return tile_of(left_ref[far, pl.ds(start, rowblk), :], right_ref[own])

    def use(step, tile):
        far, own, start = place(step)
        field_ref[own] += jnp.dot(
            far_ref[far, 0:rhs, pl.ds(start, rowblk)], tile, preferred_element_type=F32
        )
        sum_ref[far, :, pl.ds(start, rowblk)] += lax.dot_general(
            pair_ref[own, 0:rhs, :], tile, (((1,), (1,)), ((), ())), preferred_element_type=F32
        )

    two_stage(blocks * blocks * chunks, make, use, slots)
    totals = totals_in[...]
    for block in range(blocks):
        totals = totals + totals_of(sum_ref[block], far_ref[block])
        if last:
            totals = totals + totals_of(field_ref[block], pair_ref[block])
    totals_ref[...] = totals
    back_ref[...] = sum_ref[...].astype(BF16)


def pairs_field(pair, far, tables, field, totals, last):
    blocks, rows, panels = pair.shape
    rhs = rows - FEATURES
    rowblk = 256
    return in_vmem(
        functools.partial(pairs_body, rowblk, last),
        (
            jax.ShapeDtypeStruct((blocks, rhs, panels), F32),
            jax.ShapeDtypeStruct((blocks, rhs, panels), BF16),
            jax.ShapeDtypeStruct(totals.shape, F32),
        ),
        [
            pltpu.VMEM((blocks, panels, DEPTH), BF16),
            pltpu.VMEM((blocks, DEPTH, panels), BF16),
            pltpu.VMEM((blocks, rhs, panels), F32),
            pltpu.VMEM((rowblk, panels), BF16),
            pltpu.VMEM((rowblk, panels), BF16),
        ],
        flops=2 * 400 * panels * panels * blocks * blocks,
    )(pair, far, *tables, field, totals)


def near_body(
    twin_ref, own_ref, other_ref, index_ref, count_ref, odd_ref, weight_ref, out_ref, ext_ref
):
    rhs, panels = own_ref.shape
    groups, near = index_ref.shape
    for side, ref in enumerate((twin_ref, own_ref, other_ref)):
        ext_ref[:, side * panels : (side + 1) * panels] = ref[...].astype(F32)
    turn = jnp.where(odd_ref[0] == 1, 0, 2 * panels)

    @pl.loop(0, groups)
    def _(group):
        index = index_ref[pl.ds(group, 1), :]
        moved = jnp.where(index < panels, index + turn, index)
        index = jnp.where(index >= 2 * panels, index - turn, moved)
        slot = lax.broadcasted_iota(jnp.int32, (1, near), 1)
        live = slot < count_ref[group]
        lane = jnp.broadcast_to(index % near, (rhs, near))
        piece = jnp.broadcast_to(jnp.where(live, index // near, -1), (rhs, near))
        taken = jnp.zeros((rhs, near), F32)
        for part in range(3 * panels // near):
            found = jnp.take_along_axis(
                ext_ref[:, part * near : (part + 1) * near], lane, axis=1
            )
            taken = jnp.where(piece == part, found, taken)
        width = weight_ref.shape[1]
        out_ref[:, pl.ds(pl.multiple_of(group * width, width), width)] = lax.dot_general(
            taken.astype(BF16), weight_ref[group], (((1,), (1,)), ((), ())),
            preferred_element_type=F32,
        )


def near_field(twin, own, other, index, count, odd, weight):
    rhs, panels = own.shape
    vmem = pl.BlockSpec(memory_space=pltpu.VMEM)
    return pl.pallas_call(
        near_body,
        out_shape=jax.ShapeDtypeStruct((rhs, panels), F32),
        in_specs=[vmem] * 4 + [pl.BlockSpec(memory_space=pltpu.SMEM)] * 2 + [vmem],
        out_specs=vmem,
        scratch_shapes=[pltpu.VMEM((rhs, 3 * panels), F32)],
        compiler_params=pltpu.CompilerParams(vmem_limit_bytes=VMEM_LIMIT),
        cost_estimate=pl.CostEstimate(flops=2 * 10**9, bytes_accessed=2**20, transcendentals=0),
    )(twin, own, other, index, count, odd, weight)


def start_body(self_ref, near_ref, field_ref):
    field_ref[0] = self_ref[...] + near_ref[...]
    field_ref[1] = jnp.zeros_like(self_ref)


def send(value, source_of):
    count = lax.axis_size(AXES)
    return lax.ppermute(value, AXES, [(source_of(d), d) for d in range(count)])


def send_back(value, source_of):
    count = lax.axis_size(AXES)
    return lax.ppermute(value, AXES, [(d, source_of(d)) for d in range(count)])


def paired_blocks(geometry, charges, near_index, near_count, near_weight, conductor):
    cols = lax.axis_size("col")
    core, flip_x, far_z = cols, 2 * cols, cols // 2
    rhs, panels = charges.shape

    def partner(d, far):
        second = bool(d & core)
        mask = 1 + (flip_x if bool(d & 1) != second else 0) + (2 if second else 0)
        return d ^ (mask + (far_z if far else 0))

    def other_neighbour(d):
        count = lax.axis_size(AXES)
        return (d + (1 if d & 1 else -1)) % count

    tables = (chooser(True), chooser(False))
    bundle = make_bundle(geometry, charges, conductor)
    sibling = send(bundle, lambda d: d ^ core)
    pair = jnp.stack([bundle, sibling])
    close = send(pair, lambda d: partner(d, False))
    far = send(pair, lambda d: partner(d, True))
    twin = send(charges, lambda d: d ^ 1)
    other = send(charges, other_neighbour)
    own = self_field(bundle, tables)
    odd = (lax.axis_index(AXES) % 2).reshape(1)
    near = near_field(twin, charges, other, near_index, near_count, odd, near_weight)
    pair_shape = (2, rhs, panels)
    field = in_vmem(start_body, jax.ShapeDtypeStruct(pair_shape, F32))(own, near)
    totals = jnp.zeros((rhs, rhs), F32)
    field, close_back, totals = pairs_field(pair, close, tables, field, totals, False)
    close_back = send_back(close_back, lambda d: partner(d, False))
    field, far_back, totals = pairs_field(pair, far, tables, field, totals, True)
    far_back = send_back(far_back, lambda d: partner(d, True))
    for step in (core, 1, flip_x, 2, far_z):
        totals = totals + send(totals, lambda d: d ^ step)
    back = close_back.astype(F32) + far_back.astype(F32)
    field = field + back
    twin_part = send(field[1].astype(BF16), lambda d: d ^ core)
    return (field[0] + twin_part.astype(F32), totals)


def passed_along(value, axis, steps):
    count = lax.axis_size(axis)
    pairs = [(source, (source + steps) % count) for source in range(count)]
    return lax.ppermute(value, axis, pairs)


def extended_2(x, sides, width):
    for axis, dim in sides:
        count, length = (lax.axis_size(axis), x.shape[dim])
        up = [(i, (i + 1) % count) for i in range(count)]
        down = [(j, i) for i, j in up]
        last = lax.slice_in_dim(x, length - width, length, axis=dim)
        initial = lax.slice_in_dim(x, 0, width, axis=dim)
        before = lax.ppermute(last, axis, up)
        after = lax.ppermute(initial, axis, down)
        x = jnp.concatenate([before, x, after], axis=dim)
    return x


def kernel_tile(rows, cols):
    delta_x = rows[0][:, None] - cols[0][None, :]
    delta_y = rows[1][:, None] - cols[1][None, :]
    delta_z = rows[2][:, None] - cols[2][None, :]
    spread = rows[3][:, None] * rows[3][:, None] + cols[3][None, :] * cols[3][None, :]
    squared = delta_x * delta_x + delta_y * delta_y + delta_z * delta_z + spread
    return lax.rsqrt(squared).astype(BF16)


def pair_products(own_geo, own_w, other_geo, other_w, backwards):
    panels = own_geo.shape[1]
    rowblk = min(256, panels)
    pieces = []
    back = jnp.zeros(other_w.shape, F32)
    for start in range(0, panels, rowblk):
        tile = kernel_tile(own_geo[:, start : start + rowblk], other_geo)
        pieces.append(
            lax.dot_general(
                other_w, tile, (((1,), (1,)), ((), ())), preferred_element_type=F32
            )
        )
        if backwards:
            back = back + jnp.dot(
                own_w[:, start : start + rowblk], tile, preferred_element_type=F32
            )
    return (jnp.concatenate(pieces, axis=1), back)


def from_lower(geometry, weighted, offset):
    geo = passed_along(geometry, ("row", "col"), offset)
    wts = passed_along(weighted, ("row", "col"), offset)
    return (geo, wts)


def give_back(partial_value, offset):
    return passed_along(partial_value, ("row", "col"), -offset)


def offset_rounds(geometry, charges, near_index, near_count, near_weight, conductor):
    devices = lax.axis_size(("row", "col"))
    stride = devices // (2 * ROUNDS)
    offsets = [1 + k * stride for k in range(ROUNDS)]
    panels = charges.shape[1]
    groups_dev = near_index.shape[0]
    area = geometry[3] * geometry[3]
    weighted = (charges.astype(F32) * area[None, :]).astype(BF16)
    field, unused = pair_products(geometry, weighted, geometry, weighted, False)
    for turn in range(ROUNDS):
        offset = offsets[turn]
        lower_geo, lower_w = from_lower(geometry, weighted, offset)
        forward, back = pair_products(geometry, weighted, lower_geo, lower_w, True)
        field = field + forward + give_back(back.astype(BF16), offset).astype(F32)
    extended = extended_2(charges, ((("row", "col"), 1),), panels)
    gathered = jnp.take(extended, near_index.reshape(-1), axis=1).reshape(
        charges.shape[0], groups_dev, near_index.shape[1]
    )
    live = jnp.arange(near_index.shape[1], dtype=jnp.int32)[None, :] < near_count[:, None]
    gathered = jnp.where(live[None], gathered, jnp.zeros_like(gathered))
    correction = jnp.einsum(
        "rgk,gtk->rgt", gathered, near_weight, preferred_element_type=F32
    )
    field = field + correction.reshape(charges.shape[0], panels)
    member = (conductor[:, None] == jnp.arange(charges.shape[0], dtype=jnp.int32)[None, :]).astype(
        F32
    )
    local_totals = jnp.dot(
        field * area[None, :],
        member,
        precision=lax.Precision.HIGHEST,
        preferred_element_type=F32,
    )
    totals = lax.psum(local_totals, ("row", "col"))
    return (field, totals)


def on_device(geometry, *rest):
    if lax.axis_size(AXES) == 4 * ROUNDS:
        return paired_blocks(geometry, *rest)
    return offset_rounds(geometry, *rest)


def solution(mesh):
    in_specs = (
        P(None, ("row", "col")),
        P(None, ("row", "col")),
        P(("row", "col"), None),
        P(("row", "col")),
        P(("row", "col"), None, None),
        P(("row", "col")),
    )
    out_specs = (P(None, ("row", "col")), P())
    return jax.shard_map(
        on_device, mesh=mesh, in_specs=in_specs, out_specs=out_specs, check_vma=False
    )
```

profile of v0, /device:TPU:0, one launch (start us, length us, event | category | flops | bytes accessed | tf_op | source)
XLA Modules:
  0.0 86.3 jit_solution(4037966152740108089)
XLA Ops:
  0.6 0.7 reshape.11.conductor_ref
  1.3 0.0 copy-start
  1.3 0.7 copy-done
  2.1 1.0 %shard_map.95.own_ref = bf16[48,1536]{1,0:T(8,128)(2,1)S(1)} custom-call(f32[4,1536]{1,0:T(4,128)S(1)} %copy-done, bf16[32,1536]{1,0:T(8,128)(2,1)} %own_ref.1, s32[1,1536]{1,0:T(1,128)S(1)} %reshape.11.conductor_ref), custom_call_target="tpu_custom_call" | custom-call | bytes 1048576 | tf_op jit(solution)/shard_map/pallas_call | solution.py:81
  3.1 0.5 collective-permute-start
  3.6 2.6 %collective-permute-start.3 = (bf16[32,1536]{1,0:T(8,128)(2,1)}, bf16[32,1536]{1,0:T(8,128)(2,1)S(1)}, u32[]{:S(2)}, u32[]{:S(2)}) collective-permute-start(bf16[32,1536]{1,0:T(8,128)(2,1)} %own_ref.1), channel_id=1, source_target_pairs={{1,0},{0,1},{3,2},{2,3},{5,4},{4,5},{7,6},{6,7},{9,8},{8,9},{11,10... | collective-permute-start | bytes 294920 | tf_op jit(solution)/shard_map/ppermute | solution.py:284
  6.2 4.2 %collective-permute-start.4 = (bf16[32,1536]{1,0:T(8,128)(2,1)}, bf16[32,1536]{1,0:T(8,128)(2,1)S(1)}, u32[]{:S(2)}, u32[]{:S(2)}) collective-permute-start(bf16[32,1536]{1,0:T(8,128)(2,1)} %own_ref.1), channel_id=1, source_target_pairs={{31,0},{2,1},{1,2},{4,3},{3,4},{6,5},{5,6},{8,7},{7,8},{10,9},{9,1... | collective-permute-start | bytes 294920 | tf_op jit(solution)/shard_map/ppermute | solution.py:284
  10.4 0.0 collective-permute-done
  10.5 0.0 copy-start.4
  10.5 0.0 copy-start.5
  10.5 0.0 copy-start.1
  10.5 0.0 copy-start.2
  10.5 0.1 collective-permute-start.2
  10.6 0.6 copy-done.4
  11.1 0.0 copy-done.5
  11.2 2.6 %shard_map.96.self_ref = f32[32,1536]{1,0:T(8,128)S(1)} custom-call(bf16[48,1536]{1,0:T(8,128)(2,1)S(1)} %shard_map.95.own_ref, bf16[32,16]{1,0:T(8,128)(2,1)S(1)} %copy-done.5, bf16[32,16]{1,0:T(8,128)(2,1)S(1)} %copy-done.4), custom_call_target="tpu_custom_call" | custom-call | flops 1887436800 | bytes 1048576 | tf_op jit(solution)/shard_map/pallas_call | solution.py:157
  13.8 0.0 copy-start.3
  13.8 3.8 %collective-permute-done.3.twin_ref = bf16[32,1536]{1,0:T(8,128)(2,1)S(1)} collective-permute-done((bf16[32,1536]{1,0:T(8,128)(2,1)}, bf16[32,1536]{1,0:T(8,128)(2,1)S(1)}, u32[]{:S(2)}, u32[]{:S(2)}) %collective-permute-start.3) | collective-permute-done | bytes 98336 | tf_op jit(solution)/shard_map/ppermute | solution.py:284
  17.6 0.0 collective-permute-done.4.other_ref
  17.6 0.0 copy-done.1
  17.6 0.0 copy-done.2
  17.6 0.0 copy-done.3
  17.6 4.2 %shard_map.97.near_ref = f32[32,1536]{1,0:T(8,128)S(1)} custom-call(bf16[32,1536]{1,0:T(8,128)(2,1)S(1)} %collective-permute-done.3.twin_ref, bf16[32,1536]{1,0:T(8,128)(2,1)} %own_ref.1, bf16[32,1536]{1,0:T(8,128)(2,1)S(1)} %collective-permute-done.4.other_ref, s32[12,128]{1,0:T(8,128)S(1)} %copy-done.2, s32[12]{0:T(128)S(1)} %copy-done.3, ...), custom_call_target="tpu_custom_call" | custom-call | flops 2000000000 | bytes 1048576 | tf_op jit(solution)/shard_map/pallas_call | solution.py:266
  21.9 5.4 %collective-permute-start.1 = (bf16[2,48,1536]{2,1,0:T(8,128)(2,1)S(1)}, bf16[2,48,1536]{2,1,0:T(8,128)(2,1)S(1)}, u32[]{:S(2)}, u32[]{:S(2)}) collective-permute-start(bf16[2,48,1536]{2,1,0:T(8,128)(2,1)S(1)} %pad_maximum_fusion.pair_ref), channel_id=1, source_target_pairs={{5,0},{20,1},{7,2},{22,3},{1,4},{16,5},{3,6},{18,7},{31,8},{14,9},... | collective-permute-start | bytes 884744 | tf_op jit(solution)/shard_map/ppermute | solution.py:284
  27.3 0.0 collective-permute-done.2.far_ref
  27.3 14.5 %shard_map.99 = (f32[2,32,1536]{2,1,0:T(8,128)S(1)}, bf16[2,32,1536]{2,1,0:T(8,128)(2,1)S(1)}, f32[32,32]{1,0:T(8,128)S(1)}) custom-call(bf16[2,48,1536]{2,1,0:T(8,128)(2,1)S(1)} %pad_maximum_fusion.pair_ref, bf16[2,48,1536]{2,1,0:T(8,128)(2,1)S(1)} %collective-permute-done.2.far_ref, bf16[32,16]{1,0:T(8,128)(2,1)S(1)} %copy-done.5, ...), custom_call_target="tpu_custom_call" | custom-call | flops 7549747200 | bytes 1048576 | tf_op jit(solution)/shard_map/pallas_call | solution.py:214
  41.8 0.0 collective-permute-start.5
  41.8 0.0 collective-permute-done.1.far_ref
  41.8 14.7 %shard_map.100 = (f32[2,32,1536]{2,1,0:T(8,128)S(1)}, bf16[2,32,1536]{2,1,0:T(8,128)(2,1)S(1)}, f32[32,32]{1,0:T(8,128)S(1)}) custom-call(bf16[2,48,1536]{2,1,0:T(8,128)(2,1)S(1)} %pad_maximum_fusion.pair_ref, bf16[2,48,1536]{2,1,0:T(8,128)(2,1)S(1)} %collective-permute-done.1.far_ref, bf16[32,16]{1,0:T(8,128)(2,1)S(1)} %copy-done.5, ...), custom_call_target="tpu_custom_call" | custom-call | flops 7549747200 | bytes 1048576 | tf_op jit(solution)/shard_map/pallas_call | solution.py:214
  56.5 1.8 %collective-permute-start.6 = (bf16[2,32,1536]{2,1,0:T(8,128)(2,1)S(1)}, bf16[2,32,1536]{2,1,0:T(8,128)(2,1)S(1)}, u32[]{:S(2)}, u32[]{:S(2)}) collective-permute-start(bf16[2,32,1536]{2,1,0:T(8,128)(2,1)S(1)} %get-tuple-element.12), channel_id=1, source_target_pairs={{0,5},{1,20},{2,7},{3,22},{4,1},{5,16},{6,3},{7,18},{8,31},{9,14},... | collective-permute-start | bytes 589832 | tf_op jit(solution)/shard_map/ppermute | solution.py:289
  58.3 0.0 collective-permute-done.5
  58.3 9.3 %collective-permute-done.6 = bf16[2,32,1536]{2,1,0:T(8,128)(2,1)S(1)} collective-permute-done((bf16[2,32,1536]{2,1,0:T(8,128)(2,1)S(1)}, bf16[2,32,1536]{2,1,0:T(8,128)(2,1)S(1)}, u32[]{:S(2)}, u32[]{:S(2)}) %collective-permute-start.6) | collective-permute-done | bytes 196640 | tf_op jit(solution)/shard_map/ppermute | solution.py:289
  67.6 0.1 add_add_fusion
  67.7 0.1 collective-permute-start.7
  67.8 0.5 collective-permute-start.8
  68.3 0.8 collective-permute-done.8
  69.1 0.6 collective-permute-start.9
  69.7 3.2 %collective-permute-done.9 = f32[32,32]{1,0:T(8,128)S(1)} collective-permute-done((f32[32,32]{1,0:T(8,128)S(1)}, f32[32,32]{1,0:T(8,128)S(1)}, u32[]{:S(2)}, u32[]{:S(2)}) %collective-permute-start.9) | collective-permute-done | bytes 4128 | tf_op jit(solution)/shard_map/ppermute | solution.py:284
  72.9 0.3 collective-permute-start.10
  73.1 3.5 %collective-permute-done.10 = f32[32,32]{1,0:T(8,128)S(1)} collective-permute-done((f32[32,32]{1,0:T(8,128)S(1)}, f32[32,32]{1,0:T(8,128)S(1)}, u32[]{:S(2)}, u32[]{:S(2)}) %collective-permute-start.10) | collective-permute-done | bytes 4128 | tf_op jit(solution)/shard_map/ppermute | solution.py:284
  76.6 0.0 collective-permute-start.11
  76.6 3.7 %collective-permute-done.11 = f32[32,32]{1,0:T(8,128)S(1)} collective-permute-done((f32[32,32]{1,0:T(8,128)S(1)}, f32[32,32]{1,0:T(8,128)S(1)}, u32[]{:S(2)}, u32[]{:S(2)}) %collective-permute-start.11) | collective-permute-done | bytes 4128 | tf_op jit(solution)/shard_map/ppermute | solution.py:284
  80.3 0.4 collective-permute-start.12
  80.7 4.3 %collective-permute-done.12 = f32[32,32]{1,0:T(8,128)S(1)} collective-permute-done((f32[32,32]{1,0:T(8,128)S(1)}, f32[32,32]{1,0:T(8,128)S(1)}, u32[]{:S(2)}, u32[]{:S(2)}) %collective-permute-start.12) | collective-permute-done | bytes 4128 | tf_op jit(solution)/shard_map/ppermute | solution.py:284
  85.0 0.6 add.40
  85.6 0.0 collective-permute-done.7
  85.6 0.7 fusion
  (8 shorter events, 0.1 us)
Async XLA Ops:
  1.3 0.7 copy-start
  3.1 7.4 %collective-permute-start = (bf16[48,1536]{1,0:T(8,128)(2,1)S(1)}, bf16[48,1536]{1,0:T(8,128)(2,1)S(1)}, u32[]{:S(2)}, u32[]{:S(2)}) collective-permute-start(bf16[48,1536]{1,0:T(8,128)(2,1)S(1)} %shard_map.95.own_ref), channel_id=1, source_target_pairs={{8,0},{9,1},{10,2},{11,3},{12,4},{13,5},{14,6},{15,7},{0,8},{1,9},... | collective-permute-start | bytes 442376 | tf_op jit(solution)/shard_map/ppermute | solution.py:284
  3.6 14.0 %collective-permute-start.3 = (bf16[32,1536]{1,0:T(8,128)(2,1)}, bf16[32,1536]{1,0:T(8,128)(2,1)S(1)}, u32[]{:S(2)}, u32[]{:S(2)}) collective-permute-start(bf16[32,1536]{1,0:T(8,128)(2,1)} %own_ref.1), channel_id=1, source_target_pairs={{1,0},{0,1},{3,2},{2,3},{5,4},{4,5},{7,6},{6,7},{9,8},{8,9},{11,10... | collective-permute-start | bytes 294920 | tf_op jit(solution)/shard_map/ppermute | solution.py:284
  6.2 11.4 %collective-permute-start.4 = (bf16[32,1536]{1,0:T(8,128)(2,1)}, bf16[32,1536]{1,0:T(8,128)(2,1)S(1)}, u32[]{:S(2)}, u32[]{:S(2)}) collective-permute-start(bf16[32,1536]{1,0:T(8,128)(2,1)} %own_ref.1), channel_id=1, source_target_pairs={{31,0},{2,1},{1,2},{4,3},{3,4},{6,5},{5,6},{8,7},{7,8},{10,9},{9,1... | collective-permute-start | bytes 294920 | tf_op jit(solution)/shard_map/ppermute | solution.py:284
  10.5 0.7 copy-start.4
  10.5 0.7 copy-start.5
  10.5 7.1 %copy-start.1 = (bf16[12,128,128]{2,1,0:T(8,128)(2,1)S(1)}, bf16[12,128,128]{2,1,0:T(8,128)(2,1)}, u32[]{:S(2)}) copy-start(bf16[12,128,128]{2,1,0:T(8,128)(2,1)} %weight_ref.1) | copy-start | bytes 1179652
  10.5 7.1 %copy-start.2 = (s32[12,128]{1,0:T(8,128)S(1)}, s32[12,128]{1,0:T(8,128)}, u32[]{:S(2)}) copy-start(s32[12,128]{1,0:T(8,128)} %index_ref.1) | copy-start | bytes 18436
  10.5 16.8 %collective-permute-start.2 = (bf16[2,48,1536]{2,1,0:T(8,128)(2,1)S(1)}, bf16[2,48,1536]{2,1,0:T(8,128)(2,1)S(1)}, u32[]{:S(2)}, u32[]{:S(2)}) collective-permute-start(bf16[2,48,1536]{2,1,0:T(8,128)(2,1)S(1)} %pad_maximum_fusion.pair_ref), channel_id=1, source_target_pairs={{1,0},{16,1},{3,2},{18,3},{5,4},{20,5},{7,6},{22,7},{27,8},{10,9},... | collective-permute-start | bytes 884744 | tf_op jit(solution)/shard_map/ppermute | solution.py:284
  13.8 3.8 %copy-start.3 = (s32[12]{0:T(128)S(1)}, s32[12]{0:T(128)}, u32[]{:S(2)}) copy-start(s32[12]{0:T(128)} %count_ref.1) | copy-start | bytes 148
  21.9 19.9 %collective-permute-start.1 = (bf16[2,48,1536]{2,1,0:T(8,128)(2,1)S(1)}, bf16[2,48,1536]{2,1,0:T(8,128)(2,1)S(1)}, u32[]{:S(2)}, u32[]{:S(2)}) collective-permute-start(bf16[2,48,1536]{2,1,0:T(8,128)(2,1)S(1)} %pad_maximum_fusion.pair_ref), channel_id=1, source_target_pairs={{5,0},{20,1},{7,2},{22,3},{1,4},{16,5},{3,6},{18,7},{31,8},{14,9},... | collective-permute-start | bytes 884744 | tf_op jit(solution)/shard_map/ppermute | solution.py:284
  41.8 16.5 %collective-permute-start.5 = (bf16[2,32,1536]{2,1,0:T(8,128)(2,1)S(1)}, bf16[2,32,1536]{2,1,0:T(8,128)(2,1)S(1)}, u32[]{:S(2)}, u32[]{:S(2)}) collective-permute-start(bf16[2,32,1536]{2,1,0:T(8,128)(2,1)S(1)} %get-tuple-element.11), channel_id=1, source_target_pairs={{0,1},{1,16},{2,3},{3,18},{4,5},{5,20},{6,7},{7,22},{8,27},{9,10},... | collective-permute-start | bytes 589832 | tf_op jit(solution)/shard_map/ppermute | solution.py:289
  56.5 11.1 %collective-permute-start.6 = (bf16[2,32,1536]{2,1,0:T(8,128)(2,1)S(1)}, bf16[2,32,1536]{2,1,0:T(8,128)(2,1)S(1)}, u32[]{:S(2)}, u32[]{:S(2)}) collective-permute-start(bf16[2,32,1536]{2,1,0:T(8,128)(2,1)S(1)} %get-tuple-element.12), channel_id=1, source_target_pairs={{0,5},{1,20},{2,7},{3,22},{4,1},{5,16},{6,3},{7,18},{8,31},{9,14},... | collective-permute-start | bytes 589832 | tf_op jit(solution)/shard_map/ppermute | solution.py:289
  67.7 17.9 %collective-permute-start.7 = (bf16[32,1536]{1,0:T(8,128)(2,1)S(1)}, bf16[32,1536]{1,0:T(8,128)(2,1)S(1)}, u32[]{:S(2)}, u32[]{:S(2)}) collective-permute-start(bf16[32,1536]{1,0:T(8,128)(2,1)S(1)} %fusion.1), channel_id=1, source_target_pairs={{8,0},{9,1},{10,2},{11,3},{12,4},{13,5},{14,6},{15,7},{0,8},{1,9},... | collective-permute-start | bytes 294920 | tf_op jit(solution)/shard_map/ppermute | solution.py:284
  67.8 1.3 %collective-permute-start.8 = (f32[32,32]{1,0:T(8,128)S(1)}, f32[32,32]{1,0:T(8,128)S(1)}, u32[]{:S(2)}, u32[]{:S(2)}) collective-permute-start(f32[32,32]{1,0:T(8,128)S(1)} %get-tuple-element.13), channel_id=1, source_target_pairs={{8,0},{9,1},{10,2},{11,3},{12,4},{13,5},{14,6},{15,7},{0,8},{1,9},... | collective-permute-start | bytes 12296 | tf_op jit(solution)/shard_map/ppermute | solution.py:284
  69.1 3.7 %collective-permute-start.9 = (f32[32,32]{1,0:T(8,128)S(1)}, f32[32,32]{1,0:T(8,128)S(1)}, u32[]{:S(2)}, u32[]{:S(2)}) collective-permute-start(f32[32,32]{1,0:T(8,128)S(1)} %add.36), channel_id=1, source_target_pairs={{1,0},{0,1},{3,2},{2,3},{5,4},{4,5},{7,6},{6,7},{9,8},{8,9},{11,10... | collective-permute-start | bytes 12296 | tf_op jit(solution)/shard_map/ppermute | solution.py:284
  72.9 3.7 %collective-permute-start.10 = (f32[32,32]{1,0:T(8,128)S(1)}, f32[32,32]{1,0:T(8,128)S(1)}, u32[]{:S(2)}, u32[]{:S(2)}) collective-permute-start(f32[32,32]{1,0:T(8,128)S(1)} %add.37), channel_id=1, source_target_pairs={{16,0},{17,1},{18,2},{19,3},{20,4},{21,5},{22,6},{23,7},{24,8},{25... | collective-permute-start | bytes 12296 | tf_op jit(solution)/shard_map/ppermute | solution.py:284
  76.6 3.7 %collective-permute-start.11 = (f32[32,32]{1,0:T(8,128)S(1)}, f32[32,32]{1,0:T(8,128)S(1)}, u32[]{:S(2)}, u32[]{:S(2)}) collective-permute-start(f32[32,32]{1,0:T(8,128)S(1)} %add.38), channel_id=1, source_target_pairs={{2,0},{3,1},{0,2},{1,3},{6,4},{7,5},{4,6},{5,7},{10,8},{11,9},{8,1... | collective-permute-start | bytes 12296 | tf_op jit(solution)/shard_map/ppermute | solution.py:284
  80.3 4.6 %collective-permute-start.12 = (f32[32,32]{1,0:T(8,128)S(1)}, f32[32,32]{1,0:T(8,128)S(1)}, u32[]{:S(2)}, u32[]{:S(2)}) collective-permute-start(f32[32,32]{1,0:T(8,128)S(1)} %add.39), channel_id=1, source_target_pairs={{4,0},{5,1},{6,2},{7,3},{0,4},{1,5},{2,6},{3,7},{12,8},{13,9},{14,... | collective-permute-start | bytes 12296 | tf_op jit(solution)/shard_map/ppermute | solution.py:284
where the time goes:
time: 86.6 us; the launch traced here: 86.3 us
  Pallas kernels  37.1 us (43%)
  waiting for transfers between devices  28.7 us (33%)
  starting transfers between devices  16.3 us (19%)
  local copies, waits for them, and re-layouts  2.06 us (2%)
  other arithmetic  1.41 us (2%)
    pallas_call x2, Pallas kernels, pairs_field(): in_vmem(functools.partial(pairs_body, rowblk, last), (jax.ShapeDtypeStruc...  29.2 us
    ppermute x11, waiting for transfers between devices, send(): return lax.ppermute(value, AXES, [(source_of(d), d) for d in range(count)])  19.3 us
    ppermute x11, starting transfers between devices, send(): return lax.ppermute(value, AXES, [(source_of(d), d) for d in range(count)])  14.6 us
    ppermute x2, waiting for transfers between devices, send_back(): return lax.ppermute(value, AXES, [(d, source_of(d)) for d in range(count)])  9.34 us
    pallas_call x1, Pallas kernels, near_field(): pl.pallas_call(near_body, out_shape=jax.ShapeDtypeStruct((rhs, panels), F...  4.23 us
    pallas_call x1, Pallas kernels, self_field(): in_vmem(functools.partial(self_body, rowblk), jax.ShapeDtypeStruct((rhs,...  2.63 us
    ppermute x2, starting transfers between devices, send_back(): return lax.ppermute(value, AXES, [(d, source_of(d)) for d in range(count)])  1.78 us
  transfers between devices with their start and end apart: 13, of which 7 were waited for; matrix products, arithmetic and copies ran while one was open for 1% of the time, Pallas kernels for 42%

commit v1 on v0

--- a/solution.py
+++ b/solution.py
@@ -35,13 +35,18 @@
     return jnp.asarray(table, BF16)
 
 
+def blocking(panels):
+    rows = next((r for r in (384, 256, 128) if panels % (2 * r) == 0), panels // 2)
+    return rows, 256 if panels % 256 == 0 else panels
+
+
 def in_vmem(body, out_shape, scratch=(), flops=0):
     return pl.pallas_call(
         body,
         out_shape=out_shape,
         scratch_shapes=list(scratch),
         compiler_params=pltpu.CompilerParams(vmem_limit_bytes=VMEM_LIMIT),
-        cost_estimate=pl.CostEstimate(flops=flops, bytes_accessed=2**20, transcendentals=0),
+        cost_estimate=pl.CostEstimate(flops=flops, bytes_accessed=2**10, transcendentals=0),
     )
 
 
@@ -99,20 +104,27 @@
     return lax.rsqrt(jnp.dot(left, right, preferred_element_type=F32)).astype(BF16)
 
 
-def two_stage(steps, make, use, slots):
-    slots[0][...] = make(0)
+def two_stage(steps, make, use, slots, width):
+    strips = range(0, slots[0].shape[1], width)
+
+    def one(step, now, later):
+        carry = None
+        for start in strips:
+            if later is not None:
+                later[:, start : start + width] = make(step + 1, start)
+            carry = use(step, now[:, start : start + width], start, carry)
+        use(step, None, None, carry)
+
+    for start in strips:
+        slots[0][:, start : start + width] = make(0, start)
 
     @pl.loop(0, steps // 2 - 1)
     def _(half):
-        step = 2 * half
-        slots[1][...] = make(step + 1)
-        use(step, slots[0][...])
-        slots[0][...] = make(step + 2)
-        use(step + 1, slots[1][...])
-
-    slots[1][...] = make(steps - 1)
-    use(steps - 2, slots[0][...])
-    use(steps - 1, slots[1][...])
+        one(2 * half, slots[0], slots[1])
+        one(2 * half + 1, slots[1], slots[0])
+
+    one(steps - 2, slots[0], slots[1])
+    one(steps - 1, slots[1], None)
 
 
 def totals_of(field, bundle):
@@ -130,45 +142,47 @@
     )
 
 
-def self_body(rowblk, own_ref, ltab_ref, rtab_ref, out_ref, left_ref, right_ref, *slots):
-    rhs, panels = out_ref.shape
+def self_body(rowblk, width, own_ref, ltab_ref, rtab_ref, out_ref, left_ref, right_ref, *slots):
+    _, rhs, panels = out_ref.shape
     features = own_ref[rhs:, :]
     left_ref[...] = left_side(features, ltab_ref[...])
     right_ref[...] = right_side(features, rtab_ref[...])
     out_ref[...] = jnp.zeros_like(out_ref)
 
-    def make(step):
+    def make(step, strip):
         start = pl.multiple_of(step * rowblk, rowblk)
-        return tile_of(left_ref[pl.ds(start, rowblk), :], right_ref[...])
-
-    def use(step, tile):
+        return tile_of(left_ref[pl.ds(start, rowblk), :], right_ref[:, strip : strip + width])
+
+    def use(step, tile, strip, carry):
+        if tile is None:
+            return
         start = pl.multiple_of(step * rowblk, rowblk)
-        out_ref[...] += jnp.dot(
+        out_ref[0, :, strip : strip + width] += jnp.dot(
             own_ref[0:rhs, pl.ds(start, rowblk)], tile, preferred_element_type=F32
         )
 
-    two_stage(panels // rowblk, make, use, slots)
+    two_stage(panels // rowblk, make, use, slots, width)
 
 
 def self_field(own, tables):
     rows, panels = own.shape
     rhs = rows - FEATURES
-    rowblk = 256
+    rowblk, width = blocking(panels)
     return in_vmem(
-        functools.partial(self_body, rowblk),
-        jax.ShapeDtypeStruct((rhs, panels), F32),
+        functools.partial(self_body, rowblk, width),
+        jax.ShapeDtypeStruct((2, rhs, panels), F32),
         [
             pltpu.VMEM((panels, DEPTH), BF16),
             pltpu.VMEM((DEPTH, panels), BF16),
             pltpu.VMEM((rowblk, panels), BF16),
             pltpu.VMEM((rowblk, panels), BF16),
         ],
-        flops=2 * 400 * panels * panels,
+        flops=0,
     )(own, *tables)
 
 
 def pairs_body(
-    rowblk, last, pair_ref, far_ref, ltab_ref, rtab_ref, field_in, totals_in,
+    rowblk, width, last, pair_ref, far_ref, ltab_ref, rtab_ref, field_in, totals_in,
     field_ref, back_ref, totals_ref, left_ref, right_ref, sum_ref, *slots
 ):
     blocks, rhs, panels = field_ref.shape
@@ -184,20 +198,27 @@
         start = pl.multiple_of((step % chunks) * rowblk, rowblk)
         return turn // blocks, turn % blocks, start
 
-    def make(step):
+    def make(step, strip):
         far, own, start = place(step)
-        return tile_of(left_ref[far, pl.ds(start, rowblk), :], right_ref[own])
-
-    def use(step, tile):
+        return tile_of(
+            left_ref[far, pl.ds(start, rowblk), :], right_ref[own, :, strip : strip + width]
+        )
+
+    def use(step, tile, strip, carry):
         far, own, start = place(step)
-        field_ref[own] += jnp.dot(
+        if tile is None:
+            sum_ref[far, :, pl.ds(start, rowblk)] += carry
+            return
+        part = lax.dot_general(
+            pair_ref[own, 0:rhs, strip : strip + width], tile, (((1,), (1,)), ((), ())),
+            preferred_element_type=F32,
+        )
+        field_ref[own, :, strip : strip + width] += jnp.dot(
             far_ref[far, 0:rhs, pl.ds(start, rowblk)], tile, preferred_element_type=F32
         )
-        sum_ref[far, :, pl.ds(start, rowblk)] += lax.dot_general(
-            pair_ref[own, 0:rhs, :], tile, (((1,), (1,)), ((), ())), preferred_element_type=F32
-        )
-
-    two_stage(blocks * blocks * chunks, make, use, slots)
+        return part if carry is None else carry + part
+
+    two_stage(blocks * blocks * chunks, make, use, slots, width)
     totals = totals_in[...]
     for block in range(blocks):
         totals = totals + totals_of(sum_ref[block], far_ref[block])
@@ -210,9 +231,10 @@
 def pairs_field(pair, far, tables, field, totals, last):
     blocks, rows, panels = pair.shape
     rhs = rows - FEATURES
-    rowblk = 256
+    rowblk, width = blocking(panels)
+    work = 800 * panels * panels * blocks * blocks
     return in_vmem(
-        functools.partial(pairs_body, rowblk, last),
+        functools.partial(pairs_body, rowblk, width, last),
         (
             jax.ShapeDtypeStruct((blocks, rhs, panels), F32),
             jax.ShapeDtypeStruct((blocks, rhs, panels), BF16),
@@ -225,17 +247,19 @@
             pltpu.VMEM((rowblk, panels), BF16),
             pltpu.VMEM((rowblk, panels), BF16),
         ],
-        flops=2 * 400 * panels * panels * blocks * blocks,
+        flops=work if last else 0,
     )(pair, far, *tables, field, totals)
 
 
 def near_body(
-    twin_ref, own_ref, other_ref, index_ref, count_ref, odd_ref, weight_ref, out_ref, ext_ref
+    twin_ref, own_ref, other_ref, index_ref, count_ref, odd_ref, weight_ref, field_in,
+    field_ref, ext_ref
 ):
     rhs, panels = own_ref.shape
     groups, near = index_ref.shape
     for side, ref in enumerate((twin_ref, own_ref, other_ref)):
         ext_ref[:, side * panels : (side + 1) * panels] = ref[...].astype(F32)
+    field_ref[...] = field_in[...]
     turn = jnp.where(odd_ref[0] == 1, 0, 2 * panels)
 
     @pl.loop(0, groups)
@@ -254,29 +278,24 @@
             )
             taken = jnp.where(piece == part, found, taken)
         width = weight_ref.shape[1]
-        out_ref[:, pl.ds(pl.multiple_of(group * width, width), width)] = lax.dot_general(
+        field_ref[0, :, pl.ds(pl.multiple_of(group * width, width), width)] += lax.dot_general(
             taken.astype(BF16), weight_ref[group], (((1,), (1,)), ((), ())),
             preferred_element_type=F32,
         )
 
 
-def near_field(twin, own, other, index, count, odd, weight):
+def near_field(twin, own, other, index, count, odd, weight, field):
     rhs, panels = own.shape
     vmem = pl.BlockSpec(memory_space=pltpu.VMEM)
     return pl.pallas_call(
         near_body,
-        out_shape=jax.ShapeDtypeStruct((rhs, panels), F32),
-        in_specs=[vmem] * 4 + [pl.BlockSpec(memory_space=pltpu.SMEM)] * 2 + [vmem],
+        out_shape=jax.ShapeDtypeStruct(field.shape, F32),
+        in_specs=[vmem] * 4 + [pl.BlockSpec(memory_space=pltpu.SMEM)] * 2 + [vmem] * 2,
         out_specs=vmem,
         scratch_shapes=[pltpu.VMEM((rhs, 3 * panels), F32)],
         compiler_params=pltpu.CompilerParams(vmem_limit_bytes=VMEM_LIMIT),
-        cost_estimate=pl.CostEstimate(flops=2 * 10**9, bytes_accessed=2**20, transcendentals=0),
-    )(twin, own, other, index, count, odd, weight)
-
-
-def start_body(self_ref, near_ref, field_ref):
-    field_ref[0] = self_ref[...] + near_ref[...]
-    field_ref[1] = jnp.zeros_like(self_ref)
+        cost_estimate=pl.CostEstimate(flops=0, bytes_accessed=2**10, transcendentals=0),
+    )(twin, own, other, index, count, odd, weight, field)
 
 
 def send(value, source_of):
@@ -292,7 +311,7 @@
 def paired_blocks(geometry, charges, near_index, near_count, near_weight, conductor):
     cols = lax.axis_size("col")
     core, flip_x, far_z = cols, 2 * cols, cols // 2
-    rhs, panels = charges.shape
+    rhs = charges.shape[0]
 
     def partner(d, far):
         second = bool(d & core)
@@ -311,21 +330,23 @@
     far = send(pair, lambda d: partner(d, True))
     twin = send(charges, lambda d: d ^ 1)
     other = send(charges, other_neighbour)
-    own = self_field(bundle, tables)
     odd = (lax.axis_index(AXES) % 2).reshape(1)
-    near = near_field(twin, charges, other, near_index, near_count, odd, near_weight)
-    pair_shape = (2, rhs, panels)
-    field = in_vmem(start_body, jax.ShapeDtypeStruct(pair_shape, F32))(own, near)
+    field = self_field(bundle, tables)
     totals = jnp.zeros((rhs, rhs), F32)
     field, close_back, totals = pairs_field(pair, close, tables, field, totals, False)
+    field = near_field(twin, charges, other, near_index, near_count, odd, near_weight, field)
     close_back = send_back(close_back, lambda d: partner(d, False))
     field, far_back, totals = pairs_field(pair, far, tables, field, totals, True)
     far_back = send_back(far_back, lambda d: partner(d, True))
-    for step in (core, 1, flip_x, 2, far_z):
+    close_back, totals = lax.optimization_barrier((close_back, totals))
+    for step in (core, 1, flip_x):
         totals = totals + send(totals, lambda d: d ^ step)
+    far_back, totals = lax.optimization_barrier((far_back, totals))
     back = close_back.astype(F32) + far_back.astype(F32)
     field = field + back
     twin_part = send(field[1].astype(BF16), lambda d: d ^ core)
+    for step in (2, far_z):
+        totals = totals + send(totals, lambda d: d ^ step)
     return (field[0] + twin_part.astype(F32), totals)
 
 

time: 86.6 us -> 76.4 us (0.88)
  waiting for transfers between devices: 28.7 us -> 13.7 us
  starting transfers between devices: 16.3 us -> 27.3 us
  Pallas kernels: 37.1 us -> 30.2 us
    ppermute x2, waiting for transfers between devices: 9.34 us -> 0.01 us  [send_back(): return lax.ppermute(value, AXES, [(d, source_of(d)) for d in range(count)])]
    ppermute x2, starting transfers between devices: 1.78 us -> 8.9 us  [send_back(): return lax.ppermute(value, AXES, [(d, source_of(d)) for d in range(count)])]
    pallas_call x5 -> x4, Pallas kernels: 36.1 us -> 29.1 us  [the longest x2 22.7 us: pairs_field(): in_vmem(functools.partial(pairs_body, rowblk, width, last), (jax.ShapeDty...]
    ppermute x11, waiting for transfers between devices: 19.3 us -> 13.7 us  [send(): return lax.ppermute(value, AXES, [(source_of(d), d) for d in range(count)])]
    ppermute x11, starting transfers between devices: 14.6 us -> 18.4 us  [send(): return lax.ppermute(value, AXES, [(source_of(d), d) for d in range(count)])]
  transfers between devices with their start and end apart: 13 -> 13, of which waited for: 7 -> 7; matrix products, arithmetic and copies ran while one was open for 1% -> 1% of each run, Pallas kernels for 42% -> 38%
where the time goes in v1:
time: 76.4 us; the launch traced here: 76.1 us
  Pallas kernels  30.2 us (40%)
  starting transfers between devices  27.3 us (36%)
  waiting for transfers between devices  13.7 us (18%)
  local copies, waits for them, and re-layouts  2.81 us (4%)
  other arithmetic  1.41 us (2%)
    pallas_call x2, Pallas kernels, pairs_field(): in_vmem(functools.partial(pairs_body, rowblk, width, last), (jax.ShapeDty...  22.7 us
    ppermute x11, starting transfers between devices, send(): return lax.ppermute(value, AXES, [(source_of(d), d) for d in range(count)])  18.4 us
    ppermute x11, waiting for transfers between devices, send(): return lax.ppermute(value, AXES, [(source_of(d), d) for d in range(count)])  13.7 us
    ppermute x2, starting transfers between devices, send_back(): return lax.ppermute(value, AXES, [(d, source_of(d)) for d in range(count)])  8.9 us
    pallas_call x1, Pallas kernels, near_field(): pl.pallas_call(near_body, out_shape=jax.ShapeDtypeStruct(field.shape, F32...  4.26 us
    pallas_call x1, Pallas kernels, self_field(): in_vmem(functools.partial(self_body, rowblk, width), jax.ShapeDtypeStruct...  2.19 us
    unnamed x12, local copies, waits for them, and re-layouts  2.09 us
  transfers between devices with their start and end apart: 13, of which 7 were waited for; matrix products, arithmetic and copies ran while one was open for 1% of the time, Pallas kernels for 38%

profile of v1, /device:TPU:0, one launch (start us, length us, event | category | flops | bytes accessed | tf_op | source)
XLA Modules:
  0.0 76.1 jit_solution(7708619178237107750)
XLA Ops:
  0.6 0.7 reshape.11.conductor_ref
  1.3 0.0 copy-start.3
  1.3 0.7 copy-done.3
  2.1 1.0 %shard_map.95.own_ref = bf16[48,1536]{1,0:T(8,128)(2,1)S(1)} custom-call(f32[4,1536]{1,0:T(4,128)S(1)} %copy-done.3, bf16[32,1536]{1,0:T(8,128)(2,1)} %own_ref.1, s32[1,1536]{1,0:T(1,128)S(1)} %reshape.11.conductor_ref), custom_call_target="tpu_custom_call" | custom-call | bytes 1024 | tf_op jit(solution)/shard_map/pallas_call | solution.py:86
  3.1 0.5 collective-permute-start
  3.6 1.0 %collective-permute-done = bf16[48,1536]{1,0:T(8,128)(2,1)S(1)} collective-permute-done((bf16[48,1536]{1,0:T(8,128)(2,1)S(1)}, bf16[48,1536]{1,0:T(8,128)(2,1)S(1)}, u32[]{:S(2)}, u32[]{:S(2)}) %collective-permute-start) | collective-permute-done | bytes 147488 | tf_op jit(solution)/shard_map/ppermute | solution.py:303
  4.7 3.9 %collective-permute-start.4 = (bf16[2,48,1536]{2,1,0:T(8,128)(2,1)S(1)}, bf16[2,48,1536]{2,1,0:T(8,128)(2,1)S(1)}, u32[]{:S(2)}, u32[]{:S(2)}) collective-permute-start(bf16[2,48,1536]{2,1,0:T(8,128)(2,1)S(1)} %pad_maximum_fusion.pair_ref), channel_id=1, source_target_pairs={{1,0},{16,1},{3,2},{18,3},{5,4},{20,5},{7,6},{22,7},{27,8},{10,9},... | collective-permute-start | bytes 884744 | tf_op jit(solution)/shard_map/ppermute | solution.py:303
  8.5 2.5 %collective-permute-start.1 = (bf16[2,48,1536]{2,1,0:T(8,128)(2,1)S(1)}, bf16[2,48,1536]{2,1,0:T(8,128)(2,1)S(1)}, u32[]{:S(2)}, u32[]{:S(2)}) collective-permute-start(bf16[2,48,1536]{2,1,0:T(8,128)(2,1)S(1)} %pad_maximum_fusion.pair_ref), channel_id=1, source_target_pairs={{5,0},{20,1},{7,2},{22,3},{1,4},{16,5},{3,6},{18,7},{31,8},{14,9},... | collective-permute-start | bytes 884744 | tf_op jit(solution)/shard_map/ppermute | solution.py:303
  11.0 1.5 %collective-permute-start.2 = (bf16[32,1536]{1,0:T(8,128)(2,1)}, bf16[32,1536]{1,0:T(8,128)(2,1)S(1)}, u32[]{:S(2)}, u32[]{:S(2)}) collective-permute-start(bf16[32,1536]{1,0:T(8,128)(2,1)} %own_ref.1), channel_id=1, source_target_pairs={{1,0},{0,1},{3,2},{2,3},{5,4},{4,5},{7,6},{6,7},{9,8},{8,9},{11,10... | collective-permute-start | bytes 294920 | tf_op jit(solution)/shard_map/ppermute | solution.py:303
  12.6 1.1 %collective-permute-start.3 = (bf16[32,1536]{1,0:T(8,128)(2,1)}, bf16[32,1536]{1,0:T(8,128)(2,1)S(1)}, u32[]{:S(2)}, u32[]{:S(2)}) collective-permute-start(bf16[32,1536]{1,0:T(8,128)(2,1)} %own_ref.1), channel_id=1, source_target_pairs={{31,0},{2,1},{1,2},{4,3},{3,4},{6,5},{5,6},{8,7},{7,8},{10,9},{9,1... | collective-permute-start | bytes 294920 | tf_op jit(solution)/shard_map/ppermute | solution.py:303
  13.6 0.0 copy-start.2
  13.6 0.0 copy-start.1
  13.6 0.7 copy-done.2
  14.3 0.0 copy-done.1
  14.3 2.2 %shard_map.96.field_in = f32[2,32,1536]{2,1,0:T(8,128)S(1)} custom-call(bf16[48,1536]{1,0:T(8,128)(2,1)S(1)} %shard_map.95.own_ref, bf16[32,16]{1,0:T(8,128)(2,1)S(1)} %copy-done.1, bf16[32,16]{1,0:T(8,128)(2,1)S(1)} %copy-done.2), custom_call_target="tpu_custom_call" | custom-call | bytes 1024 | tf_op jit(solution)/shard_map/pallas_call | solution.py:171
  16.5 1.7 %collective-permute-done.4.far_ref = bf16[2,48,1536]{2,1,0:T(8,128)(2,1)S(1)} collective-permute-done((bf16[2,48,1536]{2,1,0:T(8,128)(2,1)S(1)}, bf16[2,48,1536]{2,1,0:T(8,128)(2,1)S(1)}, u32[]{:S(2)}, u32[]{:S(2)}) %collective-permute-start.4) | collective-permute-done | bytes 294944 | tf_op jit(solution)/shard_map/ppermute | solution.py:303
  18.2 0.0 copy-start
  18.2 0.0 copy-start.4
  18.2 11.3 %shard_map.97 = (f32[2,32,1536]{2,1,0:T(8,128)S(1)}, bf16[2,32,1536]{2,1,0:T(8,128)(2,1)S(1)}, f32[32,32]{1,0:T(8,128)S(1)}) custom-call(bf16[2,48,1536]{2,1,0:T(8,128)(2,1)S(1)} %pad_maximum_fusion.pair_ref, bf16[2,48,1536]{2,1,0:T(8,128)(2,1)S(1)} %collective-permute-done.4.far_ref, bf16[32,16]{1,0:T(8,128)(2,1)S(1)} %copy-done.1, ...), custom_call_target="tpu_custom_call" | custom-call | bytes 1024 | tf_op jit(solution)/shard_map/pallas_call | solution.py:236
  29.5 4.2 %collective-permute-start.5 = (bf16[2,32,1536]{2,1,0:T(8,128)(2,1)S(1)}, bf16[2,32,1536]{2,1,0:T(8,128)(2,1)S(1)}, u32[]{:S(2)}, u32[]{:S(2)}) collective-permute-start(bf16[2,32,1536]{2,1,0:T(8,128)(2,1)S(1)} %get-tuple-element.15), channel_id=1, source_target_pairs={{0,1},{1,16},{2,3},{3,18},{4,5},{5,20},{6,7},{7,22},{8,27},{9,10},... | collective-permute-start | bytes 589832 | tf_op jit(solution)/shard_map/ppermute | solution.py:308
  33.7 0.0 collective-permute-done.2.twin_ref
  33.7 0.0 collective-permute-done.3.other_ref
  33.7 0.0 copy-start.5
  33.7 0.0 copy-done
  33.7 0.0 copy-done.4
  33.7 0.6 copy-done.5
  34.3 4.3 %shard_map.98.field_in = f32[2,32,1536]{2,1,0:T(8,128)S(1)} custom-call(bf16[32,1536]{1,0:T(8,128)(2,1)S(1)} %collective-permute-done.2.twin_ref, bf16[32,1536]{1,0:T(8,128)(2,1)} %own_ref.1, bf16[32,1536]{1,0:T(8,128)(2,1)S(1)} %collective-permute-done.3.other_ref, s32[12,128]{1,0:T(8,128)S(1)} %copy-done.4, s32[12]{0:T(128)S(1)} %copy-done.5, ...), custom_call_target="tpu_custom_call" | custom-call | bytes 1024 | tf_op jit(solution)/shard_map/pallas_call | solution.py:290
  38.6 0.0 collective-permute-done.1.far_ref
  38.6 11.4 %shard_map.99 = (f32[2,32,1536]{2,1,0:T(8,128)S(1)}, bf16[2,32,1536]{2,1,0:T(8,128)(2,1)S(1)}, f32[32,32]{1,0:T(8,128)S(1)}) custom-call(bf16[2,48,1536]{2,1,0:T(8,128)(2,1)S(1)} %pad_maximum_fusion.pair_ref, bf16[2,48,1536]{2,1,0:T(8,128)(2,1)S(1)} %collective-permute-done.1.far_ref, bf16[32,16]{1,0:T(8,128)(2,1)S(1)} %copy-done.1, ...), custom_call_target="tpu_custom_call" | custom-call | flops 7549747200 | bytes 1024 | tf_op jit(solution)/shard_map/pallas_call | solution.py:236
  50.0 4.7 %collective-permute-start.6 = (bf16[2,32,1536]{2,1,0:T(8,128)(2,1)S(1)}, bf16[2,32,1536]{2,1,0:T(8,128)(2,1)S(1)}, u32[]{:S(2)}, u32[]{:S(2)}) collective-permute-start(bf16[2,32,1536]{2,1,0:T(8,128)(2,1)S(1)} %get-tuple-element.18), channel_id=1, source_target_pairs={{0,5},{1,20},{2,7},{3,22},{4,1},{5,16},{6,3},{7,18},{8,31},{9,14},... | collective-permute-start | bytes 589832 | tf_op jit(solution)/shard_map/ppermute | solution.py:308
  54.8 0.0 collective-permute-done.5
  54.8 0.0 collective-permute-start.7
  54.8 1.2 %collective-permute-done.7 = f32[32,32]{1,0:T(8,128)S(1)} collective-permute-done((f32[32,32]{1,0:T(8,128)S(1)}, f32[32,32]{1,0:T(8,128)S(1)}, u32[]{:S(2)}, u32[]{:S(2)}) %collective-permute-start.7) | collective-permute-done | bytes 4128 | tf_op jit(solution)/shard_map/ppermute | solution.py:303
  56.0 2.4 %collective-permute-start.8 = (f32[32,32]{1,0:T(8,128)S(1)}, f32[32,32]{1,0:T(8,128)S(1)}, u32[]{:S(2)}, u32[]{:S(2)}) collective-permute-start(f32[32,32]{1,0:T(8,128)S(1)} %add.33), channel_id=1, source_target_pairs={{1,0},{0,1},{3,2},{2,3},{5,4},{4,5},{7,6},{6,7},{9,8},{8,9},{11,10... | collective-permute-start | bytes 12296 | tf_op jit(solution)/shard_map/ppermute | solution.py:303
  58.4 1.7 %collective-permute-done.8 = f32[32,32]{1,0:T(8,128)S(1)} collective-permute-done((f32[32,32]{1,0:T(8,128)S(1)}, f32[32,32]{1,0:T(8,128)S(1)}, u32[]{:S(2)}, u32[]{:S(2)}) %collective-permute-start.8) | collective-permute-done | bytes 4128 | tf_op jit(solution)/shard_map/ppermute | solution.py:303
  60.1 0.6 collective-permute-start.9
  60.7 3.2 %collective-permute-done.9 = f32[32,32]{1,0:T(8,128)S(1)} collective-permute-done((f32[32,32]{1,0:T(8,128)S(1)}, f32[32,32]{1,0:T(8,128)S(1)}, u32[]{:S(2)}, u32[]{:S(2)}) %collective-permute-start.9) | collective-permute-done | bytes 4128 | tf_op jit(solution)/shard_map/ppermute | solution.py:303
  63.8 0.0 collective-permute-done.6
  63.8 0.1 add_add_fusion
  63.9 0.1 collective-permute-start.10
  64.0 4.4 %collective-permute-start.11 = (f32[32,32]{1,0:T(8,128)S(1)}, f32[32,32]{1,0:T(8,128)S(1)}, u32[]{:S(2)}, u32[]{:S(2)}) collective-permute-start(f32[32,32]{1,0:T(8,128)S(1)} %add.35), channel_id=1, source_target_pairs={{2,0},{3,1},{0,2},{1,3},{6,4},{7,5},{4,6},{5,7},{10,8},{11,9},{8,1... | collective-permute-start | bytes 12296 | tf_op jit(solution)/shard_map/ppermute | solution.py:303
  68.4 1.7 %collective-permute-done.11 = f32[32,32]{1,0:T(8,128)S(1)} collective-permute-done((f32[32,32]{1,0:T(8,128)S(1)}, f32[32,32]{1,0:T(8,128)S(1)}, u32[]{:S(2)}, u32[]{:S(2)}) %collective-permute-start.11) | collective-permute-done | bytes 4128 | tf_op jit(solution)/shard_map/ppermute | solution.py:303
  70.1 1.5 %collective-permute-start.12 = (f32[32,32]{1,0:T(8,128)S(1)}, f32[32,32]{1,0:T(8,128)S(1)}, u32[]{:S(2)}, u32[]{:S(2)}) collective-permute-start(f32[32,32]{1,0:T(8,128)S(1)} %add.39), channel_id=1, source_target_pairs={{4,0},{5,1},{6,2},{7,3},{0,4},{1,5},{2,6},{3,7},{12,8},{13,9},{14,... | collective-permute-start | bytes 12296 | tf_op jit(solution)/shard_map/ppermute | solution.py:303
  71.6 3.2 %collective-permute-done.12 = f32[32,32]{1,0:T(8,128)S(1)} collective-permute-done((f32[32,32]{1,0:T(8,128)S(1)}, f32[32,32]{1,0:T(8,128)S(1)}, u32[]{:S(2)}, u32[]{:S(2)}) %collective-permute-start.12) | collective-permute-done | bytes 4128 | tf_op jit(solution)/shard_map/ppermute | solution.py:303
  74.8 0.6 add.40
  75.4 0.0 collective-permute-done.10
  75.4 0.7 fusion
  (7 shorter events, 0.1 us)
Async XLA Ops:
  1.3 0.7 copy-start.3
  3.1 1.5 %collective-permute-start = (bf16[48,1536]{1,0:T(8,128)(2,1)S(1)}, bf16[48,1536]{1,0:T(8,128)(2,1)S(1)}, u32[]{:S(2)}, u32[]{:S(2)}) collective-permute-start(bf16[48,1536]{1,0:T(8,128)(2,1)S(1)} %shard_map.95.own_ref), channel_id=1, source_target_pairs={{8,0},{9,1},{10,2},{11,3},{12,4},{13,5},{14,6},{15,7},{0,8},{1,9},... | collective-permute-start | bytes 442376 | tf_op jit(solution)/shard_map/ppermute | solution.py:303
  4.7 13.6 %collective-permute-start.4 = (bf16[2,48,1536]{2,1,0:T(8,128)(2,1)S(1)}, bf16[2,48,1536]{2,1,0:T(8,128)(2,1)S(1)}, u32[]{:S(2)}, u32[]{:S(2)}) collective-permute-start(bf16[2,48,1536]{2,1,0:T(8,128)(2,1)S(1)} %pad_maximum_fusion.pair_ref), channel_id=1, source_target_pairs={{1,0},{16,1},{3,2},{18,3},{5,4},{20,5},{7,6},{22,7},{27,8},{10,9},... | collective-permute-start | bytes 884744 | tf_op jit(solution)/shard_map/ppermute | solution.py:303
  8.5 30.1 %collective-permute-start.1 = (bf16[2,48,1536]{2,1,0:T(8,128)(2,1)S(1)}, bf16[2,48,1536]{2,1,0:T(8,128)(2,1)S(1)}, u32[]{:S(2)}, u32[]{:S(2)}) collective-permute-start(bf16[2,48,1536]{2,1,0:T(8,128)(2,1)S(1)} %pad_maximum_fusion.pair_ref), channel_id=1, source_target_pairs={{5,0},{20,1},{7,2},{22,3},{1,4},{16,5},{3,6},{18,7},{31,8},{14,9},... | collective-permute-start | bytes 884744 | tf_op jit(solution)/shard_map/ppermute | solution.py:303
  11.0 22.6 %collective-permute-start.2 = (bf16[32,1536]{1,0:T(8,128)(2,1)}, bf16[32,1536]{1,0:T(8,128)(2,1)S(1)}, u32[]{:S(2)}, u32[]{:S(2)}) collective-permute-start(bf16[32,1536]{1,0:T(8,128)(2,1)} %own_ref.1), channel_id=1, source_target_pairs={{1,0},{0,1},{3,2},{2,3},{5,4},{4,5},{7,6},{6,7},{9,8},{8,9},{11,10... | collective-permute-start | bytes 294920 | tf_op jit(solution)/shard_map/ppermute | solution.py:303
  12.6 21.1 %collective-permute-start.3 = (bf16[32,1536]{1,0:T(8,128)(2,1)}, bf16[32,1536]{1,0:T(8,128)(2,1)S(1)}, u32[]{:S(2)}, u32[]{:S(2)}) collective-permute-start(bf16[32,1536]{1,0:T(8,128)(2,1)} %own_ref.1), channel_id=1, source_target_pairs={{31,0},{2,1},{1,2},{4,3},{3,4},{6,5},{5,6},{8,7},{7,8},{10,9},{9,1... | collective-permute-start | bytes 294920 | tf_op jit(solution)/shard_map/ppermute | solution.py:303
  13.6 0.7 copy-start.2
  13.6 0.7 copy-start.1
  18.2 15.4 %copy-start = (bf16[12,128,128]{2,1,0:T(8,128)(2,1)S(1)}, bf16[12,128,128]{2,1,0:T(8,128)(2,1)}, u32[]{:S(2)}) copy-start(bf16[12,128,128]{2,1,0:T(8,128)(2,1)} %weight_ref.1) | copy-start | bytes 1179652
  18.2 15.5 %copy-start.4 = (s32[12,128]{1,0:T(8,128)S(1)}, s32[12,128]{1,0:T(8,128)}, u32[]{:S(2)}) copy-start(s32[12,128]{1,0:T(8,128)} %index_ref.1) | copy-start | bytes 18436
  29.5 25.3 %collective-permute-start.5 = (bf16[2,32,1536]{2,1,0:T(8,128)(2,1)S(1)}, bf16[2,32,1536]{2,1,0:T(8,128)(2,1)S(1)}, u32[]{:S(2)}, u32[]{:S(2)}) collective-permute-start(bf16[2,32,1536]{2,1,0:T(8,128)(2,1)S(1)} %get-tuple-element.15), channel_id=1, source_target_pairs={{0,1},{1,16},{2,3},{3,18},{4,5},{5,20},{6,7},{7,22},{8,27},{9,10},... | collective-permute-start | bytes 589832 | tf_op jit(solution)/shard_map/ppermute | solution.py:308
  33.7 0.7 copy-start.5
  50.0 13.8 %collective-permute-start.6 = (bf16[2,32,1536]{2,1,0:T(8,128)(2,1)S(1)}, bf16[2,32,1536]{2,1,0:T(8,128)(2,1)S(1)}, u32[]{:S(2)}, u32[]{:S(2)}) collective-permute-start(bf16[2,32,1536]{2,1,0:T(8,128)(2,1)S(1)} %get-tuple-element.18), channel_id=1, source_target_pairs={{0,5},{1,20},{2,7},{3,22},{4,1},{5,16},{6,3},{7,18},{8,31},{9,14},... | collective-permute-start | bytes 589832 | tf_op jit(solution)/shard_map/ppermute | solution.py:308
  54.8 1.2 %collective-permute-start.7 = (f32[32,32]{1,0:T(8,128)S(1)}, f32[32,32]{1,0:T(8,128)S(1)}, u32[]{:S(2)}, u32[]{:S(2)}) collective-permute-start(f32[32,32]{1,0:T(8,128)S(1)} %get-tuple-element.19), channel_id=1, source_target_pairs={{8,0},{9,1},{10,2},{11,3},{12,4},{13,5},{14,6},{15,7},{0,8},{1,9},... | collective-permute-start | bytes 12296 | tf_op jit(solution)/shard_map/ppermute | solution.py:303
  56.0 4.1 %collective-permute-start.8 = (f32[32,32]{1,0:T(8,128)S(1)}, f32[32,32]{1,0:T(8,128)S(1)}, u32[]{:S(2)}, u32[]{:S(2)}) collective-permute-start(f32[32,32]{1,0:T(8,128)S(1)} %add.33), channel_id=1, source_target_pairs={{1,0},{0,1},{3,2},{2,3},{5,4},{4,5},{7,6},{6,7},{9,8},{8,9},{11,10... | collective-permute-start | bytes 12296 | tf_op jit(solution)/shard_map/ppermute | solution.py:303
  60.1 3.7 %collective-permute-start.9 = (f32[32,32]{1,0:T(8,128)S(1)}, f32[32,32]{1,0:T(8,128)S(1)}, u32[]{:S(2)}, u32[]{:S(2)}) collective-permute-start(f32[32,32]{1,0:T(8,128)S(1)} %add.34), channel_id=1, source_target_pairs={{16,0},{17,1},{18,2},{19,3},{20,4},{21,5},{22,6},{23,7},{24,8},{25... | collective-permute-start | bytes 12296 | tf_op jit(solution)/shard_map/ppermute | solution.py:303
  63.9 11.4 %collective-permute-start.10 = (bf16[32,1536]{1,0:T(8,128)(2,1)S(1)}, bf16[32,1536]{1,0:T(8,128)(2,1)S(1)}, u32[]{:S(2)}, u32[]{:S(2)}) collective-permute-start(bf16[32,1536]{1,0:T(8,128)(2,1)S(1)} %fusion.1), channel_id=1, source_target_pairs={{8,0},{9,1},{10,2},{11,3},{12,4},{13,5},{14,6},{15,7},{0,8},{1,9},... | collective-permute-start | bytes 294920 | tf_op jit(solution)/shard_map/ppermute | solution.py:303
  64.0 6.1 %collective-permute-start.11 = (f32[32,32]{1,0:T(8,128)S(1)}, f32[32,32]{1,0:T(8,128)S(1)}, u32[]{:S(2)}, u32[]{:S(2)}) collective-permute-start(f32[32,32]{1,0:T(8,128)S(1)} %add.35), channel_id=1, source_target_pairs={{2,0},{3,1},{0,2},{1,3},{6,4},{7,5},{4,6},{5,7},{10,8},{11,9},{8,1... | collective-permute-start | bytes 12296 | tf_op jit(solution)/shard_map/ppermute | solution.py:303
  70.1 4.6 %collective-permute-start.12 = (f32[32,32]{1,0:T(8,128)S(1)}, f32[32,32]{1,0:T(8,128)S(1)}, u32[]{:S(2)}, u32[]{:S(2)}) collective-permute-start(f32[32,32]{1,0:T(8,128)S(1)} %add.39), channel_id=1, source_target_pairs={{4,0},{5,1},{6,2},{7,3},{0,4},{1,5},{2,6},{3,7},{12,8},{13,9},{14,... | collective-permute-start | bytes 12296 | tf_op jit(solution)/shard_map/ppermute | solution.py:303

commit v2 on v1

--- a/solution.py
+++ b/solution.py
@@ -182,7 +182,7 @@
 
 
 def pairs_body(
-    rowblk, width, last, pair_ref, far_ref, ltab_ref, rtab_ref, field_in, totals_in,
+    rowblk, width, pair_ref, far_ref, ltab_ref, rtab_ref, field_in, totals_in,
     field_ref, back_ref, totals_ref, left_ref, right_ref, sum_ref, *slots
 ):
     blocks, rhs, panels = field_ref.shape
@@ -222,8 +222,6 @@
     totals = totals_in[...]
     for block in range(blocks):
         totals = totals + totals_of(sum_ref[block], far_ref[block])
-        if last:
-            totals = totals + totals_of(field_ref[block], pair_ref[block])
     totals_ref[...] = totals
     back_ref[...] = sum_ref[...].astype(BF16)
 
@@ -234,7 +232,7 @@
     rowblk, width = blocking(panels)
     work = 800 * panels * panels * blocks * blocks
     return in_vmem(
-        functools.partial(pairs_body, rowblk, width, last),
+        functools.partial(pairs_body, rowblk, width),
         (
             jax.ShapeDtypeStruct((blocks, rhs, panels), F32),
             jax.ShapeDtypeStruct((blocks, rhs, panels), BF16),
@@ -252,8 +250,8 @@
 
 
 def near_body(
-    twin_ref, own_ref, other_ref, index_ref, count_ref, odd_ref, weight_ref, field_in,
-    field_ref, ext_ref
+    twin_ref, own_ref, other_ref, index_ref, count_ref, odd_ref, weight_ref, field_in, totals_in,
+    pair_ref, field_ref, totals_ref, ext_ref
 ):
     rhs, panels = own_ref.shape
     groups, near = index_ref.shape
@@ -283,19 +281,37 @@
             preferred_element_type=F32,
         )
 
-
-def near_field(twin, own, other, index, count, odd, weight, field):
+    totals = totals_in[...]
+    for block in range(field_ref.shape[0]):
+        totals = totals + totals_of(field_ref[block], pair_ref[block])
+    height = totals_ref.shape[1]
+    flat = jnp.concatenate([totals[r : r + height, :] for r in range(0, rhs, height)], axis=1)
+    totals_ref[...] = jnp.broadcast_to(flat[None], totals_ref.shape)
+
+
+def near_field(twin, own, other, index, count, odd, weight, field, totals, pair):
     rhs, panels = own.shape
     vmem = pl.BlockSpec(memory_space=pltpu.VMEM)
     return pl.pallas_call(
         near_body,
-        out_shape=jax.ShapeDtypeStruct(field.shape, F32),
-        in_specs=[vmem] * 4 + [pl.BlockSpec(memory_space=pltpu.SMEM)] * 2 + [vmem] * 2,
-        out_specs=vmem,
+        out_shape=(
+            jax.ShapeDtypeStruct(field.shape, F32),
+            jax.ShapeDtypeStruct((lax.axis_size(AXES), rhs * rhs // 128, 128), F32),
+        ),
+        in_specs=[vmem] * 4 + [pl.BlockSpec(memory_space=pltpu.SMEM)] * 2 + [vmem] * 4,
+        out_specs=(vmem, vmem),
         scratch_shapes=[pltpu.VMEM((rhs, 3 * panels), F32)],
         compiler_params=pltpu.CompilerParams(vmem_limit_bytes=VMEM_LIMIT),
-        cost_estimate=pl.CostEstimate(flops=0, bytes_accessed=2**10, transcendentals=0),
-    )(twin, own, other, index, count, odd, weight, field)
+        cost_estimate=pl.CostEstimate(flops=4 * 10**9, bytes_accessed=2**10, transcendentals=0),
+    )(twin, own, other, index, count, odd, weight, field, totals, pair)
+
+
+def finish_body(field_ref, part_ref, totals_ref, potential_out, totals_out):
+    potential_out[...] = field_ref[0] + part_ref[...].astype(F32)
+    total = jnp.sum(totals_ref[...], axis=0)
+    rhs, height = totals_out.shape[0], total.shape[0]
+    for turn in range(rhs // height):
+        totals_out[turn * height : (turn + 1) * height, :] = total[:, turn * rhs : (turn + 1) * rhs]
 
 
 def send(value, source_of):
@@ -327,27 +343,29 @@
     sibling = send(bundle, lambda d: d ^ core)
     pair = jnp.stack([bundle, sibling])
     close = send(pair, lambda d: partner(d, False))
-    far = send(pair, lambda d: partner(d, True))
-    twin = send(charges, lambda d: d ^ 1)
-    other = send(charges, other_neighbour)
+    field = self_field(bundle, tables)
+    late_pair, field = lax.optimization_barrier((pair, field))
+    far = send(late_pair, lambda d: partner(d, True))
     odd = (lax.axis_index(AXES) % 2).reshape(1)
-    field = self_field(bundle, tables)
     totals = jnp.zeros((rhs, rhs), F32)
     field, close_back, totals = pairs_field(pair, close, tables, field, totals, False)
-    field = near_field(twin, charges, other, near_index, near_count, odd, near_weight, field)
     close_back = send_back(close_back, lambda d: partner(d, False))
+    late_charges, field = lax.optimization_barrier((charges, field))
+    twin = send(late_charges, lambda d: d ^ 1)
+    other = send(late_charges, other_neighbour)
     field, far_back, totals = pairs_field(pair, far, tables, field, totals, True)
     far_back = send_back(far_back, lambda d: partner(d, True))
+    field, totals = near_field(
+        twin, charges, other, near_index, near_count, odd, near_weight, field, totals, pair
+    )
     close_back, totals = lax.optimization_barrier((close_back, totals))
-    for step in (core, 1, flip_x):
-        totals = totals + send(totals, lambda d: d ^ step)
-    far_back, totals = lax.optimization_barrier((far_back, totals))
-    back = close_back.astype(F32) + far_back.astype(F32)
-    field = field + back
+    totals = lax.all_to_all(totals, AXES, 0, 0, tiled=True)
+    field = field + close_back.astype(F32) + far_back.astype(F32)
     twin_part = send(field[1].astype(BF16), lambda d: d ^ core)
-    for step in (2, far_z):
-        totals = totals + send(totals, lambda d: d ^ step)
-    return (field[0] + twin_part.astype(F32), totals)
+    return in_vmem(
+        finish_body,
+        (jax.ShapeDtypeStruct(charges.shape, F32), jax.ShapeDtypeStruct((rhs, rhs), F32)),
+    )(field, twin_part, totals)
 
 
 def passed_along(value, axis, steps):

time: 76.4 us -> 66.3 us (0.87)
  starting transfers between devices: 27.3 us -> 21.3 us
  waiting for transfers between devices: 13.7 us -> 10.4 us
  other arithmetic: 1.41 us -> 0.08 us
    ppermute x11 -> x6, waiting for transfers between devices: 13.7 us -> 4.14 us  [send(): return lax.ppermute(value, AXES, [(source_of(d), d) for d in range(count)])]
    ppermute x11 -> x6, starting transfers between devices: 18.4 us -> 12.1 us  [send(): return lax.ppermute(value, AXES, [(source_of(d), d) for d in range(count)])]
    all_to_all x0 -> x1, waiting for transfers between devices: none -> 6.28 us  [paired_blocks(): totals = lax.all_to_all(totals, AXES, 0, 0, tiled=True)]
    all_to_all x0 -> x1, starting transfers between devices: none -> 2.75 us  [paired_blocks(): totals = lax.all_to_all(totals, AXES, 0, 0, tiled=True)]
    ppermute x2, starting transfers between devices: 8.9 us -> 6.49 us  [send_back(): return lax.ppermute(value, AXES, [(d, source_of(d)) for d in range(count)])]
    add x7 -> x1, other arithmetic: 1.38 us -> 0.06 us  [paired_blocks(): field = field + close_back.astype(F32) + far_back.astype(F32)]
    pallas_call x3 -> x4, Pallas kernels: 27 us -> 28.2 us  [the longest x2 22.5 us: pairs_field(): in_vmem(functools.partial(pairs_body, rowblk, width), (jax.ShapeDtypeStru...]
    pallas_call x1, Pallas kernels: 1.02 us -> 0.14 us  [make_bundle(): in_vmem(bundle_body, jax.ShapeDtypeStruct((rhs + FEATURES, panels), BF16)...]
  transfers between devices with their start and end apart: 13 -> 9, of which waited for: 7 -> 4; matrix products, arithmetic and copies ran while one was open for 1% -> 0% of each run, Pallas kernels for 38% -> 45%
where the time goes in v2:
time: 66.3 us; the launch traced here: 66 us
  Pallas kernels  30.5 us (46%)
  starting transfers between devices  21.3 us (32%)
  waiting for transfers between devices  10.4 us (16%)
  local copies, waits for them, and re-layouts  3 us (5%)
  between operations  0.7 us (1%)
    pallas_call x2, Pallas kernels, pairs_field(): in_vmem(functools.partial(pairs_body, rowblk, width), (jax.ShapeDtypeStru...  22.5 us
    ppermute x6, starting transfers between devices, send(): return lax.ppermute(value, AXES, [(source_of(d), d) for d in range(count)])  12.1 us
    ppermute x2, starting transfers between devices, send_back(): return lax.ppermute(value, AXES, [(d, source_of(d)) for d in range(count)])  6.49 us
    all_to_all x1, waiting for transfers between devices, paired_blocks(): totals = lax.all_to_all(totals, AXES, 0, 0, tiled=True)  6.28 us
    pallas_call x1, Pallas kernels, near_field(): pl.pallas_call(near_body, out_shape=(jax.ShapeDtypeStruct(field.shape, F3...  4.91 us
    ppermute x6, waiting for transfers between devices, send(): return lax.ppermute(value, AXES, [(source_of(d), d) for d in range(count)])  4.14 us
    all_to_all x1, starting transfers between devices, paired_blocks(): totals = lax.all_to_all(totals, AXES, 0, 0, tiled=True)  2.75 us
    unnamed x16, local copies, waits for them, and re-layouts  2.28 us
  transfers between devices with their start and end apart: 9, of which 4 were waited for; matrix products, arithmetic and copies ran while one was open for 0% of the time, Pallas kernels for 45%

profile of v2, /device:TPU:0, one launch (start us, length us, event | category | flops | bytes accessed | tf_op | source)
XLA Modules:
  0.0 66.0 jit_solution(5434202542566443198)
XLA Ops:
  0.6 0.7 %reshape.11.conductor_ref = s32[1,1536]{1,0:T(1,128)S(1)} reshape(s32[1536]{0:T(1024)} %param.13) | data formatting | bytes 12288 | tf_op jit(solution)/shard_map/reshape | solution.py:90
  1.3 0.0 copy-start
  1.3 0.9 %copy-done = bf16[32,1536]{1,0:T(8,128)(2,1)S(1)} copy-done((bf16[32,1536]{1,0:T(8,128)(2,1)S(1)}, bf16[32,1536]{1,0:T(8,128)(2,1)}, u32[]{:S(2)}) %copy-start) | copy-done | bytes 98328
  2.2 0.0 copy-start.4
  2.2 0.7 %copy-done.4 = f32[4,1536]{1,0:T(4,128)S(1)} copy-done((f32[4,1536]{1,0:T(4,128)S(1)}, f32[4,1536]{1,0:T(4,128)}, u32[]{:S(2)}) %copy-start.4) | copy-done | bytes 24600
  3.0 0.1 shard_map.95.own_ref
  3.1 0.5 collective-permute-start
  3.6 1.0 %collective-permute-done = bf16[48,1536]{1,0:T(8,128)(2,1)S(1)} collective-permute-done((bf16[48,1536]{1,0:T(8,128)(2,1)S(1)}, bf16[48,1536]{1,0:T(8,128)(2,1)S(1)}, u32[]{:S(2)}, u32[]{:S(2)}) %collective-permute-start) | collective-permute-done | bytes 147488 | tf_op jit(solution)/shard_map/ppermute | solution.py:319
  4.6 0.0 copy-start.2
  4.6 0.0 copy-start.3
  4.7 3.9 %collective-permute-start.1 = (bf16[2,48,1536]{2,1,0:T(8,128)(2,1)S(1)}, bf16[2,48,1536]{2,1,0:T(8,128)(2,1)S(1)}, u32[]{:S(2)}, u32[]{:S(2)}) collective-permute-start(bf16[2,48,1536]{2,1,0:T(8,128)(2,1)S(1)} %pad_maximum_fusion.pair_ref), channel_id=1, source_target_pairs={{1,0},{16,1},{3,2},{18,3},{5,4},{20,5},{7,6},{22,7},{27,8},{10,9},... | collective-permute-start | bytes 884744 | tf_op jit(solution)/shard_map/ppermute | solution.py:319
  8.5 0.0 copy-done.2
  8.5 0.0 copy-done.3
  8.5 2.2 %shard_map.96.field_in = f32[2,32,1536]{2,1,0:T(8,128)S(1)} custom-call(bf16[48,1536]{1,0:T(8,128)(2,1)S(1)} %shard_map.95.own_ref, bf16[32,16]{1,0:T(8,128)(2,1)S(1)} %copy-done.2, bf16[32,16]{1,0:T(8,128)(2,1)S(1)} %copy-done.3), custom_call_target="tpu_custom_call" | custom-call | bytes 1024 | tf_op jit(solution)/shard_map/pallas_call | solution.py:171
  10.7 2.7 %collective-permute-start.4 = (bf16[2,48,1536]{2,1,0:T(8,128)(2,1)S(1)}, bf16[2,48,1536]{2,1,0:T(8,128)(2,1)S(1)}, u32[]{:S(2)}, u32[]{:S(2)}) collective-permute-start(bf16[2,48,1536]{2,1,0:T(8,128)(2,1)S(1)} %pad_maximum_fusion.pair_ref), channel_id=1, source_target_pairs={{5,0},{20,1},{7,2},{22,3},{1,4},{16,5},{3,6},{18,7},{31,8},{14,9},... | collective-permute-start | bytes 884744 | tf_op jit(solution)/shard_map/ppermute | solution.py:319
  13.4 2.1 %collective-permute-done.1.far_ref = bf16[2,48,1536]{2,1,0:T(8,128)(2,1)S(1)} collective-permute-done((bf16[2,48,1536]{2,1,0:T(8,128)(2,1)S(1)}, bf16[2,48,1536]{2,1,0:T(8,128)(2,1)S(1)}, u32[]{:S(2)}, u32[]{:S(2)}) %collective-permute-start.1) | collective-permute-done | bytes 294944 | tf_op jit(solution)/shard_map/ppermute | solution.py:319
  15.5 0.0 copy-start.1
  15.5 11.3 %shard_map.97 = (f32[2,32,1536]{2,1,0:T(8,128)S(1)}, bf16[2,32,1536]{2,1,0:T(8,128)(2,1)S(1)}, f32[32,32]{1,0:T(8,128)S(1)}) custom-call(bf16[2,48,1536]{2,1,0:T(8,128)(2,1)S(1)} %pad_maximum_fusion.pair_ref, bf16[2,48,1536]{2,1,0:T(8,128)(2,1)S(1)} %collective-permute-done.1.far_ref, bf16[32,16]{1,0:T(8,128)(2,1)S(1)} %copy-done.2, ...), custom_call_target="tpu_custom_call" | custom-call | bytes 1024 | tf_op jit(solution)/shard_map/pallas_call | solution.py:234
  26.7 0.0 copy-done.1
  26.7 2.9 %collective-permute-start.2 = (bf16[32,1536]{1,0:T(8,128)(2,1)S(1)}, bf16[32,1536]{1,0:T(8,128)(2,1)S(1)}, u32[]{:S(2)}, u32[]{:S(2)}) collective-permute-start(bf16[32,1536]{1,0:T(8,128)(2,1)S(1)} %copy-done.1), channel_id=1, source_target_pairs={{1,0},{0,1},{3,2},{2,3},{5,4},{4,5},{7,6},{6,7},{9,8},{8,9},{11,10... | collective-permute-start | bytes 294920 | tf_op jit(solution)/shard_map/ppermute | solution.py:319
  29.7 1.8 %collective-permute-start.3 = (bf16[32,1536]{1,0:T(8,128)(2,1)S(1)}, bf16[32,1536]{1,0:T(8,128)(2,1)S(1)}, u32[]{:S(2)}, u32[]{:S(2)}) collective-permute-start(bf16[32,1536]{1,0:T(8,128)(2,1)S(1)} %copy-done.1), channel_id=1, source_target_pairs={{31,0},{2,1},{1,2},{4,3},{3,4},{6,5},{5,6},{8,7},{7,8},{10,9},{9,1... | collective-permute-start | bytes 294920 | tf_op jit(solution)/shard_map/ppermute | solution.py:319
  31.5 3.2 %collective-permute-start.5 = (bf16[2,32,1536]{2,1,0:T(8,128)(2,1)S(1)}, bf16[2,32,1536]{2,1,0:T(8,128)(2,1)S(1)}, u32[]{:S(2)}, u32[]{:S(2)}) collective-permute-start(bf16[2,32,1536]{2,1,0:T(8,128)(2,1)S(1)} %get-tuple-element.25), channel_id=1, source_target_pairs={{0,1},{1,16},{2,3},{3,18},{4,5},{5,20},{6,7},{7,22},{8,27},{9,10},... | collective-permute-start | bytes 589832 | tf_op jit(solution)/shard_map/ppermute | solution.py:324
  34.7 0.0 collective-permute-done.4.far_ref
  34.7 0.0 copy-start.5
  34.7 0.0 copy-start.6
  34.7 11.3 %shard_map.98 = (f32[2,32,1536]{2,1,0:T(8,128)S(1)}, bf16[2,32,1536]{2,1,0:T(8,128)(2,1)S(1)}, f32[32,32]{1,0:T(8,128)S(1)}) custom-call(bf16[2,48,1536]{2,1,0:T(8,128)(2,1)S(1)} %pad_maximum_fusion.pair_ref, bf16[2,48,1536]{2,1,0:T(8,128)(2,1)S(1)} %collective-permute-done.4.far_ref, bf16[32,16]{1,0:T(8,128)(2,1)S(1)} %copy-done.2, ...), custom_call_target="tpu_custom_call" | custom-call | flops 7549747200 | bytes 1024 | tf_op jit(solution)/shard_map/pallas_call | solution.py:234
  46.0 3.3 %collective-permute-start.6 = (bf16[2,32,1536]{2,1,0:T(8,128)(2,1)S(1)}, bf16[2,32,1536]{2,1,0:T(8,128)(2,1)S(1)}, u32[]{:S(2)}, u32[]{:S(2)}) collective-permute-start(bf16[2,32,1536]{2,1,0:T(8,128)(2,1)S(1)} %get-tuple-element.28), channel_id=1, source_target_pairs={{0,5},{1,20},{2,7},{3,22},{4,1},{5,16},{6,3},{7,18},{8,31},{9,14},... | collective-permute-start | bytes 589832 | tf_op jit(solution)/shard_map/ppermute | solution.py:324
  49.2 0.0 collective-permute-done.2.twin_ref
  49.2 0.0 collective-permute-done.3.other_ref
  49.2 0.0 copy-start.7
  49.2 0.0 copy-done.5
  49.2 0.0 copy-done.6
  49.3 0.6 copy-done.7
  49.9 4.9 %shard_map.99 = (f32[2,32,1536]{2,1,0:T(8,128)S(1)}, f32[32,8,128]{2,1,0:T(8,128)}) custom-call(bf16[32,1536]{1,0:T(8,128)(2,1)S(1)} %collective-permute-done.2.twin_ref, bf16[32,1536]{1,0:T(8,128)(2,1)S(1)} %copy-done.1, bf16[32,1536]{1,0:T(8,128)(2,1)S(1)} %collective-permute-done.3.other_ref, s32[12,128]{1,0:T(8,128)S(1)} %copy-done.6, s32[12]{0:T(128)S(1)} %copy-done.7, ...), custom_call_target="tpu_custom_call" | custom-call | flops 4000000000 | bytes 1024 | tf_op jit(solution)/shard_map/pallas_call | solution.py:295
  54.8 0.0 collective-permute-done.5
  54.8 2.8 %all-to-all-start = ((f32[32,8,128]{2,1,0:T(8,128)}), f32[32,8,128]{2,1,0:T(8,128)S(1)}, u32[]{:S(2)}, u32[]{:S(2)}) async-start(f32[32,8,128]{2,1,0:T(8,128)} %get-tuple-element.29), calls=%async_computation | async-start | bytes 262144 | tf_op jit(solution)/shard_map/all_to_all | solution.py:362
  57.6 0.0 collective-permute-done.6
  57.6 0.1 convert_add_fusion.field_ref
  57.7 0.3 collective-permute-start.7
  58.0 1.1 %collective-permute-done.7.part_ref = bf16[32,1536]{1,0:T(8,128)(2,1)S(1)} collective-permute-done((bf16[32,1536]{1,0:T(8,128)(2,1)S(1)}, bf16[32,1536]{1,0:T(8,128)(2,1)S(1)}, u32[]{:S(2)}, u32[]{:S(2)}) %collective-permute-start.7) | collective-permute-done | bytes 98336 | tf_op jit(solution)/shard_map/ppermute | solution.py:319
  59.0 6.3 %all-to-all-done.totals_ref = f32[32,8,128]{2,1,0:T(8,128)S(1)} async-done(((f32[32,8,128]{2,1,0:T(8,128)}), f32[32,8,128]{2,1,0:T(8,128)S(1)}, u32[]{:S(2)}, u32[]{:S(2)}) %all-to-all-start) | async-done | bytes 131104 | tf_op jit(solution)/shard_map/all_to_all | solution.py:362
  65.3 0.7 %shard_map.100 = (f32[32,1536]{1,0:T(8,128)}, f32[32,32]{1,0:T(8,128)}) custom-call(f32[2,32,1536]{2,1,0:T(8,128)S(1)} %convert_add_fusion.field_ref, bf16[32,1536]{1,0:T(8,128)(2,1)S(1)} %collective-permute-done.7.part_ref, f32[32,8,128]{2,1,0:T(8,128)S(1)} %all-to-all-done.totals_ref), custom_call_target="tpu_custom_call" | custom-call | bytes 1024 | tf_op jit(solution)/shard_map/pallas_call | solution.py:365
  (3 shorter events, 0.0 us)
Async XLA Ops:
  1.3 0.9 %copy-start = (bf16[32,1536]{1,0:T(8,128)(2,1)S(1)}, bf16[32,1536]{1,0:T(8,128)(2,1)}, u32[]{:S(2)}) copy-start(bf16[32,1536]{1,0:T(8,128)(2,1)} %own_ref.1) | copy-start | bytes 294916
  2.2 0.7 %copy-start.4 = (f32[4,1536]{1,0:T(4,128)S(1)}, f32[4,1536]{1,0:T(4,128)}, u32[]{:S(2)}) copy-start(f32[4,1536]{1,0:T(4,128)} %geo_ref.1) | copy-start | bytes 73732
  3.1 1.5 %collective-permute-start = (bf16[48,1536]{1,0:T(8,128)(2,1)S(1)}, bf16[48,1536]{1,0:T(8,128)(2,1)S(1)}, u32[]{:S(2)}, u32[]{:S(2)}) collective-permute-start(bf16[48,1536]{1,0:T(8,128)(2,1)S(1)} %shard_map.95.own_ref), channel_id=1, source_target_pairs={{8,0},{9,1},{10,2},{11,3},{12,4},{13,5},{14,6},{15,7},{0,8},{1,9},... | collective-permute-start | bytes 442376 | tf_op jit(solution)/shard_map/ppermute | solution.py:319
  4.6 3.9 %copy-start.2 = (bf16[32,16]{1,0:T(8,128)(2,1)S(1)}, bf16[32,16]{1,0:T(8,128)(2,1)}, u32[]{:S(2)}) copy-start(bf16[32,16]{1,0:T(8,128)(2,1)} %constant.29.clone.ltab_ref) | copy-start | bytes 3076
  4.6 3.9 %copy-start.3 = (bf16[32,16]{1,0:T(8,128)(2,1)S(1)}, bf16[32,16]{1,0:T(8,128)(2,1)}, u32[]{:S(2)}) copy-start(bf16[32,16]{1,0:T(8,128)(2,1)} %constant.30.clone.rtab_ref) | copy-start | bytes 3076
  4.7 10.8 %collective-permute-start.1 = (bf16[2,48,1536]{2,1,0:T(8,128)(2,1)S(1)}, bf16[2,48,1536]{2,1,0:T(8,128)(2,1)S(1)}, u32[]{:S(2)}, u32[]{:S(2)}) collective-permute-start(bf16[2,48,1536]{2,1,0:T(8,128)(2,1)S(1)} %pad_maximum_fusion.pair_ref), channel_id=1, source_target_pairs={{1,0},{16,1},{3,2},{18,3},{5,4},{20,5},{7,6},{22,7},{27,8},{10,9},... | collective-permute-start | bytes 884744 | tf_op jit(solution)/shard_map/ppermute | solution.py:319
  10.7 24.0 %collective-permute-start.4 = (bf16[2,48,1536]{2,1,0:T(8,128)(2,1)S(1)}, bf16[2,48,1536]{2,1,0:T(8,128)(2,1)S(1)}, u32[]{:S(2)}, u32[]{:S(2)}) collective-permute-start(bf16[2,48,1536]{2,1,0:T(8,128)(2,1)S(1)} %pad_maximum_fusion.pair_ref), channel_id=1, source_target_pairs={{5,0},{20,1},{7,2},{22,3},{1,4},{16,5},{3,6},{18,7},{31,8},{14,9},... | collective-permute-start | bytes 884744 | tf_op jit(solution)/shard_map/ppermute | solution.py:319
  15.5 11.3 %copy-start.1 = (bf16[32,1536]{1,0:T(8,128)(2,1)S(1)}, bf16[32,1536]{1,0:T(8,128)(2,1)}, u32[]{:S(2)}) copy-start(bf16[32,1536]{1,0:T(8,128)(2,1)} %own_ref.1) | copy-start | bytes 294916
  26.7 22.5 %collective-permute-start.2 = (bf16[32,1536]{1,0:T(8,128)(2,1)S(1)}, bf16[32,1536]{1,0:T(8,128)(2,1)S(1)}, u32[]{:S(2)}, u32[]{:S(2)}) collective-permute-start(bf16[32,1536]{1,0:T(8,128)(2,1)S(1)} %copy-done.1), channel_id=1, source_target_pairs={{1,0},{0,1},{3,2},{2,3},{5,4},{4,5},{7,6},{6,7},{9,8},{8,9},{11,10... | collective-permute-start | bytes 294920 | tf_op jit(solution)/shard_map/ppermute | solution.py:319
  29.7 19.6 %collective-permute-start.3 = (bf16[32,1536]{1,0:T(8,128)(2,1)S(1)}, bf16[32,1536]{1,0:T(8,128)(2,1)S(1)}, u32[]{:S(2)}, u32[]{:S(2)}) collective-permute-start(bf16[32,1536]{1,0:T(8,128)(2,1)S(1)} %copy-done.1), channel_id=1, source_target_pairs={{31,0},{2,1},{1,2},{4,3},{3,4},{6,5},{5,6},{8,7},{7,8},{10,9},{9,1... | collective-permute-start | bytes 294920 | tf_op jit(solution)/shard_map/ppermute | solution.py:319
  31.5 23.3 %collective-permute-start.5 = (bf16[2,32,1536]{2,1,0:T(8,128)(2,1)S(1)}, bf16[2,32,1536]{2,1,0:T(8,128)(2,1)S(1)}, u32[]{:S(2)}, u32[]{:S(2)}) collective-permute-start(bf16[2,32,1536]{2,1,0:T(8,128)(2,1)S(1)} %get-tuple-element.25), channel_id=1, source_target_pairs={{0,1},{1,16},{2,3},{3,18},{4,5},{5,20},{6,7},{7,22},{8,27},{9,10},... | collective-permute-start | bytes 589832 | tf_op jit(solution)/shard_map/ppermute | solution.py:324
  34.7 14.6 %copy-start.5 = (bf16[12,128,128]{2,1,0:T(8,128)(2,1)S(1)}, bf16[12,128,128]{2,1,0:T(8,128)(2,1)}, u32[]{:S(2)}) copy-start(bf16[12,128,128]{2,1,0:T(8,128)(2,1)} %weight_ref.1) | copy-start | bytes 1179652
  34.7 14.6 %copy-start.6 = (s32[12,128]{1,0:T(8,128)S(1)}, s32[12,128]{1,0:T(8,128)}, u32[]{:S(2)}) copy-start(s32[12,128]{1,0:T(8,128)} %index_ref.1) | copy-start | bytes 18436
  46.0 11.6 %collective-permute-start.6 = (bf16[2,32,1536]{2,1,0:T(8,128)(2,1)S(1)}, bf16[2,32,1536]{2,1,0:T(8,128)(2,1)S(1)}, u32[]{:S(2)}, u32[]{:S(2)}) collective-permute-start(bf16[2,32,1536]{2,1,0:T(8,128)(2,1)S(1)} %get-tuple-element.28), channel_id=1, source_target_pairs={{0,5},{1,20},{2,7},{3,22},{4,1},{5,16},{6,3},{7,18},{8,31},{9,14},... | collective-permute-start | bytes 589832 | tf_op jit(solution)/shard_map/ppermute | solution.py:324
  49.2 0.7 copy-start.7
  54.8 10.5 %all-to-all-start = ((f32[32,8,128]{2,1,0:T(8,128)}), f32[32,8,128]{2,1,0:T(8,128)S(1)}, u32[]{:S(2)}, u32[]{:S(2)}) async-start(f32[32,8,128]{2,1,0:T(8,128)} %get-tuple-element.29), calls=%async_computation | async-start | bytes 262144 | tf_op jit(solution)/shard_map/all_to_all | solution.py:362
  57.7 1.4 %collective-permute-start.7 = (bf16[32,1536]{1,0:T(8,128)(2,1)S(1)}, bf16[32,1536]{1,0:T(8,128)(2,1)S(1)}, u32[]{:S(2)}, u32[]{:S(2)}) collective-permute-start(bf16[32,1536]{1,0:T(8,128)(2,1)S(1)} %fusion), channel_id=1, source_target_pairs={{8,0},{9,1},{10,2},{11,3},{12,4},{13,5},{14,6},{15,7},{0,8},{1,9},... | collective-permute-start | bytes 294920 | tf_op jit(solution)/shard_map/ppermute | solution.py:319

commit v3 on v2

--- a/solution.py
+++ b/solution.py
@@ -15,6 +15,7 @@
 
 X, NORM, AREA, MEMBER, ONE = 0, 6, 9, 11, 12
 FEATURES = 16
+LANES = 128
 DEPTH = 32
 VMEM_LIMIT = 48 * 2**20
 
@@ -76,7 +77,7 @@
     high = rounded(area)
     rows_ref[AREA : AREA + 1, :] = high
     rows_ref[AREA + 1 : AREA + 2, :] = area - high
-    rows_ref[MEMBER : MEMBER + 1, :] = conductor_ref[...].astype(F32)
+    rows_ref[MEMBER : MEMBER + 1, :] = conductor_ref[...].astype(F32).reshape(1, -1)
     rows_ref[ONE : ONE + 1, :] = jnp.ones_like(area)
     out_ref[rhs:, :] = rows_ref[...].astype(BF16)
 
@@ -87,7 +88,7 @@
         bundle_body,
         jax.ShapeDtypeStruct((rhs + FEATURES, panels), BF16),
         [pltpu.VMEM((FEATURES, panels), F32)],
-    )(geometry, charges, conductor.reshape(1, panels))
+    )(geometry, charges, conductor)
 
 
 def left_side(features, table):
@@ -142,8 +143,19 @@
     )
 
 
-def self_body(rowblk, width, own_ref, ltab_ref, rtab_ref, out_ref, left_ref, right_ref, *slots):
+def self_body(
+    rowblk, width, own_ref, ltab_ref, rtab_ref, index_ref, count_ref, odd_ref, out_ref, live_ref,
+    left_ref, right_ref, *slots
+):
     _, rhs, panels = out_ref.shape
+    groups, near = index_ref.shape
+    turn = jnp.where(odd_ref[0] == 1, 0, 2 * panels)
+    slot = lax.broadcasted_iota(jnp.int32, (1, near), 1)
+    for group in range(groups):
+        index = index_ref[group : group + 1, :]
+        moved = jnp.where(index < panels, index + turn, index)
+        index = jnp.where(index >= 2 * panels, index - turn, moved)
+        live_ref[group : group + 1, :] = jnp.where(slot < count_ref[group], index, -LANES)
     features = own_ref[rhs:, :]
     left_ref[...] = left_side(features, ltab_ref[...])
     right_ref[...] = right_side(features, rtab_ref[...])
@@ -164,21 +176,29 @@
     two_stage(panels // rowblk, make, use, slots, width)
 
 
-def self_field(own, tables):
+def self_field(own, tables, index, count, odd):
     rows, panels = own.shape
     rhs = rows - FEATURES
     rowblk, width = blocking(panels)
-    return in_vmem(
+    vmem = pl.BlockSpec(memory_space=pltpu.VMEM)
+    smem = pl.BlockSpec(memory_space=pltpu.SMEM)
+    return pl.pallas_call(
         functools.partial(self_body, rowblk, width),
-        jax.ShapeDtypeStruct((2, rhs, panels), F32),
-        [
+        out_shape=(
+            jax.ShapeDtypeStruct((2, rhs, panels), F32),
+            jax.ShapeDtypeStruct(index.shape, index.dtype),
+        ),
+        in_specs=[vmem] * 4 + [smem] * 2,
+        out_specs=(vmem, vmem),
+        scratch_shapes=[
             pltpu.VMEM((panels, DEPTH), BF16),
             pltpu.VMEM((DEPTH, panels), BF16),
             pltpu.VMEM((rowblk, panels), BF16),
             pltpu.VMEM((rowblk, panels), BF16),
         ],
-        flops=0,
-    )(own, *tables)
+        compiler_params=pltpu.CompilerParams(vmem_limit_bytes=VMEM_LIMIT),
+        cost_estimate=pl.CostEstimate(flops=0, bytes_accessed=2**10, transcendentals=0),
+    )(own, *tables, index, count, odd)
 
 
 def pairs_body(
@@ -250,36 +270,38 @@
 
 
 def near_body(
-    twin_ref, own_ref, other_ref, index_ref, count_ref, odd_ref, weight_ref, field_in, totals_in,
+    together, twin_ref, own_ref, other_ref, index_ref, weight_ref, field_in, totals_in,
     pair_ref, field_ref, totals_ref, ext_ref
 ):
     rhs, panels = own_ref.shape
     groups, near = index_ref.shape
+    pieces = panels // LANES
     for side, ref in enumerate((twin_ref, own_ref, other_ref)):
-        ext_ref[:, side * panels : (side + 1) * panels] = ref[...].astype(F32)
+        for piece in range(pieces):
+            start = rhs * (side * pieces + piece)
+            ext_ref[start : start + rhs, :] = ref[:, piece * LANES : (piece + 1) * LANES]
     field_ref[...] = field_in[...]
-    turn = jnp.where(odd_ref[0] == 1, 0, 2 * panels)
-
-    @pl.loop(0, groups)
-    def _(group):
-        index = index_ref[pl.ds(group, 1), :]
-        moved = jnp.where(index < panels, index + turn, index)
-        index = jnp.where(index >= 2 * panels, index - turn, moved)
-        slot = lax.broadcasted_iota(jnp.int32, (1, near), 1)
-        live = slot < count_ref[group]
-        lane = jnp.broadcast_to(index % near, (rhs, near))
-        piece = jnp.broadcast_to(jnp.where(live, index // near, -1), (rhs, near))
-        taken = jnp.zeros((rhs, near), F32)
-        for part in range(3 * panels // near):
-            found = jnp.take_along_axis(
-                ext_ref[:, part * near : (part + 1) * near], lane, axis=1
+
+    @pl.loop(0, groups // together)
+    def _(batch):
+        rows = [batch * together + member for member in range(together)]
+        index = jnp.concatenate([index_ref[pl.ds(group, 1), :] for group in rows], axis=1)
+        lane = index & (LANES - 1)
+        place = jnp.broadcast_to(index >> (LANES.bit_length() - 1), (rhs, together * near))
+        names = lax.broadcasted_iota(jnp.int32, (LANES, together * near), 0)
+        pick = jnp.where(names == lane, 1.0, 0.0).astype(BF16)
+        taken = jnp.zeros((rhs, together * near), F32)
+        found = jnp.dot(ext_ref[...], pick, preferred_element_type=F32)
+        for piece in range(3 * pieces):
+            part = found[piece * rhs : (piece + 1) * rhs, :]
+            taken = jnp.where(place == piece, part, taken)
+        taken = taken.astype(BF16)
+        width = weight_ref.shape[1]
+        for member, group in enumerate(rows):
+            field_ref[0, :, pl.ds(pl.multiple_of(group * width, width), width)] += lax.dot_general(
+                taken[:, member * near : (member + 1) * near], weight_ref[group],
+                (((1,), (1,)), ((), ())), preferred_element_type=F32,
             )
-            taken = jnp.where(piece == part, found, taken)
-        width = weight_ref.shape[1]
-        field_ref[0, :, pl.ds(pl.multiple_of(group * width, width), width)] += lax.dot_general(
-            taken.astype(BF16), weight_ref[group], (((1,), (1,)), ((), ())),
-            preferred_element_type=F32,
-        )
 
     totals = totals_in[...]
     for block in range(field_ref.shape[0]):
@@ -289,21 +311,22 @@
     totals_ref[...] = jnp.broadcast_to(flat[None], totals_ref.shape)
 
 
-def near_field(twin, own, other, index, count, odd, weight, field, totals, pair):
+def near_field(twin, own, other, index, weight, field, totals, pair):
     rhs, panels = own.shape
     vmem = pl.BlockSpec(memory_space=pltpu.VMEM)
+    together = next(n for n in (4, 2, 1) if index.shape[0] % n == 0)
     return pl.pallas_call(
-        near_body,
+        functools.partial(near_body, together),
         out_shape=(
             jax.ShapeDtypeStruct(field.shape, F32),
             jax.ShapeDtypeStruct((lax.axis_size(AXES), rhs * rhs // 128, 128), F32),
         ),
-        in_specs=[vmem] * 4 + [pl.BlockSpec(memory_space=pltpu.SMEM)] * 2 + [vmem] * 4,
+        in_specs=[vmem] * 8,
         out_specs=(vmem, vmem),
-        scratch_shapes=[pltpu.VMEM((rhs, 3 * panels), F32)],
+        scratch_shapes=[pltpu.VMEM((3 * panels // LANES * rhs, LANES), BF16)],
         compiler_params=pltpu.CompilerParams(vmem_limit_bytes=VMEM_LIMIT),
         cost_estimate=pl.CostEstimate(flops=4 * 10**9, bytes_accessed=2**10, transcendentals=0),
-    )(twin, own, other, index, count, odd, weight, field, totals, pair)
+    )(twin, own, other, index, weight, field, totals, pair)
 
 
 def finish_body(field_ref, part_ref, totals_ref, potential_out, totals_out):
@@ -343,10 +366,10 @@
     sibling = send(bundle, lambda d: d ^ core)
     pair = jnp.stack([bundle, sibling])
     close = send(pair, lambda d: partner(d, False))
-    field = self_field(bundle, tables)
+    odd = (lax.axis_index(AXES) % 2).reshape(1)
+    field, live = self_field(bundle, tables, near_index, near_count, odd)
     late_pair, field = lax.optimization_barrier((pair, field))
     far = send(late_pair, lambda d: partner(d, True))
-    odd = (lax.axis_index(AXES) % 2).reshape(1)
     totals = jnp.zeros((rhs, rhs), F32)
     field, close_back, totals = pairs_field(pair, close, tables, field, totals, False)
     close_back = send_back(close_back, lambda d: partner(d, False))
@@ -356,7 +379,7 @@
     field, far_back, totals = pairs_field(pair, far, tables, field, totals, True)
     far_back = send_back(far_back, lambda d: partner(d, True))
     field, totals = near_field(
-        twin, charges, other, near_index, near_count, odd, near_weight, field, totals, pair
+        twin, charges, other, live, near_weight, field, totals, pair
     )
     close_back, totals = lax.optimization_barrier((close_back, totals))
     totals = lax.all_to_all(totals, AXES, 0, 0, tiled=True)

time: 66.3 us -> 62.3 us (0.940)
  starting transfers between devices: 21.3 us -> 19.6 us
  Pallas kernels: 30.5 us -> 29 us
  waiting for transfers between devices: 10.4 us -> 9.59 us
    ppermute x2, waiting for transfers between devices: 0.01 us -> 2.83 us  [send_back(): return lax.ppermute(value, AXES, [(d, source_of(d)) for d in range(count)])]
    all_to_all x1, waiting for transfers between devices: 6.28 us -> 3.46 us  [paired_blocks(): totals = lax.all_to_all(totals, AXES, 0, 0, tiled=True)]
    pallas_call x2, Pallas kernels: 7.1 us -> 5.64 us  [the longest x1 2.91 us: near_field(): pl.pallas_call(functools.partial(near_body, together), out_shape=(jax.Sha...]
    ppermute x2, starting transfers between devices: 6.49 us -> 5.3 us  [send_back(): return lax.ppermute(value, AXES, [(d, source_of(d)) for d in range(count)])]
    ppermute x6, waiting for transfers between devices: 4.14 us -> 3.29 us  [send(): return lax.ppermute(value, AXES, [(source_of(d), d) for d in range(count)])]
    reshape x1 -> x0, local copies, waits for them, and re-layouts: 0.7 us -> none  [make_bundle(): conductor.reshape(1, panels)]
    unnamed x16 -> x18, local copies, waits for them, and re-layouts: 2.28 us -> 2.98 us
  transfers between devices with their start and end apart: 9 -> 9, of which waited for: 4 -> 5; matrix products, arithmetic and copies ran while one was open for 0% -> 0% of each run, Pallas kernels for 45% -> 45%
where the time goes in v3:
time: 62.3 us; the launch traced here: 62 us
  Pallas kernels  29 us (47%)
  starting transfers between devices  19.6 us (31%)
  waiting for transfers between devices  9.59 us (15%)
  local copies, waits for them, and re-layouts  3 us (5%)
  between operations  0.69 us (1%)
    pallas_call x2, Pallas kernels, pairs_field(): in_vmem(functools.partial(pairs_body, rowblk, width), (jax.ShapeDtypeStru...  22.5 us
    ppermute x6, starting transfers between devices, send(): return lax.ppermute(value, AXES, [(source_of(d), d) for d in range(count)])  11.7 us
    ppermute x2, starting transfers between devices, send_back(): return lax.ppermute(value, AXES, [(d, source_of(d)) for d in range(count)])  5.3 us
    all_to_all x1, waiting for transfers between devices, paired_blocks(): totals = lax.all_to_all(totals, AXES, 0, 0, tiled=True)  3.46 us
    ppermute x6, waiting for transfers between devices, send(): return lax.ppermute(value, AXES, [(source_of(d), d) for d in range(count)])  3.29 us
    unnamed x18, local copies, waits for them, and re-layouts  2.98 us
    pallas_call x1, Pallas kernels, near_field(): pl.pallas_call(functools.partial(near_body, together), out_shape=(jax.Sha...  2.91 us
    ppermute x2, waiting for transfers between devices, send_back(): return lax.ppermute(value, AXES, [(d, source_of(d)) for d in range(count)])  2.83 us
  transfers between devices with their start and end apart: 9, of which 5 were waited for; matrix products, arithmetic and copies ran while one was open for 0% of the time, Pallas kernels for 45%

profile of v3, /device:TPU:0, one launch (start us, length us, event | category | flops | bytes accessed | tf_op | source)
XLA Modules:
  0.0 62.0 jit_solution(4632843727691864099)
XLA Ops:
  0.6 0.0 copy-start
  0.6 0.9 %copy-done = bf16[32,1536]{1,0:T(8,128)(2,1)S(1)} copy-done((bf16[32,1536]{1,0:T(8,128)(2,1)S(1)}, bf16[32,1536]{1,0:T(8,128)(2,1)}, u32[]{:S(2)}) %copy-start) | copy-done | bytes 98328
  1.5 0.0 copy-start.4
  1.5 0.7 %copy-done.4 = f32[4,1536]{1,0:T(4,128)S(1)} copy-done((f32[4,1536]{1,0:T(4,128)S(1)}, f32[4,1536]{1,0:T(4,128)}, u32[]{:S(2)}) %copy-start.4) | copy-done | bytes 24600
  2.3 0.0 copy-start.5
  2.3 0.7 %copy-done.5 = s32[1536]{0:T(1024)S(1)} copy-done((s32[1536]{0:T(1024)S(1)}, s32[1536]{0:T(1024)}, u32[]{:S(2)}) %copy-start.5) | copy-done | bytes 6168
  3.0 0.1 shard_map.95.own_ref
  3.1 0.5 collective-permute-start
  3.6 1.0 %collective-permute-done = bf16[48,1536]{1,0:T(8,128)(2,1)S(1)} collective-permute-done((bf16[48,1536]{1,0:T(8,128)(2,1)S(1)}, bf16[48,1536]{1,0:T(8,128)(2,1)S(1)}, u32[]{:S(2)}, u32[]{:S(2)}) %collective-permute-start) | collective-permute-done | bytes 147488 | tf_op jit(solution)/shard_map/ppermute | solution.py:342
  4.6 0.0 copy-start.2
  4.6 0.0 copy-start.3
  4.6 0.0 copy-start.6
  4.7 3.9 %collective-permute-start.1 = (bf16[2,48,1536]{2,1,0:T(8,128)(2,1)S(1)}, bf16[2,48,1536]{2,1,0:T(8,128)(2,1)S(1)}, u32[]{:S(2)}, u32[]{:S(2)}) collective-permute-start(bf16[2,48,1536]{2,1,0:T(8,128)(2,1)S(1)} %pad_maximum_fusion.pair_ref), channel_id=1, source_target_pairs={{1,0},{16,1},{3,2},{18,3},{5,4},{20,5},{7,6},{22,7},{27,8},{10,9},... | collective-permute-start | bytes 884744 | tf_op jit(solution)/shard_map/ppermute | solution.py:342
  8.5 0.0 copy-start.7
  8.5 0.0 copy-done.2
  8.5 0.0 copy-done.3
  8.5 0.0 copy-done.6
  8.5 0.6 %copy-done.7 = s32[12]{0:T(128)S(1)} copy-done((s32[12]{0:T(128)S(1)}, s32[12]{0:T(128)}, u32[]{:S(2)}) %copy-start.7) | copy-done | bytes 72
  9.2 2.7 %shard_map.96 = (f32[2,32,1536]{2,1,0:T(8,128)S(1)}, s32[12,128]{1,0:T(8,128)S(1)}) custom-call(bf16[48,1536]{1,0:T(8,128)(2,1)S(1)} %shard_map.95.own_ref, bf16[32,16]{1,0:T(8,128)(2,1)S(1)} %copy-done.2, bf16[32,16]{1,0:T(8,128)(2,1)S(1)} %copy-done.3, s32[12,128]{1,0:T(8,128)S(1)} %copy-done.6, s32[12]{0:T(128)S(1)} %copy-done.7, s32[1]{0:T(128)} %bitcast.2.odd_ref), custom_call_target="tpu_custom_call" | custom-call | bytes 1024 | tf_op jit(solution)/shard_map/pallas_call | solution.py:185
  11.9 2.6 %collective-permute-start.4 = (bf16[2,48,1536]{2,1,0:T(8,128)(2,1)S(1)}, bf16[2,48,1536]{2,1,0:T(8,128)(2,1)S(1)}, u32[]{:S(2)}, u32[]{:S(2)}) collective-permute-start(bf16[2,48,1536]{2,1,0:T(8,128)(2,1)S(1)} %pad_maximum_fusion.pair_ref), channel_id=1, source_target_pairs={{5,0},{20,1},{7,2},{22,3},{1,4},{16,5},{3,6},{18,7},{31,8},{14,9},... | collective-permute-start | bytes 884744 | tf_op jit(solution)/shard_map/ppermute | solution.py:342
  14.5 1.0 %collective-permute-done.1.far_ref = bf16[2,48,1536]{2,1,0:T(8,128)(2,1)S(1)} collective-permute-done((bf16[2,48,1536]{2,1,0:T(8,128)(2,1)S(1)}, bf16[2,48,1536]{2,1,0:T(8,128)(2,1)S(1)}, u32[]{:S(2)}, u32[]{:S(2)}) %collective-permute-start.1) | collective-permute-done | bytes 294944 | tf_op jit(solution)/shard_map/ppermute | solution.py:342
  15.5 0.0 copy-start.1
  15.5 11.3 %shard_map.97 = (f32[2,32,1536]{2,1,0:T(8,128)S(1)}, bf16[2,32,1536]{2,1,0:T(8,128)(2,1)S(1)}, f32[32,32]{1,0:T(8,128)S(1)}) custom-call(bf16[2,48,1536]{2,1,0:T(8,128)(2,1)S(1)} %pad_maximum_fusion.pair_ref, bf16[2,48,1536]{2,1,0:T(8,128)(2,1)S(1)} %collective-permute-done.1.far_ref, bf16[32,16]{1,0:T(8,128)(2,1)S(1)} %copy-done.2, ...), custom_call_target="tpu_custom_call" | custom-call | bytes 1024 | tf_op jit(solution)/shard_map/pallas_call | solution.py:254
  26.7 0.0 copy-done.1
  26.7 2.1 %collective-permute-start.2 = (bf16[32,1536]{1,0:T(8,128)(2,1)S(1)}, bf16[32,1536]{1,0:T(8,128)(2,1)S(1)}, u32[]{:S(2)}, u32[]{:S(2)}) collective-permute-start(bf16[32,1536]{1,0:T(8,128)(2,1)S(1)} %copy-done.1), channel_id=1, source_target_pairs={{1,0},{0,1},{3,2},{2,3},{5,4},{4,5},{7,6},{6,7},{9,8},{8,9},{11,10... | collective-permute-start | bytes 294920 | tf_op jit(solution)/shard_map/ppermute | solution.py:342
  28.8 2.6 %collective-permute-start.3 = (bf16[32,1536]{1,0:T(8,128)(2,1)S(1)}, bf16[32,1536]{1,0:T(8,128)(2,1)S(1)}, u32[]{:S(2)}, u32[]{:S(2)}) collective-permute-start(bf16[32,1536]{1,0:T(8,128)(2,1)S(1)} %copy-done.1), channel_id=1, source_target_pairs={{31,0},{2,1},{1,2},{4,3},{3,4},{6,5},{5,6},{8,7},{7,8},{10,9},{9,1... | collective-permute-start | bytes 294920 | tf_op jit(solution)/shard_map/ppermute | solution.py:342
  31.5 1.4 %collective-permute-start.5 = (bf16[2,32,1536]{2,1,0:T(8,128)(2,1)S(1)}, bf16[2,32,1536]{2,1,0:T(8,128)(2,1)S(1)}, u32[]{:S(2)}, u32[]{:S(2)}) collective-permute-start(bf16[2,32,1536]{2,1,0:T(8,128)(2,1)S(1)} %get-tuple-element.29), channel_id=1, source_target_pairs={{0,1},{1,16},{2,3},{3,18},{4,5},{5,20},{6,7},{7,22},{8,27},{9,10},... | collective-permute-start | bytes 589832 | tf_op jit(solution)/shard_map/ppermute | solution.py:347
  32.8 0.0 collective-permute-done.4.far_ref
  32.8 0.0 copy-start.8
  32.8 11.3 %shard_map.98 = (f32[2,32,1536]{2,1,0:T(8,128)S(1)}, bf16[2,32,1536]{2,1,0:T(8,128)(2,1)S(1)}, f32[32,32]{1,0:T(8,128)S(1)}) custom-call(bf16[2,48,1536]{2,1,0:T(8,128)(2,1)S(1)} %pad_maximum_fusion.pair_ref, bf16[2,48,1536]{2,1,0:T(8,128)(2,1)S(1)} %collective-permute-done.4.far_ref, bf16[32,16]{1,0:T(8,128)(2,1)S(1)} %copy-done.2, ...), custom_call_target="tpu_custom_call" | custom-call | flops 7549747200 | bytes 1024 | tf_op jit(solution)/shard_map/pallas_call | solution.py:254
  44.1 3.9 %collective-permute-start.6 = (bf16[2,32,1536]{2,1,0:T(8,128)(2,1)S(1)}, bf16[2,32,1536]{2,1,0:T(8,128)(2,1)S(1)}, u32[]{:S(2)}, u32[]{:S(2)}) collective-permute-start(bf16[2,32,1536]{2,1,0:T(8,128)(2,1)S(1)} %get-tuple-element.32), channel_id=1, source_target_pairs={{0,5},{1,20},{2,7},{3,22},{4,1},{5,16},{6,3},{7,18},{8,31},{9,14},... | collective-permute-start | bytes 589832 | tf_op jit(solution)/shard_map/ppermute | solution.py:347
  48.0 0.0 collective-permute-done.2.twin_ref
  48.0 0.0 collective-permute-done.3.other_ref
  48.0 0.0 copy-done.8
  48.0 2.9 %shard_map.99 = (f32[2,32,1536]{2,1,0:T(8,128)S(1)}, f32[32,8,128]{2,1,0:T(8,128)}) custom-call(bf16[32,1536]{1,0:T(8,128)(2,1)S(1)} %collective-permute-done.2.twin_ref, bf16[32,1536]{1,0:T(8,128)(2,1)S(1)} %copy-done.1, bf16[32,1536]{1,0:T(8,128)(2,1)S(1)} %collective-permute-done.3.other_ref, s32[12,128]{1,0:T(8,128)S(1)} %get-tuple-element.22.index_ref, ...), custom_call_target="tpu_custom_call" | custom-call | flops 4000000000 | bytes 1024 | tf_op jit(solution)/shard_map/pallas_call | solution.py:318
  51.0 0.0 collective-permute-done.5
  51.0 2.6 %all-to-all-start = ((f32[32,8,128]{2,1,0:T(8,128)}), f32[32,8,128]{2,1,0:T(8,128)S(1)}, u32[]{:S(2)}, u32[]{:S(2)}) async-start(f32[32,8,128]{2,1,0:T(8,128)} %get-tuple-element.33), calls=%async_computation | async-start | bytes 262144 | tf_op jit(solution)/shard_map/all_to_all | solution.py:385
  53.5 2.8 %collective-permute-done.6 = bf16[2,32,1536]{2,1,0:T(8,128)(2,1)S(1)} collective-permute-done((bf16[2,32,1536]{2,1,0:T(8,128)(2,1)S(1)}, bf16[2,32,1536]{2,1,0:T(8,128)(2,1)S(1)}, u32[]{:S(2)}, u32[]{:S(2)}) %collective-permute-start.6) | collective-permute-done | bytes 196640 | tf_op jit(solution)/shard_map/ppermute | solution.py:347
  56.4 0.1 convert_add_fusion.field_ref
  56.4 0.1 collective-permute-start.7
  56.5 1.3 %collective-permute-done.7.part_ref = bf16[32,1536]{1,0:T(8,128)(2,1)S(1)} collective-permute-done((bf16[32,1536]{1,0:T(8,128)(2,1)S(1)}, bf16[32,1536]{1,0:T(8,128)(2,1)S(1)}, u32[]{:S(2)}, u32[]{:S(2)}) %collective-permute-start.7) | collective-permute-done | bytes 98336 | tf_op jit(solution)/shard_map/ppermute | solution.py:342
  57.8 3.5 %all-to-all-done.totals_ref = f32[32,8,128]{2,1,0:T(8,128)S(1)} async-done(((f32[32,8,128]{2,1,0:T(8,128)}), f32[32,8,128]{2,1,0:T(8,128)S(1)}, u32[]{:S(2)}, u32[]{:S(2)}) %all-to-all-start) | async-done | bytes 131104 | tf_op jit(solution)/shard_map/all_to_all | solution.py:385
  61.3 0.7 %shard_map.100 = (f32[32,1536]{1,0:T(8,128)}, f32[32,32]{1,0:T(8,128)}) custom-call(f32[2,32,1536]{2,1,0:T(8,128)S(1)} %convert_add_fusion.field_ref, bf16[32,1536]{1,0:T(8,128)(2,1)S(1)} %collective-permute-done.7.part_ref, f32[32,8,128]{2,1,0:T(8,128)S(1)} %all-to-all-done.totals_ref), custom_call_target="tpu_custom_call" | custom-call | bytes 1024 | tf_op jit(solution)/shard_map/pallas_call | solution.py:388
  (3 shorter events, 0.0 us)
Async XLA Ops:
  0.6 0.9 %copy-start = (bf16[32,1536]{1,0:T(8,128)(2,1)S(1)}, bf16[32,1536]{1,0:T(8,128)(2,1)}, u32[]{:S(2)}) copy-start(bf16[32,1536]{1,0:T(8,128)(2,1)} %own_ref.1) | copy-start | bytes 294916
  1.5 0.7 %copy-start.4 = (f32[4,1536]{1,0:T(4,128)S(1)}, f32[4,1536]{1,0:T(4,128)}, u32[]{:S(2)}) copy-start(f32[4,1536]{1,0:T(4,128)} %geo_ref.1) | copy-start | bytes 73732
  2.3 0.7 %copy-start.5 = (s32[1536]{0:T(1024)S(1)}, s32[1536]{0:T(1024)}, u32[]{:S(2)}) copy-start(s32[1536]{0:T(1024)} %conductor_ref.1) | copy-start | bytes 18436
  3.1 1.5 %collective-permute-start = (bf16[48,1536]{1,0:T(8,128)(2,1)S(1)}, bf16[48,1536]{1,0:T(8,128)(2,1)S(1)}, u32[]{:S(2)}, u32[]{:S(2)}) collective-permute-start(bf16[48,1536]{1,0:T(8,128)(2,1)S(1)} %shard_map.95.own_ref), channel_id=1, source_target_pairs={{8,0},{9,1},{10,2},{11,3},{12,4},{13,5},{14,6},{15,7},{0,8},{1,9},... | collective-permute-start | bytes 442376 | tf_op jit(solution)/shard_map/ppermute | solution.py:342
  4.6 3.9 %copy-start.2 = (bf16[32,16]{1,0:T(8,128)(2,1)S(1)}, bf16[32,16]{1,0:T(8,128)(2,1)}, u32[]{:S(2)}) copy-start(bf16[32,16]{1,0:T(8,128)(2,1)} %constant.29.clone.ltab_ref) | copy-start | bytes 3076
  4.6 3.9 %copy-start.3 = (bf16[32,16]{1,0:T(8,128)(2,1)S(1)}, bf16[32,16]{1,0:T(8,128)(2,1)}, u32[]{:S(2)}) copy-start(bf16[32,16]{1,0:T(8,128)(2,1)} %constant.30.clone.rtab_ref) | copy-start | bytes 3076
  4.6 3.9 %copy-start.6 = (s32[12,128]{1,0:T(8,128)S(1)}, s32[12,128]{1,0:T(8,128)}, u32[]{:S(2)}) copy-start(s32[12,128]{1,0:T(8,128)} %index_ref.1) | copy-start | bytes 18436
  4.7 10.8 %collective-permute-start.1 = (bf16[2,48,1536]{2,1,0:T(8,128)(2,1)S(1)}, bf16[2,48,1536]{2,1,0:T(8,128)(2,1)S(1)}, u32[]{:S(2)}, u32[]{:S(2)}) collective-permute-start(bf16[2,48,1536]{2,1,0:T(8,128)(2,1)S(1)} %pad_maximum_fusion.pair_ref), channel_id=1, source_target_pairs={{1,0},{16,1},{3,2},{18,3},{5,4},{20,5},{7,6},{22,7},{27,8},{10,9},... | collective-permute-start | bytes 884744 | tf_op jit(solution)/shard_map/ppermute | solution.py:342
  8.5 0.7 %copy-start.7 = (s32[12]{0:T(128)S(1)}, s32[12]{0:T(128)}, u32[]{:S(2)}) copy-start(s32[12]{0:T(128)} %count_ref.1) | copy-start | bytes 148
  11.9 20.9 %collective-permute-start.4 = (bf16[2,48,1536]{2,1,0:T(8,128)(2,1)S(1)}, bf16[2,48,1536]{2,1,0:T(8,128)(2,1)S(1)}, u32[]{:S(2)}, u32[]{:S(2)}) collective-permute-start(bf16[2,48,1536]{2,1,0:T(8,128)(2,1)S(1)} %pad_maximum_fusion.pair_ref), channel_id=1, source_target_pairs={{5,0},{20,1},{7,2},{22,3},{1,4},{16,5},{3,6},{18,7},{31,8},{14,9},... | collective-permute-start | bytes 884744 | tf_op jit(solution)/shard_map/ppermute | solution.py:342
  15.5 11.3 %copy-start.1 = (bf16[32,1536]{1,0:T(8,128)(2,1)S(1)}, bf16[32,1536]{1,0:T(8,128)(2,1)}, u32[]{:S(2)}) copy-start(bf16[32,1536]{1,0:T(8,128)(2,1)} %own_ref.1) | copy-start | bytes 294916
  26.7 21.3 %collective-permute-start.2 = (bf16[32,1536]{1,0:T(8,128)(2,1)S(1)}, bf16[32,1536]{1,0:T(8,128)(2,1)S(1)}, u32[]{:S(2)}, u32[]{:S(2)}) collective-permute-start(bf16[32,1536]{1,0:T(8,128)(2,1)S(1)} %copy-done.1), channel_id=1, source_target_pairs={{1,0},{0,1},{3,2},{2,3},{5,4},{4,5},{7,6},{6,7},{9,8},{8,9},{11,10... | collective-permute-start | bytes 294920 | tf_op jit(solution)/shard_map/ppermute | solution.py:342
  28.8 19.2 %collective-permute-start.3 = (bf16[32,1536]{1,0:T(8,128)(2,1)S(1)}, bf16[32,1536]{1,0:T(8,128)(2,1)S(1)}, u32[]{:S(2)}, u32[]{:S(2)}) collective-permute-start(bf16[32,1536]{1,0:T(8,128)(2,1)S(1)} %copy-done.1), channel_id=1, source_target_pairs={{31,0},{2,1},{1,2},{4,3},{3,4},{6,5},{5,6},{8,7},{7,8},{10,9},{9,1... | collective-permute-start | bytes 294920 | tf_op jit(solution)/shard_map/ppermute | solution.py:342
  31.5 19.5 %collective-permute-start.5 = (bf16[2,32,1536]{2,1,0:T(8,128)(2,1)S(1)}, bf16[2,32,1536]{2,1,0:T(8,128)(2,1)S(1)}, u32[]{:S(2)}, u32[]{:S(2)}) collective-permute-start(bf16[2,32,1536]{2,1,0:T(8,128)(2,1)S(1)} %get-tuple-element.29), channel_id=1, source_target_pairs={{0,1},{1,16},{2,3},{3,18},{4,5},{5,20},{6,7},{7,22},{8,27},{9,10},... | collective-permute-start | bytes 589832 | tf_op jit(solution)/shard_map/ppermute | solution.py:347
  32.8 15.2 %copy-start.8 = (bf16[12,128,128]{2,1,0:T(8,128)(2,1)S(1)}, bf16[12,128,128]{2,1,0:T(8,128)(2,1)}, u32[]{:S(2)}) copy-start(bf16[12,128,128]{2,1,0:T(8,128)(2,1)} %weight_ref.1) | copy-start | bytes 1179652
  44.1 12.3 %collective-permute-start.6 = (bf16[2,32,1536]{2,1,0:T(8,128)(2,1)S(1)}, bf16[2,32,1536]{2,1,0:T(8,128)(2,1)S(1)}, u32[]{:S(2)}, u32[]{:S(2)}) collective-permute-start(bf16[2,32,1536]{2,1,0:T(8,128)(2,1)S(1)} %get-tuple-element.32), channel_id=1, source_target_pairs={{0,5},{1,20},{2,7},{3,22},{4,1},{5,16},{6,3},{7,18},{8,31},{9,14},... | collective-permute-start | bytes 589832 | tf_op jit(solution)/shard_map/ppermute | solution.py:347
  51.0 10.3 %all-to-all-start = ((f32[32,8,128]{2,1,0:T(8,128)}), f32[32,8,128]{2,1,0:T(8,128)S(1)}, u32[]{:S(2)}, u32[]{:S(2)}) async-start(f32[32,8,128]{2,1,0:T(8,128)} %get-tuple-element.33), calls=%async_computation | async-start | bytes 262144 | tf_op jit(solution)/shard_map/all_to_all | solution.py:385
  56.4 1.4 %collective-permute-start.7 = (bf16[32,1536]{1,0:T(8,128)(2,1)S(1)}, bf16[32,1536]{1,0:T(8,128)(2,1)S(1)}, u32[]{:S(2)}, u32[]{:S(2)}) collective-permute-start(bf16[32,1536]{1,0:T(8,128)(2,1)S(1)} %fusion), channel_id=1, source_target_pairs={{8,0},{9,1},{10,2},{11,3},{12,4},{13,5},{14,6},{15,7},{0,8},{1,9},... | collective-permute-start | bytes 294920 | tf_op jit(solution)/shard_map/ppermute | solution.py:342

commit v4 on v3

--- a/solution.py
+++ b/solution.py
@@ -13,15 +13,17 @@
 F32 = jnp.float32
 BF16 = jnp.bfloat16
 
-X, NORM, AREA, MEMBER, ONE = 0, 6, 9, 11, 12
-FEATURES = 16
+X, AREA, MEMBER = 0, 6, 7
+FEATURES = 8
+NORM, ONE = 8, 11
+TERMS = 16
 LANES = 128
 DEPTH = 32
 VMEM_LIMIT = 48 * 2**20
 
 
 def chooser(left):
-    table = np.zeros((DEPTH, FEATURES), np.float32)
+    table = np.zeros((DEPTH, TERMS), np.float32)
     row = 0
     for axis in range(3):
         for first in range(2):
@@ -59,27 +61,36 @@
     rhs = charges_ref.shape[0]
     size = geo_ref[3:4, :]
     area = size * size
-    out_ref[0:rhs, :] = (charges_ref[...].astype(F32) * area).astype(BF16)
-    rows_ref[...] = jnp.zeros_like(rows_ref)
-    norm = area
+    rows_ref[0:rhs, :] = charges_ref[...].astype(F32) * area
     for axis in range(3):
         value = geo_ref[axis : axis + 1, :]
         high = rounded(value)
-        low = rounded(value - high)
-        rows_ref[X + 2 * axis : X + 2 * axis + 1, :] = high
-        rows_ref[X + 2 * axis + 1 : X + 2 * axis + 2, :] = low
-        kept = high + low
+        row = rhs + X + 2 * axis
+        rows_ref[row : row + 1, :] = high
+        rows_ref[row + 1 : row + 2, :] = value - high
+    rows_ref[rhs + AREA : rhs + AREA + 1, :] = area
+    rows_ref[rhs + MEMBER : rhs + MEMBER + 1, :] = conductor_ref[...].astype(F32).reshape(1, -1)
+    out_ref[...] = rows_ref[...].astype(BF16)
+
+
+def features_of(bundle):
+    rows = bundle.shape[0]
+    return bundle.astype(F32)[rows - FEATURES :, :]
+
+
+def write_terms(features, terms_ref):
+    norm = features[AREA : AREA + 1, :]
+    for axis in range(3):
+        row = X + 2 * axis
+        kept = features[row : row + 1, :] + features[row + 1 : row + 2, :]
         norm = norm + kept * kept
+    terms_ref[0:FEATURES, :] = features
+    terms_ref[NORM:, :] = jnp.zeros((TERMS - NORM, norm.shape[1]), F32)
     for term in range(3):
         part = rounded(norm)
-        rows_ref[NORM + term : NORM + term + 1, :] = part
+        terms_ref[NORM + term : NORM + term + 1, :] = part
         norm = norm - part
-    high = rounded(area)
-    rows_ref[AREA : AREA + 1, :] = high
-    rows_ref[AREA + 1 : AREA + 2, :] = area - high
-    rows_ref[MEMBER : MEMBER + 1, :] = conductor_ref[...].astype(F32).reshape(1, -1)
-    rows_ref[ONE : ONE + 1, :] = jnp.ones_like(area)
-    out_ref[rhs:, :] = rows_ref[...].astype(BF16)
+    terms_ref[ONE : ONE + 1, :] = jnp.ones_like(norm)
 
 
 def make_bundle(geometry, charges, conductor):
@@ -87,18 +98,18 @@
     return in_vmem(
         bundle_body,
         jax.ShapeDtypeStruct((rhs + FEATURES, panels), BF16),
-        [pltpu.VMEM((FEATURES, panels), F32)],
+        [pltpu.VMEM((rhs + FEATURES, panels), F32)],
     )(geometry, charges, conductor)
 
 
-def left_side(features, table):
+def left_side(terms_ref, table):
     return lax.dot_general(
-        features, table, (((0,), (1,)), ((), ())), preferred_element_type=F32
+        terms_ref[...].astype(BF16), table, (((0,), (1,)), ((), ())), preferred_element_type=F32
     ).astype(BF16)
 
 
-def right_side(features, table):
-    return jnp.dot(table, features, preferred_element_type=F32).astype(BF16)
+def right_side(terms_ref, table):
+    return jnp.dot(table, terms_ref[...].astype(BF16), preferred_element_type=F32).astype(BF16)
 
 
 def tile_of(left, right):
@@ -130,8 +141,8 @@
 
 def totals_of(field, bundle):
     rhs = field.shape[0]
-    features = bundle[rhs:, :].astype(F32)
-    area = features[AREA : AREA + 1, :] + features[AREA + 1 : AREA + 2, :]
+    features = features_of(bundle)
+    area = features[AREA : AREA + 1, :]
     names = lax.broadcasted_iota(jnp.int32, field.shape, 0).astype(F32)
     member = jnp.where(names == features[MEMBER : MEMBER + 1, :], 1.0, 0.0).astype(BF16)
     scaled = field * area
@@ -145,7 +156,7 @@
 
 def self_body(
     rowblk, width, own_ref, ltab_ref, rtab_ref, index_ref, count_ref, odd_ref, out_ref, live_ref,
-    left_ref, right_ref, *slots
+    left_ref, right_ref, terms_ref, *slots
 ):
     _, rhs, panels = out_ref.shape
     groups, near = index_ref.shape
@@ -156,9 +167,9 @@
         moved = jnp.where(index < panels, index + turn, index)
         index = jnp.where(index >= 2 * panels, index - turn, moved)
         live_ref[group : group + 1, :] = jnp.where(slot < count_ref[group], index, -LANES)
-    features = own_ref[rhs:, :]
-    left_ref[...] = left_side(features, ltab_ref[...])
-    right_ref[...] = right_side(features, rtab_ref[...])
+    write_terms(features_of(own_ref[...]), terms_ref)
+    left_ref[...] = left_side(terms_ref, ltab_ref[...])
+    right_ref[...] = right_side(terms_ref, rtab_ref[...])
     out_ref[...] = jnp.zeros_like(out_ref)
 
     def make(step, strip):
@@ -193,6 +204,7 @@
         scratch_shapes=[
             pltpu.VMEM((panels, DEPTH), BF16),
             pltpu.VMEM((DEPTH, panels), BF16),
+            pltpu.VMEM((TERMS, panels), F32),
             pltpu.VMEM((rowblk, panels), BF16),
             pltpu.VMEM((rowblk, panels), BF16),
         ],
@@ -203,12 +215,14 @@
 
 def pairs_body(
     rowblk, width, pair_ref, far_ref, ltab_ref, rtab_ref, field_in, totals_in,
-    field_ref, back_ref, totals_ref, left_ref, right_ref, sum_ref, *slots
+    field_ref, back_ref, totals_ref, left_ref, right_ref, terms_ref, sum_ref, *slots
 ):
     blocks, rhs, panels = field_ref.shape
     for block in range(blocks):
-        left_ref[block] = left_side(far_ref[block, rhs:, :], ltab_ref[...])
-        right_ref[block] = right_side(pair_ref[block, rhs:, :], rtab_ref[...])
+        write_terms(features_of(far_ref[block]), terms_ref)
+        left_ref[block] = left_side(terms_ref, ltab_ref[...])
+        write_terms(features_of(pair_ref[block]), terms_ref)
+        right_ref[block] = right_side(terms_ref, rtab_ref[...])
     field_ref[...] = field_in[...]
     sum_ref[...] = jnp.zeros_like(sum_ref)
     chunks = panels // rowblk
@@ -250,7 +264,7 @@
     blocks, rows, panels = pair.shape
     rhs = rows - FEATURES
     rowblk, width = blocking(panels)
-    work = 800 * panels * panels * blocks * blocks
+    work = 3200 * panels * panels * blocks * blocks
     return in_vmem(
         functools.partial(pairs_body, rowblk, width),
         (
@@ -261,6 +275,7 @@
         [
             pltpu.VMEM((blocks, panels, DEPTH), BF16),
             pltpu.VMEM((blocks, DEPTH, panels), BF16),
+            pltpu.VMEM((TERMS, panels), F32),
             pltpu.VMEM((blocks, rhs, panels), F32),
             pltpu.VMEM((rowblk, panels), BF16),
             pltpu.VMEM((rowblk, panels), BF16),
@@ -325,7 +340,7 @@
         out_specs=(vmem, vmem),
         scratch_shapes=[pltpu.VMEM((3 * panels // LANES * rhs, LANES), BF16)],
         compiler_params=pltpu.CompilerParams(vmem_limit_bytes=VMEM_LIMIT),
-        cost_estimate=pl.CostEstimate(flops=4 * 10**9, bytes_accessed=2**10, transcendentals=0),
+        cost_estimate=pl.CostEstimate(flops=2 * 10**9, bytes_accessed=2**10, transcendentals=0),
     )(twin, own, other, index, weight, field, totals, pair)
 
 

time: 62.3 us -> 60.4 us (0.970)
  waiting for transfers between devices: 9.59 us -> 8.57 us
  starting transfers between devices: 19.6 us -> 18.6 us
    ppermute x2, starting transfers between devices: 5.3 us -> 2.76 us  [send_back(): return lax.ppermute(value, AXES, [(d, source_of(d)) for d in range(count)])]
    all_to_all x1, starting transfers between devices: 2.58 us -> 4.18 us  [paired_blocks(): totals = lax.all_to_all(totals, AXES, 0, 0, tiled=True)]
    ppermute x6, waiting for transfers between devices: 3.29 us -> 2.27 us  [send(): return lax.ppermute(value, AXES, [(source_of(d), d) for d in range(count)])]
    all_to_all x1, waiting for transfers between devices: 3.46 us -> 2.63 us  [paired_blocks(): totals = lax.all_to_all(totals, AXES, 0, 0, tiled=True)]
    ppermute x2, waiting for transfers between devices: 2.83 us -> 3.67 us  [send_back(): return lax.ppermute(value, AXES, [(d, source_of(d)) for d in range(count)])]
  transfers between devices with their start and end apart: 9 -> 9, of which waited for: 5 -> 4; matrix products, arithmetic and copies ran while one was open for 0% -> 0% of each run, Pallas kernels for 45% -> 47%
where the time goes in v4:
time: 60.4 us; the launch traced here: 60.1 us
  Pallas kernels  29.2 us (48%)
  starting transfers between devices  18.6 us (31%)
  waiting for transfers between devices  8.57 us (14%)
  local copies, waits for them, and re-layouts  3 us (5%)
  between operations  0.69 us (1%)
    pallas_call x2, Pallas kernels, pairs_field(): in_vmem(functools.partial(pairs_body, rowblk, width), (jax.ShapeDtypeStru...  22.8 us
    ppermute x6, starting transfers between devices, send(): return lax.ppermute(value, AXES, [(source_of(d), d) for d in range(count)])  11.6 us
    all_to_all x1, starting transfers between devices, paired_blocks(): totals = lax.all_to_all(totals, AXES, 0, 0, tiled=True)  4.18 us
    ppermute x2, waiting for transfers between devices, send_back(): return lax.ppermute(value, AXES, [(d, source_of(d)) for d in range(count)])  3.67 us
    unnamed x18, local copies, waits for them, and re-layouts  2.98 us
    pallas_call x1, Pallas kernels, near_field(): pl.pallas_call(functools.partial(near_body, together), out_shape=(jax.Sha...  2.91 us
    pallas_call x1, Pallas kernels, self_field(): pl.pallas_call(functools.partial(self_body, rowblk, width), out_shape=(ja...  2.77 us
    ppermute x2, starting transfers between devices, send_back(): return lax.ppermute(value, AXES, [(d, source_of(d)) for d in range(count)])  2.76 us
  transfers between devices with their start and end apart: 9, of which 4 were waited for; matrix products, arithmetic and copies ran while one was open for 0% of the time, Pallas kernels for 47%

profile of v4, /device:TPU:0, one launch (start us, length us, event | category | flops | bytes accessed | tf_op | source)
XLA Modules:
  0.0 60.1 jit_solution(700464855730324564)
XLA Ops:
  0.6 0.0 copy-start
  0.6 0.9 %copy-done = bf16[32,1536]{1,0:T(8,128)(2,1)S(1)} copy-done((bf16[32,1536]{1,0:T(8,128)(2,1)S(1)}, bf16[32,1536]{1,0:T(8,128)(2,1)}, u32[]{:S(2)}) %copy-start) | copy-done | bytes 98328
  1.5 0.0 copy-start.4
  1.5 0.7 %copy-done.4 = f32[4,1536]{1,0:T(4,128)S(1)} copy-done((f32[4,1536]{1,0:T(4,128)S(1)}, f32[4,1536]{1,0:T(4,128)}, u32[]{:S(2)}) %copy-start.4) | copy-done | bytes 24600
  2.3 0.0 copy-start.5
  2.3 0.7 %copy-done.5 = s32[1536]{0:T(1024)S(1)} copy-done((s32[1536]{0:T(1024)S(1)}, s32[1536]{0:T(1024)}, u32[]{:S(2)}) %copy-start.5) | copy-done | bytes 6168
  3.0 0.1 shard_map.95.own_ref
  3.0 0.5 collective-permute-start
  3.5 1.0 %collective-permute-done = bf16[40,1536]{1,0:T(8,128)(2,1)S(1)} collective-permute-done((bf16[40,1536]{1,0:T(8,128)(2,1)S(1)}, bf16[40,1536]{1,0:T(8,128)(2,1)S(1)}, u32[]{:S(2)}, u32[]{:S(2)}) %collective-permute-start) | collective-permute-done | bytes 122912 | tf_op jit(solution)/shard_map/ppermute | solution.py:357
  4.5 0.0 copy-start.2
  4.5 0.0 copy-start.3
  4.5 0.0 copy-start.6
  4.5 3.9 %collective-permute-start.1 = (bf16[2,40,1536]{2,1,0:T(8,128)(2,1)S(1)}, bf16[2,40,1536]{2,1,0:T(8,128)(2,1)S(1)}, u32[]{:S(2)}, u32[]{:S(2)}) collective-permute-start(bf16[2,40,1536]{2,1,0:T(8,128)(2,1)S(1)} %pad_maximum_fusion.pair_ref), channel_id=1, source_target_pairs={{1,0},{16,1},{3,2},{18,3},{5,4},{20,5},{7,6},{22,7},{27,8},{10,9},... | collective-permute-start | bytes 737288 | tf_op jit(solution)/shard_map/ppermute | solution.py:357
  8.4 0.0 copy-start.7
  8.4 0.0 copy-done.2
  8.4 0.0 copy-done.3
  8.4 0.0 copy-done.6
  8.4 0.6 %copy-done.7 = s32[12]{0:T(128)S(1)} copy-done((s32[12]{0:T(128)S(1)}, s32[12]{0:T(128)}, u32[]{:S(2)}) %copy-start.7) | copy-done | bytes 72
  9.1 2.8 %shard_map.96 = (f32[2,32,1536]{2,1,0:T(8,128)S(1)}, s32[12,128]{1,0:T(8,128)S(1)}) custom-call(bf16[40,1536]{1,0:T(8,128)(2,1)S(1)} %shard_map.95.own_ref, bf16[32,16]{1,0:T(8,128)(2,1)S(1)} %copy-done.2, bf16[32,16]{1,0:T(8,128)(2,1)S(1)} %copy-done.3, s32[12,128]{1,0:T(8,128)S(1)} %copy-done.6, s32[12]{0:T(128)S(1)} %copy-done.7, s32[1]{0:T(128)} %bitcast.2.odd_ref), custom_call_target="tpu_custom_call" | custom-call | bytes 1024 | tf_op jit(solution)/shard_map/pallas_call | solution.py:196
  11.8 2.6 %collective-permute-start.4 = (bf16[2,40,1536]{2,1,0:T(8,128)(2,1)S(1)}, bf16[2,40,1536]{2,1,0:T(8,128)(2,1)S(1)}, u32[]{:S(2)}, u32[]{:S(2)}) collective-permute-start(bf16[2,40,1536]{2,1,0:T(8,128)(2,1)S(1)} %pad_maximum_fusion.pair_ref), channel_id=1, source_target_pairs={{5,0},{20,1},{7,2},{22,3},{1,4},{16,5},{3,6},{18,7},{31,8},{14,9},... | collective-permute-start | bytes 737288 | tf_op jit(solution)/shard_map/ppermute | solution.py:357
  14.4 0.0 collective-permute-done.1.far_ref
  14.4 0.0 copy-start.1
  14.4 11.4 %shard_map.97 = (f32[2,32,1536]{2,1,0:T(8,128)S(1)}, bf16[2,32,1536]{2,1,0:T(8,128)(2,1)S(1)}, f32[32,32]{1,0:T(8,128)S(1)}) custom-call(bf16[2,40,1536]{2,1,0:T(8,128)(2,1)S(1)} %pad_maximum_fusion.pair_ref, bf16[2,40,1536]{2,1,0:T(8,128)(2,1)S(1)} %collective-permute-done.1.far_ref, bf16[32,16]{1,0:T(8,128)(2,1)S(1)} %copy-done.2, ...), custom_call_target="tpu_custom_call" | custom-call | bytes 1024 | tf_op jit(solution)/shard_map/pallas_call | solution.py:268
  25.8 0.0 copy-done.1
  25.8 2.0 %collective-permute-start.2 = (bf16[32,1536]{1,0:T(8,128)(2,1)S(1)}, bf16[32,1536]{1,0:T(8,128)(2,1)S(1)}, u32[]{:S(2)}, u32[]{:S(2)}) collective-permute-start(bf16[32,1536]{1,0:T(8,128)(2,1)S(1)} %copy-done.1), channel_id=1, source_target_pairs={{1,0},{0,1},{3,2},{2,3},{5,4},{4,5},{7,6},{6,7},{9,8},{8,9},{11,10... | collective-permute-start | bytes 294920 | tf_op jit(solution)/shard_map/ppermute | solution.py:357
  27.8 2.6 %collective-permute-start.3 = (bf16[32,1536]{1,0:T(8,128)(2,1)S(1)}, bf16[32,1536]{1,0:T(8,128)(2,1)S(1)}, u32[]{:S(2)}, u32[]{:S(2)}) collective-permute-start(bf16[32,1536]{1,0:T(8,128)(2,1)S(1)} %copy-done.1), channel_id=1, source_target_pairs={{31,0},{2,1},{1,2},{4,3},{3,4},{6,5},{5,6},{8,7},{7,8},{10,9},{9,1... | collective-permute-start | bytes 294920 | tf_op jit(solution)/shard_map/ppermute | solution.py:357
  30.4 0.9 %collective-permute-start.5 = (bf16[2,32,1536]{2,1,0:T(8,128)(2,1)S(1)}, bf16[2,32,1536]{2,1,0:T(8,128)(2,1)S(1)}, u32[]{:S(2)}, u32[]{:S(2)}) collective-permute-start(bf16[2,32,1536]{2,1,0:T(8,128)(2,1)S(1)} %get-tuple-element.29), channel_id=1, source_target_pairs={{0,1},{1,16},{2,3},{3,18},{4,5},{5,20},{6,7},{7,22},{8,27},{9,10},... | collective-permute-start | bytes 589832 | tf_op jit(solution)/shard_map/ppermute | solution.py:362
  31.3 0.0 collective-permute-done.4.far_ref
  31.3 0.0 copy-start.8
  31.3 11.4 %shard_map.98 = (f32[2,32,1536]{2,1,0:T(8,128)S(1)}, bf16[2,32,1536]{2,1,0:T(8,128)(2,1)S(1)}, f32[32,32]{1,0:T(8,128)S(1)}) custom-call(bf16[2,40,1536]{2,1,0:T(8,128)(2,1)S(1)} %pad_maximum_fusion.pair_ref, bf16[2,40,1536]{2,1,0:T(8,128)(2,1)S(1)} %collective-permute-done.4.far_ref, bf16[32,16]{1,0:T(8,128)(2,1)S(1)} %copy-done.2, ...), custom_call_target="tpu_custom_call" | custom-call | flops 30198988800 | bytes 1024 | tf_op jit(solution)/shard_map/pallas_call | solution.py:268
  42.7 1.9 %collective-permute-start.6 = (bf16[2,32,1536]{2,1,0:T(8,128)(2,1)S(1)}, bf16[2,32,1536]{2,1,0:T(8,128)(2,1)S(1)}, u32[]{:S(2)}, u32[]{:S(2)}) collective-permute-start(bf16[2,32,1536]{2,1,0:T(8,128)(2,1)S(1)} %get-tuple-element.32), channel_id=1, source_target_pairs={{0,5},{1,20},{2,7},{3,22},{4,1},{5,16},{6,3},{7,18},{8,31},{9,14},... | collective-permute-start | bytes 589832 | tf_op jit(solution)/shard_map/ppermute | solution.py:362
  44.5 0.0 collective-permute-done.2.twin_ref
  44.5 0.0 collective-permute-done.3.other_ref
  44.5 0.0 copy-done.8
  44.6 2.9 %shard_map.99 = (f32[2,32,1536]{2,1,0:T(8,128)S(1)}, f32[32,8,128]{2,1,0:T(8,128)}) custom-call(bf16[32,1536]{1,0:T(8,128)(2,1)S(1)} %collective-permute-done.2.twin_ref, bf16[32,1536]{1,0:T(8,128)(2,1)S(1)} %copy-done.1, bf16[32,1536]{1,0:T(8,128)(2,1)S(1)} %collective-permute-done.3.other_ref, s32[12,128]{1,0:T(8,128)S(1)} %get-tuple-element.22.index_ref, ...), custom_call_target="tpu_custom_call" | custom-call | flops 2000000000 | bytes 1024 | tf_op jit(solution)/shard_map/pallas_call | solution.py:333
  47.5 0.0 collective-permute-done.5
  47.5 4.2 %all-to-all-start = ((f32[32,8,128]{2,1,0:T(8,128)}), f32[32,8,128]{2,1,0:T(8,128)S(1)}, u32[]{:S(2)}, u32[]{:S(2)}) async-start(f32[32,8,128]{2,1,0:T(8,128)} %get-tuple-element.33), calls=%async_computation | async-start | bytes 262144 | tf_op jit(solution)/shard_map/all_to_all | solution.py:400
  51.7 3.7 %collective-permute-done.6 = bf16[2,32,1536]{2,1,0:T(8,128)(2,1)S(1)} collective-permute-done((bf16[2,32,1536]{2,1,0:T(8,128)(2,1)S(1)}, bf16[2,32,1536]{2,1,0:T(8,128)(2,1)S(1)}, u32[]{:S(2)}, u32[]{:S(2)}) %collective-permute-start.6) | collective-permute-done | bytes 196640 | tf_op jit(solution)/shard_map/ppermute | solution.py:362
  55.3 0.1 convert_add_fusion.field_ref
  55.4 0.1 collective-permute-start.7
  55.5 1.3 %collective-permute-done.7.part_ref = bf16[32,1536]{1,0:T(8,128)(2,1)S(1)} collective-permute-done((bf16[32,1536]{1,0:T(8,128)(2,1)S(1)}, bf16[32,1536]{1,0:T(8,128)(2,1)S(1)}, u32[]{:S(2)}, u32[]{:S(2)}) %collective-permute-start.7) | collective-permute-done | bytes 98336 | tf_op jit(solution)/shard_map/ppermute | solution.py:357
  56.8 2.6 %all-to-all-done.totals_ref = f32[32,8,128]{2,1,0:T(8,128)S(1)} async-done(((f32[32,8,128]{2,1,0:T(8,128)}), f32[32,8,128]{2,1,0:T(8,128)S(1)}, u32[]{:S(2)}, u32[]{:S(2)}) %all-to-all-start) | async-done | bytes 131104 | tf_op jit(solution)/shard_map/all_to_all | solution.py:400
  59.4 0.7 %shard_map.100 = (f32[32,1536]{1,0:T(8,128)}, f32[32,32]{1,0:T(8,128)}) custom-call(f32[2,32,1536]{2,1,0:T(8,128)S(1)} %convert_add_fusion.field_ref, bf16[32,1536]{1,0:T(8,128)(2,1)S(1)} %collective-permute-done.7.part_ref, f32[32,8,128]{2,1,0:T(8,128)S(1)} %all-to-all-done.totals_ref), custom_call_target="tpu_custom_call" | custom-call | bytes 1024 | tf_op jit(solution)/shard_map/pallas_call | solution.py:403
  (3 shorter events, 0.0 us)
Async XLA Ops:
  0.6 0.9 %copy-start = (bf16[32,1536]{1,0:T(8,128)(2,1)S(1)}, bf16[32,1536]{1,0:T(8,128)(2,1)}, u32[]{:S(2)}) copy-start(bf16[32,1536]{1,0:T(8,128)(2,1)} %own_ref.1) | copy-start | bytes 294916
  1.5 0.7 %copy-start.4 = (f32[4,1536]{1,0:T(4,128)S(1)}, f32[4,1536]{1,0:T(4,128)}, u32[]{:S(2)}) copy-start(f32[4,1536]{1,0:T(4,128)} %geo_ref.1) | copy-start | bytes 73732
  2.3 0.7 %copy-start.5 = (s32[1536]{0:T(1024)S(1)}, s32[1536]{0:T(1024)}, u32[]{:S(2)}) copy-start(s32[1536]{0:T(1024)} %conductor_ref.1) | copy-start | bytes 18436
  3.0 1.5 %collective-permute-start = (bf16[40,1536]{1,0:T(8,128)(2,1)S(1)}, bf16[40,1536]{1,0:T(8,128)(2,1)S(1)}, u32[]{:S(2)}, u32[]{:S(2)}) collective-permute-start(bf16[40,1536]{1,0:T(8,128)(2,1)S(1)} %shard_map.95.own_ref), channel_id=1, source_target_pairs={{8,0},{9,1},{10,2},{11,3},{12,4},{13,5},{14,6},{15,7},{0,8},{1,9},... | collective-permute-start | bytes 368648 | tf_op jit(solution)/shard_map/ppermute | solution.py:357
  4.5 3.9 %copy-start.2 = (bf16[32,16]{1,0:T(8,128)(2,1)S(1)}, bf16[32,16]{1,0:T(8,128)(2,1)}, u32[]{:S(2)}) copy-start(bf16[32,16]{1,0:T(8,128)(2,1)} %constant.29.clone.ltab_ref) | copy-start | bytes 3076
  4.5 3.9 %copy-start.3 = (bf16[32,16]{1,0:T(8,128)(2,1)S(1)}, bf16[32,16]{1,0:T(8,128)(2,1)}, u32[]{:S(2)}) copy-start(bf16[32,16]{1,0:T(8,128)(2,1)} %constant.30.clone.rtab_ref) | copy-start | bytes 3076
  4.5 3.9 %copy-start.6 = (s32[12,128]{1,0:T(8,128)S(1)}, s32[12,128]{1,0:T(8,128)}, u32[]{:S(2)}) copy-start(s32[12,128]{1,0:T(8,128)} %index_ref.1) | copy-start | bytes 18436
  4.5 9.8 %collective-permute-start.1 = (bf16[2,40,1536]{2,1,0:T(8,128)(2,1)S(1)}, bf16[2,40,1536]{2,1,0:T(8,128)(2,1)S(1)}, u32[]{:S(2)}, u32[]{:S(2)}) collective-permute-start(bf16[2,40,1536]{2,1,0:T(8,128)(2,1)S(1)} %pad_maximum_fusion.pair_ref), channel_id=1, source_target_pairs={{1,0},{16,1},{3,2},{18,3},{5,4},{20,5},{7,6},{22,7},{27,8},{10,9},... | collective-permute-start | bytes 737288 | tf_op jit(solution)/shard_map/ppermute | solution.py:357
  8.4 0.7 %copy-start.7 = (s32[12]{0:T(128)S(1)}, s32[12]{0:T(128)}, u32[]{:S(2)}) copy-start(s32[12]{0:T(128)} %count_ref.1) | copy-start | bytes 148
  11.8 19.5 %collective-permute-start.4 = (bf16[2,40,1536]{2,1,0:T(8,128)(2,1)S(1)}, bf16[2,40,1536]{2,1,0:T(8,128)(2,1)S(1)}, u32[]{:S(2)}, u32[]{:S(2)}) collective-permute-start(bf16[2,40,1536]{2,1,0:T(8,128)(2,1)S(1)} %pad_maximum_fusion.pair_ref), channel_id=1, source_target_pairs={{5,0},{20,1},{7,2},{22,3},{1,4},{16,5},{3,6},{18,7},{31,8},{14,9},... | collective-permute-start | bytes 737288 | tf_op jit(solution)/shard_map/ppermute | solution.py:357
  14.4 11.4 %copy-start.1 = (bf16[32,1536]{1,0:T(8,128)(2,1)S(1)}, bf16[32,1536]{1,0:T(8,128)(2,1)}, u32[]{:S(2)}) copy-start(bf16[32,1536]{1,0:T(8,128)(2,1)} %own_ref.1) | copy-start | bytes 294916
  25.8 18.8 %collective-permute-start.2 = (bf16[32,1536]{1,0:T(8,128)(2,1)S(1)}, bf16[32,1536]{1,0:T(8,128)(2,1)S(1)}, u32[]{:S(2)}, u32[]{:S(2)}) collective-permute-start(bf16[32,1536]{1,0:T(8,128)(2,1)S(1)} %copy-done.1), channel_id=1, source_target_pairs={{1,0},{0,1},{3,2},{2,3},{5,4},{4,5},{7,6},{6,7},{9,8},{8,9},{11,10... | collective-permute-start | bytes 294920 | tf_op jit(solution)/shard_map/ppermute | solution.py:357
  27.8 16.8 %collective-permute-start.3 = (bf16[32,1536]{1,0:T(8,128)(2,1)S(1)}, bf16[32,1536]{1,0:T(8,128)(2,1)S(1)}, u32[]{:S(2)}, u32[]{:S(2)}) collective-permute-start(bf16[32,1536]{1,0:T(8,128)(2,1)S(1)} %copy-done.1), channel_id=1, source_target_pairs={{31,0},{2,1},{1,2},{4,3},{3,4},{6,5},{5,6},{8,7},{7,8},{10,9},{9,1... | collective-permute-start | bytes 294920 | tf_op jit(solution)/shard_map/ppermute | solution.py:357
  30.4 17.1 %collective-permute-start.5 = (bf16[2,32,1536]{2,1,0:T(8,128)(2,1)S(1)}, bf16[2,32,1536]{2,1,0:T(8,128)(2,1)S(1)}, u32[]{:S(2)}, u32[]{:S(2)}) collective-permute-start(bf16[2,32,1536]{2,1,0:T(8,128)(2,1)S(1)} %get-tuple-element.29), channel_id=1, source_target_pairs={{0,1},{1,16},{2,3},{3,18},{4,5},{5,20},{6,7},{7,22},{8,27},{9,10},... | collective-permute-start | bytes 589832 | tf_op jit(solution)/shard_map/ppermute | solution.py:362
  31.3 13.3 %copy-start.8 = (bf16[12,128,128]{2,1,0:T(8,128)(2,1)S(1)}, bf16[12,128,128]{2,1,0:T(8,128)(2,1)}, u32[]{:S(2)}) copy-start(bf16[12,128,128]{2,1,0:T(8,128)(2,1)} %weight_ref.1) | copy-start | bytes 1179652
  42.7 12.7 %collective-permute-start.6 = (bf16[2,32,1536]{2,1,0:T(8,128)(2,1)S(1)}, bf16[2,32,1536]{2,1,0:T(8,128)(2,1)S(1)}, u32[]{:S(2)}, u32[]{:S(2)}) collective-permute-start(bf16[2,32,1536]{2,1,0:T(8,128)(2,1)S(1)} %get-tuple-element.32), channel_id=1, source_target_pairs={{0,5},{1,20},{2,7},{3,22},{4,1},{5,16},{6,3},{7,18},{8,31},{9,14},... | collective-permute-start | bytes 589832 | tf_op jit(solution)/shard_map/ppermute | solution.py:362
  47.5 11.9 %all-to-all-start = ((f32[32,8,128]{2,1,0:T(8,128)}), f32[32,8,128]{2,1,0:T(8,128)S(1)}, u32[]{:S(2)}, u32[]{:S(2)}) async-start(f32[32,8,128]{2,1,0:T(8,128)} %get-tuple-element.33), calls=%async_computation | async-start | bytes 262144 | tf_op jit(solution)/shard_map/all_to_all | solution.py:400
  55.4 1.4 %collective-permute-start.7 = (bf16[32,1536]{1,0:T(8,128)(2,1)S(1)}, bf16[32,1536]{1,0:T(8,128)(2,1)S(1)}, u32[]{:S(2)}, u32[]{:S(2)}) collective-permute-start(bf16[32,1536]{1,0:T(8,128)(2,1)S(1)} %fusion), channel_id=1, source_target_pairs={{8,0},{9,1},{10,2},{11,3},{12,4},{13,5},{14,6},{15,7},{0,8},{1,9},... | collective-permute-start | bytes 294920 | tf_op jit(solution)/shard_map/ppermute | solution.py:357

commit v5 on v4

--- a/solution.py
+++ b/solution.py
@@ -155,8 +155,8 @@
 
 
 def self_body(
-    rowblk, width, own_ref, ltab_ref, rtab_ref, index_ref, count_ref, odd_ref, out_ref, live_ref,
-    left_ref, right_ref, terms_ref, *slots
+    rowblk, width, pair_ref, ltab_ref, rtab_ref, index_ref, count_ref, odd_ref, out_ref, live_ref,
+    right_ref, left_ref, terms_ref, *slots
 ):
     _, rhs, panels = out_ref.shape
     groups, near = index_ref.shape
@@ -167,28 +167,30 @@
         moved = jnp.where(index < panels, index + turn, index)
         index = jnp.where(index >= 2 * panels, index - turn, moved)
         live_ref[group : group + 1, :] = jnp.where(slot < count_ref[group], index, -LANES)
-    write_terms(features_of(own_ref[...]), terms_ref)
+    write_terms(features_of(pair_ref[1]), terms_ref)
+    right_ref[1] = right_side(terms_ref, rtab_ref[...])
+    write_terms(features_of(pair_ref[0]), terms_ref)
     left_ref[...] = left_side(terms_ref, ltab_ref[...])
-    right_ref[...] = right_side(terms_ref, rtab_ref[...])
+    right_ref[0] = right_side(terms_ref, rtab_ref[...])
     out_ref[...] = jnp.zeros_like(out_ref)
 
     def make(step, strip):
         start = pl.multiple_of(step * rowblk, rowblk)
-        return tile_of(left_ref[pl.ds(start, rowblk), :], right_ref[:, strip : strip + width])
+        return tile_of(left_ref[pl.ds(start, rowblk), :], right_ref[0, :, strip : strip + width])
 
     def use(step, tile, strip, carry):
         if tile is None:
             return
         start = pl.multiple_of(step * rowblk, rowblk)
         out_ref[0, :, strip : strip + width] += jnp.dot(
-            own_ref[0:rhs, pl.ds(start, rowblk)], tile, preferred_element_type=F32
+            pair_ref[0, 0:rhs, pl.ds(start, rowblk)], tile, preferred_element_type=F32
         )
 
     two_stage(panels // rowblk, make, use, slots, width)
 
 
-def self_field(own, tables, index, count, odd):
-    rows, panels = own.shape
+def self_field(pair, tables, index, count, odd):
+    blocks, rows, panels = pair.shape
     rhs = rows - FEATURES
     rowblk, width = blocking(panels)
     vmem = pl.BlockSpec(memory_space=pltpu.VMEM)
@@ -196,33 +198,31 @@
     return pl.pallas_call(
         functools.partial(self_body, rowblk, width),
         out_shape=(
-            jax.ShapeDtypeStruct((2, rhs, panels), F32),
+            jax.ShapeDtypeStruct((blocks, rhs, panels), F32),
             jax.ShapeDtypeStruct(index.shape, index.dtype),
+            jax.ShapeDtypeStruct((blocks, DEPTH, panels), BF16),
         ),
         in_specs=[vmem] * 4 + [smem] * 2,
-        out_specs=(vmem, vmem),
+        out_specs=(vmem, vmem, vmem),
         scratch_shapes=[
             pltpu.VMEM((panels, DEPTH), BF16),
-            pltpu.VMEM((DEPTH, panels), BF16),
             pltpu.VMEM((TERMS, panels), F32),
             pltpu.VMEM((rowblk, panels), BF16),
             pltpu.VMEM((rowblk, panels), BF16),
         ],
         compiler_params=pltpu.CompilerParams(vmem_limit_bytes=VMEM_LIMIT),
         cost_estimate=pl.CostEstimate(flops=0, bytes_accessed=2**10, transcendentals=0),
-    )(own, *tables, index, count, odd)
+    )(pair, *tables, index, count, odd)
 
 
 def pairs_body(
-    rowblk, width, pair_ref, far_ref, ltab_ref, rtab_ref, field_in, totals_in,
-    field_ref, back_ref, totals_ref, left_ref, right_ref, terms_ref, sum_ref, *slots
+    rowblk, width, pair_ref, far_ref, ltab_ref, right_ref, field_in, totals_in,
+    field_ref, back_ref, totals_ref, left_ref, terms_ref, sum_ref, *slots
 ):
     blocks, rhs, panels = field_ref.shape
     for block in range(blocks):
         write_terms(features_of(far_ref[block]), terms_ref)
         left_ref[block] = left_side(terms_ref, ltab_ref[...])
-        write_terms(features_of(pair_ref[block]), terms_ref)
-        right_ref[block] = right_side(terms_ref, rtab_ref[...])
     field_ref[...] = field_in[...]
     sum_ref[...] = jnp.zeros_like(sum_ref)
     chunks = panels // rowblk
@@ -260,7 +260,7 @@
     back_ref[...] = sum_ref[...].astype(BF16)
 
 
-def pairs_field(pair, far, tables, field, totals, last):
+def pairs_field(pair, far, table, right, field, totals, last):
     blocks, rows, panels = pair.shape
     rhs = rows - FEATURES
     rowblk, width = blocking(panels)
@@ -274,14 +274,13 @@
         ),
         [
             pltpu.VMEM((blocks, panels, DEPTH), BF16),
-            pltpu.VMEM((blocks, DEPTH, panels), BF16),
             pltpu.VMEM((TERMS, panels), F32),
             pltpu.VMEM((blocks, rhs, panels), F32),
             pltpu.VMEM((rowblk, panels), BF16),
             pltpu.VMEM((rowblk, panels), BF16),
         ],
         flops=work if last else 0,
-    )(pair, far, *tables, field, totals)
+    )(pair, far, table, right, field, totals)
 
 
 def near_body(
@@ -382,16 +381,16 @@
     pair = jnp.stack([bundle, sibling])
     close = send(pair, lambda d: partner(d, False))
     odd = (lax.axis_index(AXES) % 2).reshape(1)
-    field, live = self_field(bundle, tables, near_index, near_count, odd)
+    field, live, right = self_field(pair, tables, near_index, near_count, odd)
     late_pair, field = lax.optimization_barrier((pair, field))
     far = send(late_pair, lambda d: partner(d, True))
     totals = jnp.zeros((rhs, rhs), F32)
-    field, close_back, totals = pairs_field(pair, close, tables, field, totals, False)
+    field, close_back, totals = pairs_field(pair, close, tables[0], right, field, totals, False)
     close_back = send_back(close_back, lambda d: partner(d, False))
     late_charges, field = lax.optimization_barrier((charges, field))
     twin = send(late_charges, lambda d: d ^ 1)
     other = send(late_charges, other_neighbour)
-    field, far_back, totals = pairs_field(pair, far, tables, field, totals, True)
+    field, far_back, totals = pairs_field(pair, far, tables[0], right, field, totals, True)
     far_back = send_back(far_back, lambda d: partner(d, True))
     field, totals = near_field(
         twin, charges, other, live, near_weight, field, totals, pair

time: 60.4 us -> 60.3 us (level)
  no operation moved by 1% of the time
where the time goes in v5:
time: 60.3 us; the launch traced here: 60 us
  Pallas kernels  29 us (48%)
  starting transfers between devices  18.6 us (31%)
  waiting for transfers between devices  8.57 us (14%)
  local copies, waits for them, and re-layouts  3 us (5%)
  between operations  0.69 us (1%)
    pallas_call x2, Pallas kernels, pairs_field(): in_vmem(functools.partial(pairs_body, rowblk, width), (jax.ShapeDtypeStru...  22.6 us
    ppermute x6, starting transfers between devices, send(): return lax.ppermute(value, AXES, [(source_of(d), d) for d in range(count)])  11.7 us
    all_to_all x1, starting transfers between devices, paired_blocks(): totals = lax.all_to_all(totals, AXES, 0, 0, tiled=True)  4.18 us
    ppermute x2, waiting for transfers between devices, send_back(): return lax.ppermute(value, AXES, [(d, source_of(d)) for d in range(count)])  3.66 us
    unnamed x18, local copies, waits for them, and re-layouts  2.98 us
    pallas_call x1, Pallas kernels, near_field(): pl.pallas_call(functools.partial(near_body, together), out_shape=(jax.Sha...  2.91 us
    ppermute x2, starting transfers between devices, send_back(): return lax.ppermute(value, AXES, [(d, source_of(d)) for d in range(count)])  2.79 us
    pallas_call x1, Pallas kernels, self_field(): pl.pallas_call(functools.partial(self_body, rowblk, width), out_shape=(ja...  2.73 us
  transfers between devices with their start and end apart: 9, of which 4 were waited for; matrix products, arithmetic and copies ran while one was open for 0% of the time, Pallas kernels for 47%

profile of v5, /device:TPU:0, one launch (start us, length us, event | category | flops | bytes accessed | tf_op | source)
XLA Modules:
  0.0 60.0 jit_solution(8750826237972841510)
XLA Ops:
  0.6 0.0 copy-start
  0.6 0.9 %copy-done = bf16[32,1536]{1,0:T(8,128)(2,1)S(1)} copy-done((bf16[32,1536]{1,0:T(8,128)(2,1)S(1)}, bf16[32,1536]{1,0:T(8,128)(2,1)}, u32[]{:S(2)}) %copy-start) | copy-done | bytes 98328
  1.5 0.0 copy-start.3
  1.5 0.7 %copy-done.3 = f32[4,1536]{1,0:T(4,128)S(1)} copy-done((f32[4,1536]{1,0:T(4,128)S(1)}, f32[4,1536]{1,0:T(4,128)}, u32[]{:S(2)}) %copy-start.3) | copy-done | bytes 24600
  2.3 0.0 copy-start.4
  2.3 0.7 %copy-done.4 = s32[1536]{0:T(1024)S(1)} copy-done((s32[1536]{0:T(1024)S(1)}, s32[1536]{0:T(1024)}, u32[]{:S(2)}) %copy-start.4) | copy-done | bytes 6168
  3.0 0.1 shard_map.95
  3.0 0.5 collective-permute-start
  3.5 1.0 %collective-permute-done = bf16[40,1536]{1,0:T(8,128)(2,1)S(1)} collective-permute-done((bf16[40,1536]{1,0:T(8,128)(2,1)S(1)}, bf16[40,1536]{1,0:T(8,128)(2,1)S(1)}, u32[]{:S(2)}, u32[]{:S(2)}) %collective-permute-start) | collective-permute-done | bytes 122912 | tf_op jit(solution)/shard_map/ppermute | solution.py:356
  4.5 0.0 copy-start.2
  4.5 0.0 copy-start.5
  4.5 0.0 copy-start.6
  4.5 3.9 %collective-permute-start.1 = (bf16[2,40,1536]{2,1,0:T(8,128)(2,1)S(1)}, bf16[2,40,1536]{2,1,0:T(8,128)(2,1)S(1)}, u32[]{:S(2)}, u32[]{:S(2)}) collective-permute-start(bf16[2,40,1536]{2,1,0:T(8,128)(2,1)S(1)} %pad_maximum_fusion.pair_ref), channel_id=1, source_target_pairs={{1,0},{16,1},{3,2},{18,3},{5,4},{20,5},{7,6},{22,7},{27,8},{10,9},... | collective-permute-start | bytes 737288 | tf_op jit(solution)/shard_map/ppermute | solution.py:356
  8.4 0.0 copy-start.7
  8.4 0.0 copy-done.2
  8.4 0.0 copy-done.5
  8.4 0.0 copy-done.6
  8.4 0.6 %copy-done.7 = s32[12]{0:T(128)S(1)} copy-done((s32[12]{0:T(128)S(1)}, s32[12]{0:T(128)}, u32[]{:S(2)}) %copy-start.7) | copy-done | bytes 72
  9.1 2.7 %shard_map.96 = (f32[2,32,1536]{2,1,0:T(8,128)S(1)}, s32[12,128]{1,0:T(8,128)S(1)}, bf16[2,32,1536]{2,1,0:T(8,128)(2,1)S(1)}) custom-call(bf16[2,40,1536]{2,1,0:T(8,128)(2,1)S(1)} %pad_maximum_fusion.pair_ref, bf16[32,16]{1,0:T(8,128)(2,1)S(1)} %copy-done.2, bf16[32,16]{1,0:T(8,128)(2,1)S(1)} %copy-done.6, s32[12,128]{1,0:T(8,128)S(1)} %copy-done.5, ...), custom_call_target="tpu_custom_call" | custom-call | bytes 1024 | tf_op jit(solution)/shard_map/pallas_call | solution.py:198
  11.8 2.6 %collective-permute-start.4 = (bf16[2,40,1536]{2,1,0:T(8,128)(2,1)S(1)}, bf16[2,40,1536]{2,1,0:T(8,128)(2,1)S(1)}, u32[]{:S(2)}, u32[]{:S(2)}) collective-permute-start(bf16[2,40,1536]{2,1,0:T(8,128)(2,1)S(1)} %pad_maximum_fusion.pair_ref), channel_id=1, source_target_pairs={{5,0},{20,1},{7,2},{22,3},{1,4},{16,5},{3,6},{18,7},{31,8},{14,9},... | collective-permute-start | bytes 737288 | tf_op jit(solution)/shard_map/ppermute | solution.py:356
  14.3 0.0 collective-permute-done.1.far_ref
  14.4 0.0 copy-start.1
  14.4 11.3 %shard_map.97 = (f32[2,32,1536]{2,1,0:T(8,128)S(1)}, bf16[2,32,1536]{2,1,0:T(8,128)(2,1)S(1)}, f32[32,32]{1,0:T(8,128)S(1)}) custom-call(bf16[2,40,1536]{2,1,0:T(8,128)(2,1)S(1)} %pad_maximum_fusion.pair_ref, bf16[2,40,1536]{2,1,0:T(8,128)(2,1)S(1)} %collective-permute-done.1.far_ref, bf16[32,16]{1,0:T(8,128)(2,1)S(1)} %copy-done.2, ...), custom_call_target="tpu_custom_call" | custom-call | bytes 1024 | tf_op jit(solution)/shard_map/pallas_call | solution.py:268
  25.7 0.0 copy-done.1
  25.7 2.0 %collective-permute-start.2 = (bf16[32,1536]{1,0:T(8,128)(2,1)S(1)}, bf16[32,1536]{1,0:T(8,128)(2,1)S(1)}, u32[]{:S(2)}, u32[]{:S(2)}) collective-permute-start(bf16[32,1536]{1,0:T(8,128)(2,1)S(1)} %copy-done.1), channel_id=1, source_target_pairs={{1,0},{0,1},{3,2},{2,3},{5,4},{4,5},{7,6},{6,7},{9,8},{8,9},{11,10... | collective-permute-start | bytes 294920 | tf_op jit(solution)/shard_map/ppermute | solution.py:356
  27.7 2.6 %collective-permute-start.3 = (bf16[32,1536]{1,0:T(8,128)(2,1)S(1)}, bf16[32,1536]{1,0:T(8,128)(2,1)S(1)}, u32[]{:S(2)}, u32[]{:S(2)}) collective-permute-start(bf16[32,1536]{1,0:T(8,128)(2,1)S(1)} %copy-done.1), channel_id=1, source_target_pairs={{31,0},{2,1},{1,2},{4,3},{3,4},{6,5},{5,6},{8,7},{7,8},{10,9},{9,1... | collective-permute-start | bytes 294920 | tf_op jit(solution)/shard_map/ppermute | solution.py:356
  30.3 0.9 %collective-permute-start.5 = (bf16[2,32,1536]{2,1,0:T(8,128)(2,1)S(1)}, bf16[2,32,1536]{2,1,0:T(8,128)(2,1)S(1)}, u32[]{:S(2)}, u32[]{:S(2)}) collective-permute-start(bf16[2,32,1536]{2,1,0:T(8,128)(2,1)S(1)} %get-tuple-element.31), channel_id=1, source_target_pairs={{0,1},{1,16},{2,3},{3,18},{4,5},{5,20},{6,7},{7,22},{8,27},{9,10},... | collective-permute-start | bytes 589832 | tf_op jit(solution)/shard_map/ppermute | solution.py:361
  31.3 0.0 collective-permute-done.4.far_ref
  31.3 0.0 copy-start.8
  31.3 11.3 %shard_map.98 = (f32[2,32,1536]{2,1,0:T(8,128)S(1)}, bf16[2,32,1536]{2,1,0:T(8,128)(2,1)S(1)}, f32[32,32]{1,0:T(8,128)S(1)}) custom-call(bf16[2,40,1536]{2,1,0:T(8,128)(2,1)S(1)} %pad_maximum_fusion.pair_ref, bf16[2,40,1536]{2,1,0:T(8,128)(2,1)S(1)} %collective-permute-done.4.far_ref, bf16[32,16]{1,0:T(8,128)(2,1)S(1)} %copy-done.2, ...), custom_call_target="tpu_custom_call" | custom-call | flops 30198988800 | bytes 1024 | tf_op jit(solution)/shard_map/pallas_call | solution.py:268
  42.6 1.9 %collective-permute-start.6 = (bf16[2,32,1536]{2,1,0:T(8,128)(2,1)S(1)}, bf16[2,32,1536]{2,1,0:T(8,128)(2,1)S(1)}, u32[]{:S(2)}, u32[]{:S(2)}) collective-permute-start(bf16[2,32,1536]{2,1,0:T(8,128)(2,1)S(1)} %get-tuple-element.34), channel_id=1, source_target_pairs={{0,5},{1,20},{2,7},{3,22},{4,1},{5,16},{6,3},{7,18},{8,31},{9,14},... | collective-permute-start | bytes 589832 | tf_op jit(solution)/shard_map/ppermute | solution.py:361
  44.4 0.0 collective-permute-done.2.twin_ref
  44.4 0.0 collective-permute-done.3.other_ref
  44.4 0.0 copy-done.8
  44.4 2.9 %shard_map.99 = (f32[2,32,1536]{2,1,0:T(8,128)S(1)}, f32[32,8,128]{2,1,0:T(8,128)}) custom-call(bf16[32,1536]{1,0:T(8,128)(2,1)S(1)} %collective-permute-done.2.twin_ref, bf16[32,1536]{1,0:T(8,128)(2,1)S(1)} %copy-done.1, bf16[32,1536]{1,0:T(8,128)(2,1)S(1)} %collective-permute-done.3.other_ref, s32[12,128]{1,0:T(8,128)S(1)} %get-tuple-element.24.index_ref, ...), custom_call_target="tpu_custom_call" | custom-call | flops 2000000000 | bytes 1024 | tf_op jit(solution)/shard_map/pallas_call | solution.py:332
  47.4 0.0 collective-permute-done.5
  47.4 4.2 %all-to-all-start = ((f32[32,8,128]{2,1,0:T(8,128)}), f32[32,8,128]{2,1,0:T(8,128)S(1)}, u32[]{:S(2)}, u32[]{:S(2)}) async-start(f32[32,8,128]{2,1,0:T(8,128)} %get-tuple-element.35), calls=%async_computation | async-start | bytes 262144 | tf_op jit(solution)/shard_map/all_to_all | solution.py:399
  51.5 3.7 %collective-permute-done.6 = bf16[2,32,1536]{2,1,0:T(8,128)(2,1)S(1)} collective-permute-done((bf16[2,32,1536]{2,1,0:T(8,128)(2,1)S(1)}, bf16[2,32,1536]{2,1,0:T(8,128)(2,1)S(1)}, u32[]{:S(2)}, u32[]{:S(2)}) %collective-permute-start.6) | collective-permute-done | bytes 196640 | tf_op jit(solution)/shard_map/ppermute | solution.py:361
  55.2 0.1 convert_add_fusion.field_ref
  55.3 0.1 collective-permute-start.7
  55.4 1.3 %collective-permute-done.7.part_ref = bf16[32,1536]{1,0:T(8,128)(2,1)S(1)} collective-permute-done((bf16[32,1536]{1,0:T(8,128)(2,1)S(1)}, bf16[32,1536]{1,0:T(8,128)(2,1)S(1)}, u32[]{:S(2)}, u32[]{:S(2)}) %collective-permute-start.7) | collective-permute-done | bytes 98336 | tf_op jit(solution)/shard_map/ppermute | solution.py:356
  56.7 2.6 %all-to-all-done.totals_ref = f32[32,8,128]{2,1,0:T(8,128)S(1)} async-done(((f32[32,8,128]{2,1,0:T(8,128)}), f32[32,8,128]{2,1,0:T(8,128)S(1)}, u32[]{:S(2)}, u32[]{:S(2)}) %all-to-all-start) | async-done | bytes 131104 | tf_op jit(solution)/shard_map/all_to_all | solution.py:399
  59.3 0.7 %shard_map.100 = (f32[32,1536]{1,0:T(8,128)}, f32[32,32]{1,0:T(8,128)}) custom-call(f32[2,32,1536]{2,1,0:T(8,128)S(1)} %convert_add_fusion.field_ref, bf16[32,1536]{1,0:T(8,128)(2,1)S(1)} %collective-permute-done.7.part_ref, f32[32,8,128]{2,1,0:T(8,128)S(1)} %all-to-all-done.totals_ref), custom_call_target="tpu_custom_call" | custom-call | bytes 1024 | tf_op jit(solution)/shard_map/pallas_call | solution.py:402
  (3 shorter events, 0.0 us)
Async XLA Ops:
  0.6 0.9 %copy-start = (bf16[32,1536]{1,0:T(8,128)(2,1)S(1)}, bf16[32,1536]{1,0:T(8,128)(2,1)}, u32[]{:S(2)}) copy-start(bf16[32,1536]{1,0:T(8,128)(2,1)} %own_ref.1) | copy-start | bytes 294916
  1.5 0.7 %copy-start.3 = (f32[4,1536]{1,0:T(4,128)S(1)}, f32[4,1536]{1,0:T(4,128)}, u32[]{:S(2)}) copy-start(f32[4,1536]{1,0:T(4,128)} %geo_ref.1) | copy-start | bytes 73732
  2.3 0.7 %copy-start.4 = (s32[1536]{0:T(1024)S(1)}, s32[1536]{0:T(1024)}, u32[]{:S(2)}) copy-start(s32[1536]{0:T(1024)} %conductor_ref.1) | copy-start | bytes 18436
  3.0 1.5 %collective-permute-start = (bf16[40,1536]{1,0:T(8,128)(2,1)S(1)}, bf16[40,1536]{1,0:T(8,128)(2,1)S(1)}, u32[]{:S(2)}, u32[]{:S(2)}) collective-permute-start(bf16[40,1536]{1,0:T(8,128)(2,1)S(1)} %shard_map.95), channel_id=1, source_target_pairs={{8,0},{9,1},{10,2},{11,3},{12,4},{13,5},{14,6},{15,7},{0,8},{1,9},... | collective-permute-start | bytes 368648 | tf_op jit(solution)/shard_map/ppermute | solution.py:356
  4.5 3.9 %copy-start.2 = (bf16[32,16]{1,0:T(8,128)(2,1)S(1)}, bf16[32,16]{1,0:T(8,128)(2,1)}, u32[]{:S(2)}) copy-start(bf16[32,16]{1,0:T(8,128)(2,1)} %constant.29.clone.ltab_ref) | copy-start | bytes 3076
  4.5 3.9 %copy-start.5 = (s32[12,128]{1,0:T(8,128)S(1)}, s32[12,128]{1,0:T(8,128)}, u32[]{:S(2)}) copy-start(s32[12,128]{1,0:T(8,128)} %index_ref.1) | copy-start | bytes 18436
  4.5 3.9 %copy-start.6 = (bf16[32,16]{1,0:T(8,128)(2,1)S(1)}, bf16[32,16]{1,0:T(8,128)(2,1)}, u32[]{:S(2)}) copy-start(bf16[32,16]{1,0:T(8,128)(2,1)} %constant.30.clone.rtab_ref) | copy-start | bytes 3076
  4.5 9.8 %collective-permute-start.1 = (bf16[2,40,1536]{2,1,0:T(8,128)(2,1)S(1)}, bf16[2,40,1536]{2,1,0:T(8,128)(2,1)S(1)}, u32[]{:S(2)}, u32[]{:S(2)}) collective-permute-start(bf16[2,40,1536]{2,1,0:T(8,128)(2,1)S(1)} %pad_maximum_fusion.pair_ref), channel_id=1, source_target_pairs={{1,0},{16,1},{3,2},{18,3},{5,4},{20,5},{7,6},{22,7},{27,8},{10,9},... | collective-permute-start | bytes 737288 | tf_op jit(solution)/shard_map/ppermute | solution.py:356
  8.4 0.7 %copy-start.7 = (s32[12]{0:T(128)S(1)}, s32[12]{0:T(128)}, u32[]{:S(2)}) copy-start(s32[12]{0:T(128)} %count_ref.1) | copy-start | bytes 148
  11.8 19.5 %collective-permute-start.4 = (bf16[2,40,1536]{2,1,0:T(8,128)(2,1)S(1)}, bf16[2,40,1536]{2,1,0:T(8,128)(2,1)S(1)}, u32[]{:S(2)}, u32[]{:S(2)}) collective-permute-start(bf16[2,40,1536]{2,1,0:T(8,128)(2,1)S(1)} %pad_maximum_fusion.pair_ref), channel_id=1, source_target_pairs={{5,0},{20,1},{7,2},{22,3},{1,4},{16,5},{3,6},{18,7},{31,8},{14,9},... | collective-permute-start | bytes 737288 | tf_op jit(solution)/shard_map/ppermute | solution.py:356
  14.4 11.3 %copy-start.1 = (bf16[32,1536]{1,0:T(8,128)(2,1)S(1)}, bf16[32,1536]{1,0:T(8,128)(2,1)}, u32[]{:S(2)}) copy-start(bf16[32,1536]{1,0:T(8,128)(2,1)} %own_ref.1) | copy-start | bytes 294916
  25.7 18.8 %collective-permute-start.2 = (bf16[32,1536]{1,0:T(8,128)(2,1)S(1)}, bf16[32,1536]{1,0:T(8,128)(2,1)S(1)}, u32[]{:S(2)}, u32[]{:S(2)}) collective-permute-start(bf16[32,1536]{1,0:T(8,128)(2,1)S(1)} %copy-done.1), channel_id=1, source_target_pairs={{1,0},{0,1},{3,2},{2,3},{5,4},{4,5},{7,6},{6,7},{9,8},{8,9},{11,10... | collective-permute-start | bytes 294920 | tf_op jit(solution)/shard_map/ppermute | solution.py:356
  27.7 16.7 %collective-permute-start.3 = (bf16[32,1536]{1,0:T(8,128)(2,1)S(1)}, bf16[32,1536]{1,0:T(8,128)(2,1)S(1)}, u32[]{:S(2)}, u32[]{:S(2)}) collective-permute-start(bf16[32,1536]{1,0:T(8,128)(2,1)S(1)} %copy-done.1), channel_id=1, source_target_pairs={{31,0},{2,1},{1,2},{4,3},{3,4},{6,5},{5,6},{8,7},{7,8},{10,9},{9,1... | collective-permute-start | bytes 294920 | tf_op jit(solution)/shard_map/ppermute | solution.py:356
  30.3 17.0 %collective-permute-start.5 = (bf16[2,32,1536]{2,1,0:T(8,128)(2,1)S(1)}, bf16[2,32,1536]{2,1,0:T(8,128)(2,1)S(1)}, u32[]{:S(2)}, u32[]{:S(2)}) collective-permute-start(bf16[2,32,1536]{2,1,0:T(8,128)(2,1)S(1)} %get-tuple-element.31), channel_id=1, source_target_pairs={{0,1},{1,16},{2,3},{3,18},{4,5},{5,20},{6,7},{7,22},{8,27},{9,10},... | collective-permute-start | bytes 589832 | tf_op jit(solution)/shard_map/ppermute | solution.py:361
  31.3 13.2 %copy-start.8 = (bf16[12,128,128]{2,1,0:T(8,128)(2,1)S(1)}, bf16[12,128,128]{2,1,0:T(8,128)(2,1)}, u32[]{:S(2)}) copy-start(bf16[12,128,128]{2,1,0:T(8,128)(2,1)} %weight_ref.1) | copy-start | bytes 1179652
  42.6 12.6 %collective-permute-start.6 = (bf16[2,32,1536]{2,1,0:T(8,128)(2,1)S(1)}, bf16[2,32,1536]{2,1,0:T(8,128)(2,1)S(1)}, u32[]{:S(2)}, u32[]{:S(2)}) collective-permute-start(bf16[2,32,1536]{2,1,0:T(8,128)(2,1)S(1)} %get-tuple-element.34), channel_id=1, source_target_pairs={{0,5},{1,20},{2,7},{3,22},{4,1},{5,16},{6,3},{7,18},{8,31},{9,14},... | collective-permute-start | bytes 589832 | tf_op jit(solution)/shard_map/ppermute | solution.py:361
  47.4 11.9 %all-to-all-start = ((f32[32,8,128]{2,1,0:T(8,128)}), f32[32,8,128]{2,1,0:T(8,128)S(1)}, u32[]{:S(2)}, u32[]{:S(2)}) async-start(f32[32,8,128]{2,1,0:T(8,128)} %get-tuple-element.35), calls=%async_computation | async-start | bytes 262144 | tf_op jit(solution)/shard_map/all_to_all | solution.py:399
  55.3 1.4 %collective-permute-start.7 = (bf16[32,1536]{1,0:T(8,128)(2,1)S(1)}, bf16[32,1536]{1,0:T(8,128)(2,1)S(1)}, u32[]{:S(2)}, u32[]{:S(2)}) collective-permute-start(bf16[32,1536]{1,0:T(8,128)(2,1)S(1)} %fusion), channel_id=1, source_target_pairs={{8,0},{9,1},{10,2},{11,3},{12,4},{13,5},{14,6},{15,7},{0,8},{1,9},... | collective-permute-start | bytes 294920 | tf_op jit(solution)/shard_map/ppermute | solution.py:356

commit v6 on v5

--- a/solution.py
+++ b/solution.py
@@ -385,11 +385,11 @@
     late_pair, field = lax.optimization_barrier((pair, field))
     far = send(late_pair, lambda d: partner(d, True))
     totals = jnp.zeros((rhs, rhs), F32)
+    late_charges, close = lax.optimization_barrier((charges, close))
+    twin = send(late_charges, lambda d: d ^ 1)
+    other = send(late_charges, other_neighbour)
     field, close_back, totals = pairs_field(pair, close, tables[0], right, field, totals, False)
     close_back = send_back(close_back, lambda d: partner(d, False))
-    late_charges, field = lax.optimization_barrier((charges, field))
-    twin = send(late_charges, lambda d: d ^ 1)
-    other = send(late_charges, other_neighbour)
     field, far_back, totals = pairs_field(pair, far, tables[0], right, field, totals, True)
     far_back = send_back(far_back, lambda d: partner(d, True))
     field, totals = near_field(

time: 60.3 us -> 60.3 us (level)
  no operation moved by 1% of the time
where the time goes in v6:
time: 60.3 us; the launch traced here: 60 us
  Pallas kernels  29 us (48%)
  starting transfers between devices  18.7 us (31%)
  waiting for transfers between devices  8.57 us (14%)
  local copies, waits for them, and re-layouts  3 us (5%)
  between operations  0.69 us (1%)
    pallas_call x2, Pallas kernels, pairs_field(): in_vmem(functools.partial(pairs_body, rowblk, width), (jax.ShapeDtypeStru...  22.6 us
    ppermute x6, starting transfers between devices, send(): return lax.ppermute(value, AXES, [(source_of(d), d) for d in range(count)])  11.6 us
    all_to_all x1, starting transfers between devices, paired_blocks(): totals = lax.all_to_all(totals, AXES, 0, 0, tiled=True)  4.19 us
    ppermute x2, waiting for transfers between devices, send_back(): return lax.ppermute(value, AXES, [(d, source_of(d)) for d in range(count)])  3.66 us
    unnamed x18, local copies, waits for them, and re-layouts  2.98 us
    pallas_call x1, Pallas kernels, near_field(): pl.pallas_call(functools.partial(near_body, together), out_shape=(jax.Sha...  2.91 us
    ppermute x2, starting transfers between devices, send_back(): return lax.ppermute(value, AXES, [(d, source_of(d)) for d in range(count)])  2.86 us
    pallas_call x1, Pallas kernels, self_field(): pl.pallas_call(functools.partial(self_body, rowblk, width), out_shape=(ja...  2.73 us
  transfers between devices with their start and end apart: 9, of which 4 were waited for; matrix products, arithmetic and copies ran while one was open for 0% of the time, Pallas kernels for 47%

profile of v6, /device:TPU:0, one launch (start us, length us, event | category | flops | bytes accessed | tf_op | source)
XLA Modules:
  0.0 60.0 jit_solution(16704255421878183145)
XLA Ops:
  0.6 0.0 copy-start
  0.6 0.9 %copy-done = bf16[32,1536]{1,0:T(8,128)(2,1)S(1)} copy-done((bf16[32,1536]{1,0:T(8,128)(2,1)S(1)}, bf16[32,1536]{1,0:T(8,128)(2,1)}, u32[]{:S(2)}) %copy-start) | copy-done | bytes 98328
  1.5 0.0 copy-start.3
  1.5 0.7 %copy-done.3 = f32[4,1536]{1,0:T(4,128)S(1)} copy-done((f32[4,1536]{1,0:T(4,128)S(1)}, f32[4,1536]{1,0:T(4,128)}, u32[]{:S(2)}) %copy-start.3) | copy-done | bytes 24600
  2.3 0.0 copy-start.4
  2.3 0.7 %copy-done.4 = s32[1536]{0:T(1024)S(1)} copy-done((s32[1536]{0:T(1024)S(1)}, s32[1536]{0:T(1024)}, u32[]{:S(2)}) %copy-start.4) | copy-done | bytes 6168
  3.0 0.1 shard_map.95
  3.0 0.5 collective-permute-start
  3.5 1.0 %collective-permute-done = bf16[40,1536]{1,0:T(8,128)(2,1)S(1)} collective-permute-done((bf16[40,1536]{1,0:T(8,128)(2,1)S(1)}, bf16[40,1536]{1,0:T(8,128)(2,1)S(1)}, u32[]{:S(2)}, u32[]{:S(2)}) %collective-permute-start) | collective-permute-done | bytes 122912 | tf_op jit(solution)/shard_map/ppermute | solution.py:356
  4.5 0.0 copy-start.2
  4.5 0.0 copy-start.5
  4.5 0.0 copy-start.6
  4.5 3.9 %collective-permute-start.1 = (bf16[2,40,1536]{2,1,0:T(8,128)(2,1)S(1)}, bf16[2,40,1536]{2,1,0:T(8,128)(2,1)S(1)}, u32[]{:S(2)}, u32[]{:S(2)}) collective-permute-start(bf16[2,40,1536]{2,1,0:T(8,128)(2,1)S(1)} %pad_maximum_fusion.pair_ref), channel_id=1, source_target_pairs={{1,0},{16,1},{3,2},{18,3},{5,4},{20,5},{7,6},{22,7},{27,8},{10,9},... | collective-permute-start | bytes 737288 | tf_op jit(solution)/shard_map/ppermute | solution.py:356
  8.4 0.0 copy-start.7
  8.4 0.0 copy-done.2
  8.4 0.0 copy-done.5
  8.4 0.0 copy-done.6
  8.4 0.6 %copy-done.7 = s32[12]{0:T(128)S(1)} copy-done((s32[12]{0:T(128)S(1)}, s32[12]{0:T(128)}, u32[]{:S(2)}) %copy-start.7) | copy-done | bytes 72
  9.1 0.0 copy-start.1
  9.1 2.7 %shard_map.96 = (f32[2,32,1536]{2,1,0:T(8,128)S(1)}, s32[12,128]{1,0:T(8,128)S(1)}, bf16[2,32,1536]{2,1,0:T(8,128)(2,1)S(1)}) custom-call(bf16[2,40,1536]{2,1,0:T(8,128)(2,1)S(1)} %pad_maximum_fusion.pair_ref, bf16[32,16]{1,0:T(8,128)(2,1)S(1)} %copy-done.2, bf16[32,16]{1,0:T(8,128)(2,1)S(1)} %copy-done.6, s32[12,128]{1,0:T(8,128)S(1)} %copy-done.5, ...), custom_call_target="tpu_custom_call" | custom-call | bytes 1024 | tf_op jit(solution)/shard_map/pallas_call | solution.py:198
  11.8 2.6 %collective-permute-start.4 = (bf16[2,40,1536]{2,1,0:T(8,128)(2,1)S(1)}, bf16[2,40,1536]{2,1,0:T(8,128)(2,1)S(1)}, u32[]{:S(2)}, u32[]{:S(2)}) collective-permute-start(bf16[2,40,1536]{2,1,0:T(8,128)(2,1)S(1)} %pad_maximum_fusion.pair_ref), channel_id=1, source_target_pairs={{5,0},{20,1},{7,2},{22,3},{1,4},{16,5},{3,6},{18,7},{31,8},{14,9},... | collective-permute-start | bytes 737288 | tf_op jit(solution)/shard_map/ppermute | solution.py:356
  14.3 0.0 collective-permute-done.1.far_ref
  14.4 0.0 copy-done.1
  14.4 2.0 %collective-permute-start.2 = (bf16[32,1536]{1,0:T(8,128)(2,1)S(1)}, bf16[32,1536]{1,0:T(8,128)(2,1)S(1)}, u32[]{:S(2)}, u32[]{:S(2)}) collective-permute-start(bf16[32,1536]{1,0:T(8,128)(2,1)S(1)} %copy-done.1), channel_id=1, source_target_pairs={{1,0},{0,1},{3,2},{2,3},{5,4},{4,5},{7,6},{6,7},{9,8},{8,9},{11,10... | collective-permute-start | bytes 294920 | tf_op jit(solution)/shard_map/ppermute | solution.py:356
  16.4 2.6 %collective-permute-start.3 = (bf16[32,1536]{1,0:T(8,128)(2,1)S(1)}, bf16[32,1536]{1,0:T(8,128)(2,1)S(1)}, u32[]{:S(2)}, u32[]{:S(2)}) collective-permute-start(bf16[32,1536]{1,0:T(8,128)(2,1)S(1)} %copy-done.1), channel_id=1, source_target_pairs={{31,0},{2,1},{1,2},{4,3},{3,4},{6,5},{5,6},{8,7},{7,8},{10,9},{9,1... | collective-permute-start | bytes 294920 | tf_op jit(solution)/shard_map/ppermute | solution.py:356
  19.0 11.3 %shard_map.97 = (f32[2,32,1536]{2,1,0:T(8,128)S(1)}, bf16[2,32,1536]{2,1,0:T(8,128)(2,1)S(1)}, f32[32,32]{1,0:T(8,128)S(1)}) custom-call(bf16[2,40,1536]{2,1,0:T(8,128)(2,1)S(1)} %pad_maximum_fusion.pair_ref, bf16[2,40,1536]{2,1,0:T(8,128)(2,1)S(1)} %collective-permute-done.1.far_ref, bf16[32,16]{1,0:T(8,128)(2,1)S(1)} %copy-done.2, ...), custom_call_target="tpu_custom_call" | custom-call | bytes 1024 | tf_op jit(solution)/shard_map/pallas_call | solution.py:268
  30.3 1.0 %collective-permute-start.5 = (bf16[2,32,1536]{2,1,0:T(8,128)(2,1)S(1)}, bf16[2,32,1536]{2,1,0:T(8,128)(2,1)S(1)}, u32[]{:S(2)}, u32[]{:S(2)}) collective-permute-start(bf16[2,32,1536]{2,1,0:T(8,128)(2,1)S(1)} %get-tuple-element.31), channel_id=1, source_target_pairs={{0,1},{1,16},{2,3},{3,18},{4,5},{5,20},{6,7},{7,22},{8,27},{9,10},... | collective-permute-start | bytes 589832 | tf_op jit(solution)/shard_map/ppermute | solution.py:361
  31.3 0.0 collective-permute-done.4.far_ref
  31.3 0.0 copy-start.8
  31.3 11.3 %shard_map.98 = (f32[2,32,1536]{2,1,0:T(8,128)S(1)}, bf16[2,32,1536]{2,1,0:T(8,128)(2,1)S(1)}, f32[32,32]{1,0:T(8,128)S(1)}) custom-call(bf16[2,40,1536]{2,1,0:T(8,128)(2,1)S(1)} %pad_maximum_fusion.pair_ref, bf16[2,40,1536]{2,1,0:T(8,128)(2,1)S(1)} %collective-permute-done.4.far_ref, bf16[32,16]{1,0:T(8,128)(2,1)S(1)} %copy-done.2, ...), custom_call_target="tpu_custom_call" | custom-call | flops 30198988800 | bytes 1024 | tf_op jit(solution)/shard_map/pallas_call | solution.py:268
  42.6 1.9 %collective-permute-start.6 = (bf16[2,32,1536]{2,1,0:T(8,128)(2,1)S(1)}, bf16[2,32,1536]{2,1,0:T(8,128)(2,1)S(1)}, u32[]{:S(2)}, u32[]{:S(2)}) collective-permute-start(bf16[2,32,1536]{2,1,0:T(8,128)(2,1)S(1)} %get-tuple-element.34), channel_id=1, source_target_pairs={{0,5},{1,20},{2,7},{3,22},{4,1},{5,16},{6,3},{7,18},{8,31},{9,14},... | collective-permute-start | bytes 589832 | tf_op jit(solution)/shard_map/ppermute | solution.py:361
  44.4 0.0 collective-permute-done.2.twin_ref
  44.4 0.0 collective-permute-done.3.other_ref
  44.4 0.0 copy-done.8
  44.4 2.9 %shard_map.99 = (f32[2,32,1536]{2,1,0:T(8,128)S(1)}, f32[32,8,128]{2,1,0:T(8,128)}) custom-call(bf16[32,1536]{1,0:T(8,128)(2,1)S(1)} %collective-permute-done.2.twin_ref, bf16[32,1536]{1,0:T(8,128)(2,1)S(1)} %copy-done.1, bf16[32,1536]{1,0:T(8,128)(2,1)S(1)} %collective-permute-done.3.other_ref, s32[12,128]{1,0:T(8,128)S(1)} %get-tuple-element.20.index_ref, ...), custom_call_target="tpu_custom_call" | custom-call | flops 2000000000 | bytes 1024 | tf_op jit(solution)/shard_map/pallas_call | solution.py:332
  47.4 0.0 collective-permute-done.5
  47.4 4.2 %all-to-all-start = ((f32[32,8,128]{2,1,0:T(8,128)}), f32[32,8,128]{2,1,0:T(8,128)S(1)}, u32[]{:S(2)}, u32[]{:S(2)}) async-start(f32[32,8,128]{2,1,0:T(8,128)} %get-tuple-element.35), calls=%async_computation | async-start | bytes 262144 | tf_op jit(solution)/shard_map/all_to_all | solution.py:399
  51.6 3.7 %collective-permute-done.6 = bf16[2,32,1536]{2,1,0:T(8,128)(2,1)S(1)} collective-permute-done((bf16[2,32,1536]{2,1,0:T(8,128)(2,1)S(1)}, bf16[2,32,1536]{2,1,0:T(8,128)(2,1)S(1)}, u32[]{:S(2)}, u32[]{:S(2)}) %collective-permute-start.6) | collective-permute-done | bytes 196640 | tf_op jit(solution)/shard_map/ppermute | solution.py:361
  55.2 0.1 convert_add_fusion.field_ref
  55.3 0.1 collective-permute-start.7
  55.4 1.3 %collective-permute-done.7.part_ref = bf16[32,1536]{1,0:T(8,128)(2,1)S(1)} collective-permute-done((bf16[32,1536]{1,0:T(8,128)(2,1)S(1)}, bf16[32,1536]{1,0:T(8,128)(2,1)S(1)}, u32[]{:S(2)}, u32[]{:S(2)}) %collective-permute-start.7) | collective-permute-done | bytes 98336 | tf_op jit(solution)/shard_map/ppermute | solution.py:356
  56.7 2.6 %all-to-all-done.totals_ref = f32[32,8,128]{2,1,0:T(8,128)S(1)} async-done(((f32[32,8,128]{2,1,0:T(8,128)}), f32[32,8,128]{2,1,0:T(8,128)S(1)}, u32[]{:S(2)}, u32[]{:S(2)}) %all-to-all-start) | async-done | bytes 131104 | tf_op jit(solution)/shard_map/all_to_all | solution.py:399
  59.3 0.7 %shard_map.100 = (f32[32,1536]{1,0:T(8,128)}, f32[32,32]{1,0:T(8,128)}) custom-call(f32[2,32,1536]{2,1,0:T(8,128)S(1)} %convert_add_fusion.field_ref, bf16[32,1536]{1,0:T(8,128)(2,1)S(1)} %collective-permute-done.7.part_ref, f32[32,8,128]{2,1,0:T(8,128)S(1)} %all-to-all-done.totals_ref), custom_call_target="tpu_custom_call" | custom-call | bytes 1024 | tf_op jit(solution)/shard_map/pallas_call | solution.py:402
  (3 shorter events, 0.0 us)
Async XLA Ops:
  0.6 0.9 %copy-start = (bf16[32,1536]{1,0:T(8,128)(2,1)S(1)}, bf16[32,1536]{1,0:T(8,128)(2,1)}, u32[]{:S(2)}) copy-start(bf16[32,1536]{1,0:T(8,128)(2,1)} %own_ref.1) | copy-start | bytes 294916
  1.5 0.7 %copy-start.3 = (f32[4,1536]{1,0:T(4,128)S(1)}, f32[4,1536]{1,0:T(4,128)}, u32[]{:S(2)}) copy-start(f32[4,1536]{1,0:T(4,128)} %geo_ref.1) | copy-start | bytes 73732
  2.3 0.7 %copy-start.4 = (s32[1536]{0:T(1024)S(1)}, s32[1536]{0:T(1024)}, u32[]{:S(2)}) copy-start(s32[1536]{0:T(1024)} %conductor_ref.1) | copy-start | bytes 18436
  3.0 1.5 %collective-permute-start = (bf16[40,1536]{1,0:T(8,128)(2,1)S(1)}, bf16[40,1536]{1,0:T(8,128)(2,1)S(1)}, u32[]{:S(2)}, u32[]{:S(2)}) collective-permute-start(bf16[40,1536]{1,0:T(8,128)(2,1)S(1)} %shard_map.95), channel_id=1, source_target_pairs={{8,0},{9,1},{10,2},{11,3},{12,4},{13,5},{14,6},{15,7},{0,8},{1,9},... | collective-permute-start | bytes 368648 | tf_op jit(solution)/shard_map/ppermute | solution.py:356
  4.5 3.9 %copy-start.2 = (bf16[32,16]{1,0:T(8,128)(2,1)S(1)}, bf16[32,16]{1,0:T(8,128)(2,1)}, u32[]{:S(2)}) copy-start(bf16[32,16]{1,0:T(8,128)(2,1)} %constant.29.clone.ltab_ref) | copy-start | bytes 3076
  4.5 3.9 %copy-start.5 = (s32[12,128]{1,0:T(8,128)S(1)}, s32[12,128]{1,0:T(8,128)}, u32[]{:S(2)}) copy-start(s32[12,128]{1,0:T(8,128)} %index_ref.1) | copy-start | bytes 18436
  4.5 3.9 %copy-start.6 = (bf16[32,16]{1,0:T(8,128)(2,1)S(1)}, bf16[32,16]{1,0:T(8,128)(2,1)}, u32[]{:S(2)}) copy-start(bf16[32,16]{1,0:T(8,128)(2,1)} %constant.30.clone.rtab_ref) | copy-start | bytes 3076
  4.5 9.8 %collective-permute-start.1 = (bf16[2,40,1536]{2,1,0:T(8,128)(2,1)S(1)}, bf16[2,40,1536]{2,1,0:T(8,128)(2,1)S(1)}, u32[]{:S(2)}, u32[]{:S(2)}) collective-permute-start(bf16[2,40,1536]{2,1,0:T(8,128)(2,1)S(1)} %pad_maximum_fusion.pair_ref), channel_id=1, source_target_pairs={{1,0},{16,1},{3,2},{18,3},{5,4},{20,5},{7,6},{22,7},{27,8},{10,9},... | collective-permute-start | bytes 737288 | tf_op jit(solution)/shard_map/ppermute | solution.py:356
  8.4 0.7 %copy-start.7 = (s32[12]{0:T(128)S(1)}, s32[12]{0:T(128)}, u32[]{:S(2)}) copy-start(s32[12]{0:T(128)} %count_ref.1) | copy-start | bytes 148
  9.1 5.3 %copy-start.1 = (bf16[32,1536]{1,0:T(8,128)(2,1)S(1)}, bf16[32,1536]{1,0:T(8,128)(2,1)}, u32[]{:S(2)}) copy-start(bf16[32,1536]{1,0:T(8,128)(2,1)} %own_ref.1) | copy-start | bytes 294916
  11.8 19.5 %collective-permute-start.4 = (bf16[2,40,1536]{2,1,0:T(8,128)(2,1)S(1)}, bf16[2,40,1536]{2,1,0:T(8,128)(2,1)S(1)}, u32[]{:S(2)}, u32[]{:S(2)}) collective-permute-start(bf16[2,40,1536]{2,1,0:T(8,128)(2,1)S(1)} %pad_maximum_fusion.pair_ref), channel_id=1, source_target_pairs={{5,0},{20,1},{7,2},{22,3},{1,4},{16,5},{3,6},{18,7},{31,8},{14,9},... | collective-permute-start | bytes 737288 | tf_op jit(solution)/shard_map/ppermute | solution.py:356
  14.4 30.1 %collective-permute-start.2 = (bf16[32,1536]{1,0:T(8,128)(2,1)S(1)}, bf16[32,1536]{1,0:T(8,128)(2,1)S(1)}, u32[]{:S(2)}, u32[]{:S(2)}) collective-permute-start(bf16[32,1536]{1,0:T(8,128)(2,1)S(1)} %copy-done.1), channel_id=1, source_target_pairs={{1,0},{0,1},{3,2},{2,3},{5,4},{4,5},{7,6},{6,7},{9,8},{8,9},{11,10... | collective-permute-start | bytes 294920 | tf_op jit(solution)/shard_map/ppermute | solution.py:356
  16.4 28.1 %collective-permute-start.3 = (bf16[32,1536]{1,0:T(8,128)(2,1)S(1)}, bf16[32,1536]{1,0:T(8,128)(2,1)S(1)}, u32[]{:S(2)}, u32[]{:S(2)}) collective-permute-start(bf16[32,1536]{1,0:T(8,128)(2,1)S(1)} %copy-done.1), channel_id=1, source_target_pairs={{31,0},{2,1},{1,2},{4,3},{3,4},{6,5},{5,6},{8,7},{7,8},{10,9},{9,1... | collective-permute-start | bytes 294920 | tf_op jit(solution)/shard_map/ppermute | solution.py:356
  30.3 17.1 %collective-permute-start.5 = (bf16[2,32,1536]{2,1,0:T(8,128)(2,1)S(1)}, bf16[2,32,1536]{2,1,0:T(8,128)(2,1)S(1)}, u32[]{:S(2)}, u32[]{:S(2)}) collective-permute-start(bf16[2,32,1536]{2,1,0:T(8,128)(2,1)S(1)} %get-tuple-element.31), channel_id=1, source_target_pairs={{0,1},{1,16},{2,3},{3,18},{4,5},{5,20},{6,7},{7,22},{8,27},{9,10},... | collective-permute-start | bytes 589832 | tf_op jit(solution)/shard_map/ppermute | solution.py:361
  31.3 13.2 %copy-start.8 = (bf16[12,128,128]{2,1,0:T(8,128)(2,1)S(1)}, bf16[12,128,128]{2,1,0:T(8,128)(2,1)}, u32[]{:S(2)}) copy-start(bf16[12,128,128]{2,1,0:T(8,128)(2,1)} %weight_ref.1) | copy-start | bytes 1179652
  42.6 12.6 %collective-permute-start.6 = (bf16[2,32,1536]{2,1,0:T(8,128)(2,1)S(1)}, bf16[2,32,1536]{2,1,0:T(8,128)(2,1)S(1)}, u32[]{:S(2)}, u32[]{:S(2)}) collective-permute-start(bf16[2,32,1536]{2,1,0:T(8,128)(2,1)S(1)} %get-tuple-element.34), channel_id=1, source_target_pairs={{0,5},{1,20},{2,7},{3,22},{4,1},{5,16},{6,3},{7,18},{8,31},{9,14},... | collective-permute-start | bytes 589832 | tf_op jit(solution)/shard_map/ppermute | solution.py:361
  47.4 11.9 %all-to-all-start = ((f32[32,8,128]{2,1,0:T(8,128)}), f32[32,8,128]{2,1,0:T(8,128)S(1)}, u32[]{:S(2)}, u32[]{:S(2)}) async-start(f32[32,8,128]{2,1,0:T(8,128)} %get-tuple-element.35), calls=%async_computation | async-start | bytes 262144 | tf_op jit(solution)/shard_map/all_to_all | solution.py:399
  55.3 1.4 %collective-permute-start.7 = (bf16[32,1536]{1,0:T(8,128)(2,1)S(1)}, bf16[32,1536]{1,0:T(8,128)(2,1)S(1)}, u32[]{:S(2)}, u32[]{:S(2)}) collective-permute-start(bf16[32,1536]{1,0:T(8,128)(2,1)S(1)} %fusion), channel_id=1, source_target_pairs={{8,0},{9,1},{10,2},{11,3},{12,4},{13,5},{14,6},{15,7},{0,8},{1,9},... | collective-permute-start | bytes 294920 | tf_op jit(solution)/shard_map/ppermute | solution.py:356
